TPU v7x, 32 devices: a whole 2x2x4 slice. The times are simulated.
32 devices in a mesh: section: 2 (over core), clip: 4 (over z), tm: 4 (over y, x).
Axes of the slice: x: 2, y: 2, z: 4, core: 2. Of those that a mesh axis runs over, the one named last changes fastest.
Arguments:
- slow_input: float32 [2, 4, 16, 1024, 196], P(None, 'tm', 'clip'), may hold values from -6 to 6
- fast_input: float32 [2, 4, 64, 128, 196], P(None, 'tm', 'clip'), may hold values from -6 to 6
- frame_counts: int32 [2, 4], P(None, 'tm'), may hold values from 4 to 16, as said below
- fast_reduce: float32 [2, 3, 32, 128], P('section'), may hold values from -0.3125 to 0.3125
- fast_spatial: float32 [2, 9, 32, 32], P('section'), may hold values from -0.375 to 0.375
- fast_expand: float32 [2, 128, 32], P('section'), may hold values from -1 to 1
- lateral_conv: float32 [2, 5, 256, 128], P('section'), may hold values from -0.25 to 0.25
- slow_reduce: float32 [2, 3, 256, 1280], P('section'), may hold values from -0.09375 to 0.09375
- slow_spatial: float32 [2, 9, 256, 256], P('section'), may hold values from -0.125 to 0.125
- slow_expand: float32 [2, 1024, 256], P('section'), may hold values from -0.375 to 0.375
- shortcut: float32 [2, 1024, 1280], P('section'), may hold values from -0.15625 to 0.15625
- norm_gain: float32 [2, 3008], P('section'), may hold values from 0.25 to 1.75
- norm_bias: float32 [2, 3008], P('section'), may hold values from -3 to 3
- slow_cotangent: float32 [2, 4, 16, 1024, 196], P(None, 'tm', 'clip'), may hold values from -6 to 6
- fast_cotangent: float32 [2, 4, 64, 128, 196], P(None, 'tm', 'clip'), may hold values from -6 to 6
Outputs:
- slow_output: float32 [2, 2, 4, 16, 1024, 196], P('section', None, 'tm', 'clip')
- fast_output: float32 [2, 2, 4, 64, 128, 196], P('section', None, 'tm', 'clip')
- slow_input_grad: float32 [2, 2, 4, 16, 1024, 196], P('section', None, 'tm', 'clip')
- fast_input_grad: float32 [2, 2, 4, 64, 128, 196], P('section', None, 'tm', 'clip')
- grad_fast_reduce: float32 [2, 3, 32, 128], P('section')
- grad_fast_spatial: float32 [2, 9, 32, 32], P('section')
- grad_fast_expand: float32 [2, 128, 32], P('section')
- grad_lateral_conv: float32 [2, 5, 256, 128], P('section')
- grad_slow_reduce: float32 [2, 3, 256, 1280], P('section')
- grad_slow_spatial: float32 [2, 9, 256, 256], P('section')
- grad_slow_expand: float32 [2, 1024, 256], P('section')
- grad_shortcut: float32 [2, 1024, 1280], P('section')
- grad_norm_gain: float32 [2, 3008], P('section')
- grad_norm_bias: float32 [2, 3008], P('section')
Inputs may be any that keep to these rules, and one draw needn't show every extreme that they name: `frame_counts`: in each micro-batch one of the 4 clips has 16 valid slow frames and another one 4; frames at or after a clip's count are padding.
All inputs are finite; a program needn't handle non-finite values.
Results may differ from a plain program's by a relative error of at most 0.0003.
Values sent between devices are 32-bit elements; how exact they have to be, the bound alone decides.
No kernel may reach another device: no remote copies, remote signals or barrier semaphores. Data moves between devices by JAX's collectives and lax.ppermute only.
A program may use at most 448 MiB of HBM per device.

v0:
```python
from functools import partial
import math

import jax
import jax.numpy as jnp
from jax import lax
from jax.sharding import PartitionSpec as P

EPSILON = 1e-05
PRECISE = lax.Precision.HIGHEST


def padded_2(block, sides, width):
    for axis, dim in sides:
        count = lax.axis_size(axis)
        forward = [(i, i + 1) for i in range(count - 1)]
        backward = [(target, source) for source, target in forward]
        low = lax.ppermute(
            lax.slice_in_dim(block, block.shape[dim] - width, None, axis=dim), axis, forward
        )
        high = lax.ppermute(lax.slice_in_dim(block, 0, width, axis=dim), axis, backward)
        block = jnp.concatenate([low, block, high], axis=dim)
    return block


def shifted_2(x, axis, by):
    count = lax.axis_size(axis)
    pairs = [(i, i + by) for i in range(count) if 0 <= i + by < count]
    return lax.ppermute(x, axis, pairs)


def shift_table(grid_side):
    places = jnp.arange(grid_side * grid_side, dtype=jnp.int32)
    row_index = places // grid_side
    columns = places % grid_side
    tables = []
    for row_step in (-1, 0, 1):
        for column_step in (-1, 0, 1):
            source_row = row_index + row_step
            source_column = columns + column_step
            inside = (
                (source_row >= 0)
                & (source_row < grid_side)
                & (source_column >= 0)
                & (source_column < grid_side)
            )
            source = source_row * grid_side + source_column
            matched = (places[:, None] == source[None, :]) & inside[None, :]
            tables.append(matched.astype(jnp.float32))
    return jnp.stack(tables)


def pointwise(weight, values):
    return jnp.einsum("oc,btcp->btop", weight, values, precision=PRECISE)


def temporal(padded, weight, stride):
    tap_count = weight.shape[0]
    frames = (padded.shape[1] - tap_count) // stride + 1
    reach_span = stride * (frames - 1) + 1
    result = pointwise(weight[0], padded[:, 0:reach_span:stride])
    for offset in range(1, tap_count):
        result = result + pointwise(
            weight[offset], padded[:, offset : offset + reach_span : stride]
        )
    return result


def spatial(values, weight, shift_map):
    shifted = jnp.einsum("btcp,kpq->btkcq", values, shift_map, precision=PRECISE)
    return jnp.einsum("btkcq,koc->btoq", shifted, weight, precision=PRECISE)


def expand_channel(vector):
    return vector[None, None, :, None]


def norm_widths(weights):
    (
        fast_reduce,
        fast_spatial,
        fast_expand,
        lateral_conv,
        slow_reduce,
        slow_spatial,
        slow_expand,
        shortcut,
    ) = weights
    return [
        fast_reduce.shape[1],
        fast_spatial.shape[1],
        fast_expand.shape[0],
        lateral_conv.shape[1],
        slow_reduce.shape[1],
        slow_spatial.shape[1],
        slow_expand.shape[0],
        shortcut.shape[0],
    ]


def norm_pieces(vector, widths):
    pieces = []
    cursor = 0
    for span_width in widths:
        pieces.append(vector[cursor : cursor + span_width])
        cursor = cursor + span_width
    return pieces


def frame_halo(values, span_width):
    return padded_2(values, (("clip", 1),), span_width)


def return_rims(padded_grad, span_width):
    length = padded_grad.shape[1]
    core_part = padded_grad[:, span_width : length - span_width]
    rim_parts = jnp.concatenate(
        [padded_grad[:, :span_width], padded_grad[:, length - span_width :]], axis=1
    )
    arrived = padded_2(rim_parts, (("clip", 1),), span_width)
    core_part = core_part.at[:, :span_width].add(arrived[:, :span_width])
    core_length = core_part.shape[1]
    return core_part.at[:, core_length - span_width :].add(
        arrived[:, arrived.shape[1] - span_width :]
    )


def norm_stats(values_list, frame_mask, count_local):
    moments = []
    for values in values_list:
        weighted = values * frame_mask
        moments.append(jnp.sum(weighted, axis=(0, 1, 3)))
        moments.append(jnp.sum(weighted * values, axis=(0, 1, 3)))
    moments, count_total = lax.psum((jnp.concatenate(moments), count_local), ("clip", "tm"))
    results = []
    cursor = 0
    for values in values_list:
        span_width = values.shape[2]
        mean_value = moments[cursor : cursor + span_width] / count_total
        square = moments[cursor + span_width : cursor + 2 * span_width] / count_total
        cursor = cursor + 2 * span_width
        reciprocal = lax.rsqrt(square - mean_value * mean_value + EPSILON)
        results.append(
            ((values - expand_channel(mean_value)) * expand_channel(reciprocal), reciprocal)
        )
    return (results, count_total)


def norm_back(items, frame_mask, count_total):
    partial_sums = []
    for gradient, normed, reciprocal, gain_part in items:
        masked = gradient * frame_mask
        partial_sums.append(jnp.sum(masked, axis=(0, 1, 3)))
        partial_sums.append(jnp.sum(masked * normed, axis=(0, 1, 3)))
    channel_sums = lax.psum(jnp.concatenate(partial_sums), ("clip", "tm"))
    data_grads = []
    gain_grads = []
    bias_grads = []
    cursor = 0
    for gradient, normed, reciprocal, gain_part in items:
        span_width = normed.shape[2]
        bias_grad = channel_sums[cursor : cursor + span_width]
        gain_grad = channel_sums[cursor + span_width : cursor + 2 * span_width]
        cursor = cursor + 2 * span_width
        scaled = gradient * frame_mask * expand_channel(gain_part)
        data_grad = (
            frame_mask
            * expand_channel(reciprocal)
            * (
                scaled
                - expand_channel(gain_part * bias_grad / count_total)
                - normed * expand_channel(gain_part * gain_grad / count_total)
            )
        )
        data_grads.append(data_grad)
        gain_grads.append(gain_grad)
        bias_grads.append(bias_grad)
    return (data_grads, gain_grads, bias_grads)


def silu_back(before, gradient):
    sigma = jax.nn.sigmoid(before)
    return gradient * sigma * (1.0 + before * (1.0 - sigma))


def affine(normed, frame_mask, gain_part, bias_part):
    return frame_mask * (expand_channel(gain_part) * normed + expand_channel(bias_part))


def local_back(function, inputs, gradient):
    unused, pullback = jax.vjp(function, *inputs)
    return pullback(gradient)


def block_forward(
    slow_data, fast_data, counts, frame_base, weights, gain_vector, bias_vector, shift_map
):
    (
        fast_reduce,
        fast_spatial,
        fast_expand,
        lateral_conv,
        slow_reduce,
        slow_spatial,
        slow_expand,
        shortcut,
    ) = weights
    widths = norm_widths(weights)
    gain_parts = norm_pieces(gain_vector, widths)
    bias_parts = norm_pieces(bias_vector, widths)
    frames = slow_data.shape[1]
    places = frame_base + jnp.arange(frames, dtype=jnp.int32)
    slow_mask = (places[None, :] < counts[:, None]).astype(jnp.float32)[:, :, None, None]
    fast_mask = jnp.repeat(slow_mask, 4, axis=1)
    positions = slow_data.shape[3]
    slow_local = jnp.sum(slow_mask) * positions
    fast_local = jnp.sum(fast_mask) * positions
    fast_in = fast_data * fast_mask
    slow_in = slow_data * slow_mask
    fast_padded = frame_halo(fast_in, 1)
    [(first_norm, first_rstd)], fast_total = norm_stats(
        [temporal(fast_padded, fast_reduce, 1)], fast_mask, fast_local
    )
    first_pre = affine(first_norm, fast_mask, gain_parts[0], bias_parts[0])
    first_act = jax.nn.silu(first_pre)
    [(second_norm, second_rstd)], fast_total = norm_stats(
        [spatial(first_act, fast_spatial, shift_map)], fast_mask, fast_local
    )
    second_pre = affine(second_norm, fast_mask, gain_parts[1], bias_parts[1])
    second_act = jax.nn.silu(second_pre)
    [(third_norm, third_rstd)], fast_total = norm_stats(
        [pointwise(fast_expand, second_act)], fast_mask, fast_local
    )
    fast_pre = affine(third_norm, fast_mask, gain_parts[2], bias_parts[2]) + fast_in
    fast_out = jax.nn.silu(fast_pre)
    fast_wide = frame_halo(fast_out, 2)
    [(lateral_norm, lateral_rstd)], slow_total = norm_stats(
        [temporal(fast_wide, lateral_conv, 4)], slow_mask, slow_local
    )
    lateral_pre = affine(lateral_norm, slow_mask, gain_parts[3], bias_parts[3])
    joined = jnp.concatenate([slow_in, jax.nn.silu(lateral_pre)], axis=2)
    joined_padded = frame_halo(joined, 1)
    reduced = temporal(joined_padded, slow_reduce, 1)
    skipped = pointwise(shortcut, joined)
    [(inner_norm, inner_rstd), (skip_norm, skip_rstd)], slow_total = norm_stats(
        [reduced, skipped], slow_mask, slow_local
    )
    inner_pre = affine(inner_norm, slow_mask, gain_parts[4], bias_parts[4])
    inner_act = jax.nn.silu(inner_pre)
    [(middle_norm, middle_rstd)], slow_total = norm_stats(
        [spatial(inner_act, slow_spatial, shift_map)], slow_mask, slow_local
    )
    middle_pre = affine(middle_norm, slow_mask, gain_parts[5], bias_parts[5])
    middle_act = jax.nn.silu(middle_pre)
    [(expand_norm, expand_rstd)], slow_total = norm_stats(
        [pointwise(slow_expand, middle_act)], slow_mask, slow_local
    )
    slow_pre = affine(expand_norm, slow_mask, gain_parts[6], bias_parts[6]) + affine(
        skip_norm, slow_mask, gain_parts[7], bias_parts[7]
    )
    slow_out = jax.nn.silu(slow_pre)
    stored = {
        "slow_mask": slow_mask,
        "fast_mask": fast_mask,
        "slow_total": slow_total,
        "fast_total": fast_total,
        "fast_padded": fast_padded,
        "first_norm": first_norm,
        "first_rstd": first_rstd,
        "first_pre": first_pre,
        "first_act": first_act,
        "second_norm": second_norm,
        "second_rstd": second_rstd,
        "second_pre": second_pre,
        "second_act": second_act,
        "third_norm": third_norm,
        "third_rstd": third_rstd,
        "fast_pre": fast_pre,
        "fast_wide": fast_wide,
        "lateral_norm": lateral_norm,
        "lateral_rstd": lateral_rstd,
        "lateral_pre": lateral_pre,
        "joined_padded": joined_padded,
        "inner_norm": inner_norm,
        "inner_rstd": inner_rstd,
        "inner_pre": inner_pre,
        "inner_act": inner_act,
        "middle_norm": middle_norm,
        "middle_rstd": middle_rstd,
        "middle_pre": middle_pre,
        "middle_act": middle_act,
        "expand_norm": expand_norm,
        "expand_rstd": expand_rstd,
        "skip_norm": skip_norm,
        "skip_rstd": skip_rstd,
        "slow_pre": slow_pre,
    }
    return (slow_out, fast_out, stored)


def block_backward(slow_grad, fast_grad, stored, weights, gain_vector, shift_map):
    (
        fast_reduce,
        fast_spatial,
        fast_expand,
        lateral_conv,
        slow_reduce,
        slow_spatial,
        slow_expand,
        shortcut,
    ) = weights
    gain_parts = norm_pieces(gain_vector, norm_widths(weights))
    slow_mask = stored["slow_mask"]
    fast_mask = stored["fast_mask"]
    slow_total = stored["slow_total"]
    fast_total = stored["fast_total"]
    joined_padded = stored["joined_padded"]
    joined = joined_padded[:, 1 : joined_padded.shape[1] - 1]
    slow_pre_grad = silu_back(stored["slow_pre"], slow_grad)
    (expand_grad, skip_grad), gains_last, biases_last = norm_back(
        [
            (slow_pre_grad, stored["expand_norm"], stored["expand_rstd"], gain_parts[6]),
            (slow_pre_grad, stored["skip_norm"], stored["skip_rstd"], gain_parts[7]),
        ],
        slow_mask,
        slow_total,
    )
    slow_expand_grad, middle_act_grad = local_back(
        pointwise, (slow_expand, stored["middle_act"]), expand_grad
    )
    shortcut_grad, joined_skip_grad = local_back(pointwise, (shortcut, joined), skip_grad)
    (middle_grad,), gains_middle, biases_middle = norm_back(
        [
            (
                silu_back(stored["middle_pre"], middle_act_grad),
                stored["middle_norm"],
                stored["middle_rstd"],
                gain_parts[5],
            )
        ],
        slow_mask,
        slow_total,
    )
    inner_act_grad, slow_spatial_grad = local_back(
        partial(spatial, shift_map=shift_map), (stored["inner_act"], slow_spatial), middle_grad
    )
    (inner_grad,), gains_inner, biases_inner = norm_back(
        [
            (
                silu_back(stored["inner_pre"], inner_act_grad),
                stored["inner_norm"],
                stored["inner_rstd"],
                gain_parts[4],
            )
        ],
        slow_mask,
        slow_total,
    )
    joined_padded_grad, slow_reduce_grad = local_back(
        partial(temporal, stride=1), (joined_padded, slow_reduce), inner_grad
    )
    joined_grad = return_rims(joined_padded_grad, 1) + joined_skip_grad
    slow_width = slow_grad.shape[2]
    slow_in_grad = joined_grad[:, :, :slow_width]
    lateral_act_grad = joined_grad[:, :, slow_width:]
    (lateral_grad,), gains_lateral, biases_lateral = norm_back(
        [
            (
                silu_back(stored["lateral_pre"], lateral_act_grad),
                stored["lateral_norm"],
                stored["lateral_rstd"],
                gain_parts[3],
            )
        ],
        slow_mask,
        slow_total,
    )
    wide_grad, lateral_conv_grad = local_back(
        partial(temporal, stride=4), (stored["fast_wide"], lateral_conv), lateral_grad
    )
    fast_out_grad = fast_grad + return_rims(wide_grad, 2)
    fast_pre_grad = silu_back(stored["fast_pre"], fast_out_grad)
    (third_grad,), gains_third, biases_third = norm_back(
        [(fast_pre_grad, stored["third_norm"], stored["third_rstd"], gain_parts[2])],
        fast_mask,
        fast_total,
    )
    fast_expand_grad, second_act_grad = local_back(
        pointwise, (fast_expand, stored["second_act"]), third_grad
    )
    (second_grad,), gains_second, biases_second = norm_back(
        [
            (
                silu_back(stored["second_pre"], second_act_grad),
                stored["second_norm"],
                stored["second_rstd"],
                gain_parts[1],
            )
        ],
        fast_mask,
        fast_total,
    )
    first_act_grad, fast_spatial_grad = local_back(
        partial(spatial, shift_map=shift_map), (stored["first_act"], fast_spatial), second_grad
    )
    (first_grad,), gains_first, biases_first = norm_back(
        [
            (
                silu_back(stored["first_pre"], first_act_grad),
                stored["first_norm"],
                stored["first_rstd"],
                gain_parts[0],
            )
        ],
        fast_mask,
        fast_total,
    )
    fast_padded_grad, fast_reduce_grad = local_back(
        partial(temporal, stride=1), (stored["fast_padded"], fast_reduce), first_grad
    )
    fast_in_grad = return_rims(fast_padded_grad, 1) + fast_pre_grad
    weight_grads = [
        fast_reduce_grad,
        fast_spatial_grad,
        fast_expand_grad,
        lateral_conv_grad,
        slow_reduce_grad,
        slow_spatial_grad,
        slow_expand_grad,
        shortcut_grad,
    ]
    gain_grad = jnp.concatenate(
        gains_first
        + gains_second
        + gains_third
        + gains_lateral
        + gains_inner
        + gains_middle
        + gains_last
    )
    bias_grad = jnp.concatenate(
        biases_first
        + biases_second
        + biases_third
        + biases_lateral
        + biases_inner
        + biases_middle
        + biases_last
    )
    return (slow_in_grad * slow_mask, fast_in_grad * fast_mask, weight_grads, gain_grad, bias_grad)


def place_rows(buffer, micro_slot, live_flag, update):
    current = lax.dynamic_index_in_dim(buffer, micro_slot, 0, keepdims=False)
    chosen = jnp.where(live_flag > 0, update, current)
    return lax.dynamic_update_index_in_dim(buffer, chosen, micro_slot, 0)


def body(
    slow_input,
    fast_input,
    frame_counts,
    fast_reduce,
    fast_spatial,
    fast_expand,
    lateral_conv,
    slow_reduce,
    slow_spatial,
    slow_expand,
    shortcut,
    norm_gain,
    norm_bias,
    slow_cotangent,
    fast_cotangent,
):
    micro_count = slow_input.shape[0]
    positions = slow_input.shape[4]
    shift_map = shift_table(math.isqrt(positions))
    weights = (
        fast_reduce[0],
        fast_spatial[0],
        fast_expand[0],
        lateral_conv[0],
        slow_reduce[0],
        slow_spatial[0],
        slow_expand[0],
        shortcut[0],
    )
    gain_vector = norm_gain[0]
    bias_vector = norm_bias[0]
    section_index = lax.axis_index("section")
    first_section = section_index == 0
    last_section = section_index == 1
    frame_base = lax.axis_index("clip") * slow_input.shape[2]
    received = (jnp.zeros_like(slow_input[0]), jnp.zeros_like(fast_input[0]))
    slow_store = jnp.zeros_like(slow_input)
    fast_store = jnp.zeros_like(fast_input)
    retained = []
    for tick_index in range(micro_count + 1):
        micro_slot = jnp.clip(tick_index - section_index, 0, micro_count - 1)
        live_flag = (
            (tick_index - section_index >= 0) & (tick_index - section_index < micro_count)
        ).astype(jnp.float32)
        feed_slot = min(tick_index, micro_count - 1)
        slow_data = jnp.where(first_section, slow_input[feed_slot], received[0])
        fast_data = jnp.where(first_section, fast_input[feed_slot], received[1])
        counts = lax.dynamic_index_in_dim(frame_counts, micro_slot, 0, keepdims=False)
        slow_out, fast_out, stored = block_forward(
            slow_data, fast_data, counts, frame_base, weights, gain_vector, bias_vector, shift_map
        )
        retained.append((stored, micro_slot, live_flag))
        slow_store = place_rows(slow_store, micro_slot, live_flag, slow_out)
        fast_store = place_rows(fast_store, micro_slot, live_flag, fast_out)
        if tick_index < micro_count:
            received = shifted_2((slow_out, fast_out), "section", 1)
    returned = (jnp.zeros_like(slow_input[0]), jnp.zeros_like(fast_input[0]))
    slow_grad_store = jnp.zeros_like(slow_input)
    fast_grad_store = jnp.zeros_like(fast_input)
    weight_sums = [jnp.zeros_like(member) for member in weights]
    gain_sum = jnp.zeros_like(gain_vector)
    bias_sum = jnp.zeros_like(bias_vector)
    for tick_index in range(micro_count + 1):
        stored, micro_slot, live_flag = retained[micro_count - tick_index]
        slow_back = jnp.where(
            last_section,
            lax.dynamic_index_in_dim(slow_cotangent, micro_slot, 0, keepdims=False),
            returned[0],
        )
        fast_back = jnp.where(
            last_section,
            lax.dynamic_index_in_dim(fast_cotangent, micro_slot, 0, keepdims=False),
            returned[1],
        )
        slow_in_grad, fast_in_grad, weight_grads, gain_grad, bias_grad = block_backward(
            slow_back, fast_back, stored, weights, gain_vector, shift_map
        )
        weight_sums = [
            total + live_flag * update for total, update in zip(weight_sums, weight_grads)
        ]
        gain_sum = gain_sum + live_flag * gain_grad
        bias_sum = bias_sum + live_flag * bias_grad
        slow_grad_store = place_rows(slow_grad_store, micro_slot, live_flag, slow_in_grad)
        fast_grad_store = place_rows(fast_grad_store, micro_slot, live_flag, fast_in_grad)
        if tick_index < micro_count:
            returned = shifted_2((slow_in_grad, fast_in_grad), "section", -1)
    totals = lax.psum(
        (
            weight_sums[0],
            weight_sums[1],
            weight_sums[2],
            weight_sums[3],
            weight_sums[4],
            weight_sums[5],
            weight_sums[6],
            weight_sums[7],
        ),
        ("clip", "tm"),
    )
    return (
        slow_store[None],
        fast_store[None],
        slow_grad_store[None],
        fast_grad_store[None],
        totals[0][None],
        totals[1][None],
        totals[2][None],
        totals[3][None],
        totals[4][None],
        totals[5][None],
        totals[6][None],
        totals[7][None],
        gain_sum[None],
        bias_sum[None],
    )


def solution(mesh):
    placed = (
        P(None, "tm", "clip", None, None),
        P(None, "tm", "clip", None, None),
        P(None, "tm"),
        P("section", None, None, None),
        P("section", None, None, None),
        P("section", None, None),
        P("section", None, None, None),
        P("section", None, None, None),
        P("section", None, None, None),
        P("section", None, None),
        P("section", None, None),
        P("section", None),
        P("section", None),
        P(None, "tm", "clip", None, None),
        P(None, "tm", "clip", None, None),
    )
    return jax.shard_map(
        body,
        mesh=mesh,
        in_specs=placed,
        out_specs=(
            P("section", None, "tm", "clip", None, None),
            P("section", None, "tm", "clip", None, None),
            P("section", None, "tm", "clip", None, None),
            P("section", None, "tm", "clip", None, None),
            P("section", None, None, None),
            P("section", None, None, None),
            P("section", None, None),
            P("section", None, None, None),
            P("section", None, None, None),
            P("section", None, None, None),
            P("section", None, None),
            P("section", None, None),
            P("section", None),
            P("section", None),
        ),
        check_vma=False,
    )
```

profile of v0, /device:TPU:0, one launch (start us, length us, event | category | flops | bytes accessed | tf_op | source)
XLA Modules:
  0.0 3058.9 jit_solution(11582274410276268498)
XLA Ops:
  74.1 40.7 %all-reduce.81 = (f32[64]{0:T(128)S(1)}, f32[]{:T(128)}) all-reduce(f32[64]{0:T(128)S(1)} %pad_maximum_fusion.54, f32[]{:T(128)S(6)} %mul.3141), channel_id=1, replica_groups=mesh['section'=2,'clip'=4,'tm'=4] {'clip','tm'}, use_global_device_ids=true, to_apply=%region_2.3 | all-reduce | flops 65 | bytes 520 | tf_op jit(solution)/shard_map/psum | solution.py:134
  167.9 38.6 %psum.440 = f32[256]{0:T(256)S(1)} all-reduce(f32[256]{0:T(256)S(1)} %pad_maximum_fusion.48), channel_id=1, replica_groups=mesh['section'=2,'clip'=4,'tm'=4] {'clip','tm'}, use_global_device_ids=true, to_apply=%region_10.11 | all-reduce | flops 256 | bytes 2048 | tf_op jit(solution)/shard_map/psum | solution.py:134
  245.1 37.5 %all-reduce.80 = (f32[512]{0:T(512)}, f32[]{:T(128)}, f32[64]{0:T(128)}, f32[]{:T(128)}) all-reduce(f32[512]{0:T(512)} %pad_maximum_fusion.33, f32[]{:T(128)S(6)} %mul.3166, f32[64]{0:T(128)} %pad_maximum_fusion.56, f32[]{:T(128)S(6)} %mul.3214), channel_id=1, replica_groups=mesh['section'=2,'clip'=4,'tm'=4] {'clip','tm'}, use_global_device_ids=true, to_apply=%region_13.14 | all-reduce | flops 578 | bytes 4624 | tf_op jit(solution)/shard_map/psum | solution.py:134
  335.5 73.7 %all-reduce.79 = (f32[2560]{0:T(1024)}, f32[64]{0:T(128)}) all-reduce(f32[2560]{0:T(1024)} %pad_maximum_fusion.27, f32[64]{0:T(128)} %pad_maximum_fusion.57), channel_id=1, replica_groups=mesh['section'=2,'clip'=4,'tm'=4] {'clip','tm'}, use_global_device_ids=true, to_apply=%region_20.21 | all-reduce | flops 2624 | bytes 20992 | tf_op jit(solution)/shard_map/psum | solution.py:134
  429.3 37.3 %all-reduce.78 = (f32[512]{0:T(512)}, f32[256]{0:T(256)}) all-reduce(f32[512]{0:T(512)} %pad_maximum_fusion.34, f32[256]{0:T(256)} %pad_maximum_fusion.49), channel_id=1, replica_groups=mesh['section'=2,'clip'=4,'tm'=4] {'clip','tm'}, use_global_device_ids=true, to_apply=%region_23.24 | all-reduce | flops 768 | bytes 6144 | tf_op jit(solution)/shard_map/psum | solution.py:134
  511.3 73.6 %all-reduce.77 = (f32[2048]{0:T(1024)S(1)}, f32[512]{0:T(512)S(1)}, f32[]{:T(128)}, f32[64]{0:T(128)S(1)}, f32[]{:T(128)}) all-reduce(f32[2048]{0:T(1024)} %pad_maximum_fusion.30, f32[512]{0:T(512)} %pad_maximum_fusion.35, f32[]{:T(128)S(6)} %mul.3239, ...), channel_id=1, replica_groups=mesh['section'=2,'clip'=4,'tm'=4] {'clip','tm'}, use_global_device_ids=true, to_apply=%region_26.27 | all-reduce | flops 2626 | bytes 21008 | tf_op jit(solution)/shard_map/psum | solution.py:134
  677.7 71.8 %all-reduce.76 = (f32[2560]{0:T(1024)}, f32[64]{0:T(128)}) all-reduce(f32[2560]{0:T(1024)S(1)} %pad_maximum_fusion.28, f32[64]{0:T(128)} %pad_maximum_fusion.59), channel_id=1, replica_groups=mesh['section'=2,'clip'=4,'tm'=4] {'clip','tm'}, use_global_device_ids=true, to_apply=%region_47.48 | all-reduce | flops 2624 | bytes 20992 | tf_op jit(solution)/shard_map/psum | solution.py:134
  827.6 74.0 %all-reduce.74 = (f32[2048]{0:T(1024)S(1)}, f32[512]{0:T(512)S(1)}, f32[]{:T(128)}) all-reduce(f32[2048]{0:T(1024)S(1)} %pad_maximum_fusion.31, f32[512]{0:T(512)S(1)} %pad_maximum_fusion.37, f32[]{:T(128)S(6)} %mul.3310), channel_id=1, replica_groups=mesh['section'=2,'clip'=4,'tm'=4] {'clip','tm'}, use_global_device_ids=true, to_apply=%region_53.54 | all-reduce | flops 2561 | bytes 20488 | tf_op jit(solution)/shard_map/psum | solution.py:134
  964.9 71.8 %psum.461 = f32[2560]{0:T(1024)S(1)} all-reduce(f32[2560]{0:T(1024)S(1)} %pad_maximum_fusion.29), channel_id=1, replica_groups=mesh['section'=2,'clip'=4,'tm'=4] {'clip','tm'}, use_global_device_ids=true, to_apply=%region_74.75 | all-reduce | flops 2560 | bytes 20480 | tf_op jit(solution)/shard_map/psum | solution.py:134
  1049.8 36.8 %psum.462 = f32[512]{0:T(512)S(1)} all-reduce(f32[512]{0:T(512)S(1)} %pad_maximum_fusion.38), channel_id=1, replica_groups=mesh['section'=2,'clip'=4,'tm'=4] {'clip','tm'}, use_global_device_ids=true, to_apply=%region_77.78 | all-reduce | flops 512 | bytes 4096 | tf_op jit(solution)/shard_map/psum | solution.py:134
  1093.8 39.1 %psum.463 = f32[2048]{0:T(1024)S(1)} all-reduce(f32[2048]{0:T(1024)S(1)} %pad_maximum_fusion.32), channel_id=1, replica_groups=mesh['section'=2,'clip'=4,'tm'=4] {'clip','tm'}, use_global_device_ids=true, to_apply=%region_80.81 | all-reduce | flops 2048 | bytes 16384 | tf_op jit(solution)/shard_map/psum | solution.py:134
  1142.3 71.7 %psum.464 = f32[4096]{0:T(1024)S(1)} all-reduce(f32[4096]{0:T(1024)S(1)} %pad_maximum_fusion.24), channel_id=1, replica_groups=mesh['section'=2,'clip'=4,'tm'=4] {'clip','tm'}, use_global_device_ids=true, to_apply=%region_84.85 | all-reduce | flops 4096 | bytes 32768 | tf_op jit(solution)/shard_map/psum | solution.py:155
  1223.2 37.0 %psum.465 = f32[512]{0:T(512)S(1)} all-reduce(f32[512]{0:T(512)S(1)} %pad_maximum_fusion.39), channel_id=1, replica_groups=mesh['section'=2,'clip'=4,'tm'=4] {'clip','tm'}, use_global_device_ids=true, to_apply=%region_87.88 | all-reduce | flops 512 | bytes 4096 | tf_op jit(solution)/shard_map/psum | solution.py:155
  1275.7 39.0 %psum.466 = f32[512]{0:T(512)S(1)} all-reduce(f32[512]{0:T(512)S(1)} %pad_maximum_fusion.40), channel_id=1, replica_groups=mesh['section'=2,'clip'=4,'tm'=4] {'clip','tm'}, use_global_device_ids=true, to_apply=%region_90.91 | all-reduce | flops 512 | bytes 4096 | tf_op jit(solution)/shard_map/psum | solution.py:155
  1439.6 71.7 %all-reduce.73 = (f32[4096]{0:T(1024)S(1)}, f32[512]{0:T(512)S(1)}) all-reduce(f32[4096]{0:T(1024)S(1)} %pad_maximum_fusion.25, f32[512]{0:T(512)S(1)} %pad_maximum_fusion.45), channel_id=1, replica_groups=mesh['section'=2,'clip'=4,'tm'=4] {'clip','tm'}, use_global_device_ids=true, to_apply=%region_94.95 | all-reduce | flops 4608 | bytes 36864 | tf_op jit(solution)/shard_map/psum | solution.py:155
  1598.4 39.7 %all-reduce.72 = (f32[512]{0:T(512)S(1)}, f32[256]{0:T(256)S(1)}) all-reduce(f32[512]{0:T(512)S(1)} %pad_maximum_fusion.41, f32[256]{0:T(256)S(1)} %pad_maximum_fusion.51), channel_id=1, replica_groups=mesh['section'=2,'clip'=4,'tm'=4] {'clip','tm'}, use_global_device_ids=true, to_apply=%region_97.98 | all-reduce | flops 768 | bytes 6144 | tf_op jit(solution)/shard_map/psum | solution.py:155
  1659.1 37.1 %all-reduce.71 = (f32[512]{0:T(512)S(1)}, f32[64]{0:T(128)S(1)}) all-reduce(f32[512]{0:T(512)S(1)} %pad_maximum_fusion.42, f32[64]{0:T(128)S(1)} %pad_maximum_fusion.60), channel_id=1, replica_groups=mesh['section'=2,'clip'=4,'tm'=4] {'clip','tm'}, use_global_device_ids=true, to_apply=%region_100.101 | all-reduce | flops 576 | bytes 4608 | tf_op jit(solution)/shard_map/psum | solution.py:155
  1814.4 76.1 %all-reduce.70 = (f32[4096]{0:T(1024)S(1)}, f32[64]{0:T(128)S(1)}, f32[512]{0:T(512)S(1)}) all-reduce(f32[4096]{0:T(1024)S(1)} %pad_maximum_fusion.26, f32[64]{0:T(128)S(1)} %pad_maximum_fusion.61, f32[512]{0:T(512)S(1)} %pad_maximum_fusion.46), channel_id=1, replica_groups=mesh['section'=2,'clip'=4,'tm'=4] {'clip','tm'}, use_global_device_ids=true, to_apply=%region_104.105 | all-reduce | flops 4672 | bytes 37376 | tf_op jit(solution)/shard_map/psum | solution.py:155
  2089.6 39.1 %all-reduce.68 = (f32[512]{0:T(512)}, f32[64]{0:T(128)}) all-reduce(f32[512]{0:T(512)S(1)} %pad_maximum_fusion.44, f32[64]{0:T(128)S(1)} %pad_maximum_fusion.62), channel_id=1, replica_groups=mesh['section'=2,'clip'=4,'tm'=4] {'clip','tm'}, use_global_device_ids=true, to_apply=%region_110.111 | all-reduce | flops 576 | bytes 4608 | tf_op jit(solution)/shard_map/psum | solution.py:155
  2252.4 39.8 %all-reduce.67 = (f32[64]{0:T(128)S(1)}, f32[512]{0:T(512)S(1)}) all-reduce(f32[64]{0:T(128)S(1)} %pad_maximum_fusion.63, f32[512]{0:T(512)S(1)} %pad_maximum_fusion.47), channel_id=1, replica_groups=mesh['section'=2,'clip'=4,'tm'=4] {'clip','tm'}, use_global_device_ids=true, to_apply=%region_134.135 | all-reduce | flops 576 | bytes 4608 | tf_op jit(solution)/shard_map/psum | solution.py:155
  2426.6 38.9 %psum.483 = f32[64]{0:T(128)S(1)} all-reduce(f32[64]{0:T(128)S(1)} %pad_maximum_fusion.64), channel_id=1, replica_groups=mesh['section'=2,'clip'=4,'tm'=4] {'clip','tm'}, use_global_device_ids=true, to_apply=%region_143.144 | all-reduce | flops 64 | bytes 512 | tf_op jit(solution)/shard_map/psum | solution.py:155
  2478.2 36.7 %psum.484 = f32[64]{0:T(128)S(1)} all-reduce(f32[64]{0:T(128)S(1)} %pad_maximum_fusion.65), channel_id=1, replica_groups=mesh['section'=2,'clip'=4,'tm'=4] {'clip','tm'}, use_global_device_ids=true, to_apply=%region_146.147 | all-reduce | flops 64 | bytes 512 | tf_op jit(solution)/shard_map/psum | solution.py:155
  2597.0 50.0 %all-reduce.86.cloned.1.call-done = (f32[1,3,32,128]{3,2,1,0:T(8,128)}, f32[1,9,32,32]{3,2,1,0:T(8,128)}, f32[1,128,32]{1,2,0:T(8,128)}) async-done(((f32[1,3,32,128]{3,2,1,0:T(8,128)}, f32[1,9,32,32]{3,2,1,0:T(8,128)}, f32[1,128,32]{1,2,0:T(8,128)}), (f32[1,3,32,128]{3,2,1,0:T(8,128)}, f32[1,9,32,32]{3,2,1,0:T(8,128)}, f32[1,128,32]{1,2,0:T(8,128)})) %all-reduce.86.cloned.1.call-update) | async-done | bytes 102416 | tf_op jit(solution)/shard_map/psum | solution.py:546
  2646.9 388.8 %all-reduce.88.cloned.1.call-done = (f32[1,5,256,128]{3,2,1,0:T(8,128)}, f32[1,3,256,1280]{3,2,1,0:T(8,128)}, f32[1,9,256,256]{3,2,1,0:T(8,128)}, f32[1,1024,256]{2,1,0:T(8,128)}, f32[1,1024,1280]{2,1,0:T(8,128)}) async-done(((f32[1,5,256,128]{3,2,1,0:T(8,128)}, f32[1,3,256,1280]{3,2,1,0:T(8,128)}, f32[1,9,256,256]{3,2,1,0:T(8,128)}, f32[1,1024,256]{2,1,0:T(8,128)}, f32[1,1024,1280]{2,1,0:T(8,128)}), ...) | async-done | bytes 13238288 | tf_op jit(solution)/shard_map/psum | solution.py:546
  (1596 shorter events, 1472.9 us)
Async XLA Ops:
  7.2 2639.7 %all-reduce.86.cloned.1.call-start = ((), (), s32[]{:S(2)}) async-start(), calls=%async_computation | async-start | bytes 425984 | tf_op jit(solution)/shard_map/psum | solution.py:546
  17.2 47.4 %collective-permute-start.1 = (f32[1,1,128,196]{2,3,1,0:T(8,128)}, f32[1,1,128,196]{2,3,1,0:T(8,128)S(1)}, u32[]{:S(2)}, u32[]{:S(2)}) collective-permute-start(f32[1,1,128,196]{2,3,1,0:T(8,128)} %get-tuple-element.511), channel_id=1, source_target_pairs={{4,0},{8,4},{12,8},{5,1},{9,5},{13,9},{6,2},{10,6},{14,10},{7,3},{... | collective-permute-start | bytes 301064 | tf_op jit(solution)/shard_map/ppermute | solution.py:21
  18.5 50.7 %collective-permute-start = (f32[1,1,128,196]{2,3,1,0:T(8,128)}, f32[1,1,128,196]{2,3,1,0:T(8,128)}, u32[]{:S(2)}, u32[]{:S(2)}) collective-permute-start(f32[1,1,128,196]{2,3,1,0:T(8,128)} %get-tuple-element.510), channel_id=1, source_target_pairs={{0,4},{4,8},{8,12},{1,5},{5,9},{9,13},{2,6},{6,10},{10,14},{3,7},{... | collective-permute-start | bytes 301064 | tf_op jit(solution)/shard_map/ppermute | solution.py:18
  288.4 38.5 %collective-permute-start.5 = (f32[1,1,1280,196]{2,1,3,0:T(1,128)S(1)}, f32[1,1,1280,196]{2,1,3,0:T(1,128)S(1)}, u32[]{:S(2)}, u32[]{:S(2)}) collective-permute-start(f32[1,1,1280,196]{2,1,3,0:T(1,128)S(1)} %copy.78), channel_id=1, source_target_pairs={{4,0},{8,4},{12,8},{5,1},{9,5},{13,9},{6,2},{10,6},{14,10},{7,3},{... | collective-permute-start | bytes 3010568 | tf_op jit(solution)/shard_map/ppermute | solution.py:21
  290.7 39.7 %collective-permute-start.4 = (f32[1,1,1280,196]{2,1,3,0:T(1,128)S(1)}, f32[1,1,1280,196]{2,1,3,0:T(1,128)S(1)}, u32[]{:S(2)}, u32[]{:S(2)}) collective-permute-start(f32[1,1,1280,196]{2,1,3,0:T(1,128)S(1)} %copy.76), channel_id=1, source_target_pairs={{0,4},{4,8},{8,12},{1,5},{5,9},{9,13},{2,6},{6,10},{10,14},{3,7},{... | collective-permute-start | bytes 3010568 | tf_op jit(solution)/shard_map/ppermute | solution.py:18
  595.7 35.5 %collective-permute-start.6 = (f32[1,4,1024,196]{2,1,3,0:T(4,128)}, f32[1,4,1024,196]{2,1,3,0:T(4,128)}, u32[]{:S(2)}, u32[]{:S(2)}) collective-permute-start(f32[1,4,1024,196]{2,1,3,0:T(4,128)} %copy.84), channel_id=1, source_target_pairs={{0,16},{1,17},{2,18},{3,19},{4,20},{5,21},{6,22},{7,23},{8,24},{9,... | collective-permute-start | bytes 9633800 | tf_op jit(solution)/shard_map/ppermute | solution.py:29
  640.2 29.3 collective-permute-start.13
  645.8 27.1 collective-permute-start.12
  927.9 28.8 collective-permute-start.21
  934.2 26.0 collective-permute-start.20
  1377.6 53.3 %collective-permute-start.24 = (f32[1,4,1024,196]{2,1,3,0:T(4,128)}, f32[1,4,1024,196]{2,1,3,0:T(4,128)}, u32[]{:S(2)}, u32[]{:S(2)}) collective-permute-start(f32[1,4,1024,196]{2,1,3,0:T(4,128)} %copy.123), channel_id=1, source_target_pairs={{16,0},{17,1},{18,2},{19,3},{20,4},{21,5},{22,6},{23,7},{24,8},{25... | collective-permute-start | bytes 9633800 | tf_op jit(solution)/shard_map/ppermute | solution.py:29
  1566.6 29.1 collective-permute-start.30
  1567.9 27.8 collective-permute-start.31
  1714.7 18.6 collective-permute-start.25
  1761.1 47.4 %collective-permute-start.27 = (f32[1,4,1024,196]{2,1,3,0:T(4,128)S(1)}, f32[1,4,1024,196]{2,1,3,0:T(4,128)S(1)}, u32[]{:S(2)}, u32[]{:S(2)}) collective-permute-start(f32[1,4,1024,196]{2,1,3,0:T(4,128)S(1)} %copy.132), channel_id=1, source_target_pairs={{16,0},{17,1},{18,2},{19,3},{20,4},{21,5},{22,6},{23,7},{24,8},{25... | collective-permute-start | bytes 9633800 | tf_op jit(solution)/shard_map/ppermute | solution.py:29
  1971.5 56.5 %collective-permute-start.35 = (f32[1,2,128,196]{2,3,1,0:T(8,128)S(1)}, f32[1,2,128,196]{2,3,1,0:T(8,128)S(1)}, u32[]{:S(2)}, u32[]{:S(2)}) collective-permute-start(f32[1,2,128,196]{2,3,1,0:T(8,128)S(1)} %get-tuple-element.497), channel_id=1, source_target_pairs={{0,4},{4,8},{8,12},{1,5},{5,9},{9,13},{2,6},{6,10},{10,14},{3,7},{... | collective-permute-start | bytes 602120 | tf_op jit(solution)/shard_map/ppermute | solution.py:18
  1973.1 55.0 %collective-permute-start.36 = (f32[1,2,128,196]{2,3,1,0:T(8,128)S(1)}, f32[1,2,128,196]{2,3,1,0:T(8,128)S(1)}, u32[]{:S(2)}, u32[]{:S(2)}) collective-permute-start(f32[1,2,128,196]{2,3,1,0:T(8,128)S(1)} %get-tuple-element.496), channel_id=1, source_target_pairs={{4,0},{8,4},{12,8},{5,1},{9,5},{13,9},{6,2},{10,6},{14,10},{7,3},{... | collective-permute-start | bytes 602120 | tf_op jit(solution)/shard_map/ppermute | solution.py:21
  1974.4 30.2 collective-permute-start.32
  2181.9 47.9 %collective-permute-start.28 = (f32[1,1,1280,196]{2,1,3,0:T(1,128)}, f32[1,1,1280,196]{2,1,3,0:T(1,128)}, u32[]{:S(2)}, u32[]{:S(2)}) collective-permute-start(f32[1,1,1280,196]{2,1,3,0:T(1,128)} %copy.134), channel_id=1, source_target_pairs={{0,4},{4,8},{8,12},{1,5},{5,9},{9,13},{2,6},{6,10},{10,14},{3,7},{... | collective-permute-start | bytes 3010568 | tf_op jit(solution)/shard_map/ppermute | solution.py:18
  2186.6 44.9 %collective-permute-start.29 = (f32[1,1,1280,196]{2,1,3,0:T(1,128)}, f32[1,1,1280,196]{2,1,3,0:T(1,128)}, u32[]{:S(2)}, u32[]{:S(2)}) collective-permute-start(f32[1,1,1280,196]{2,1,3,0:T(1,128)} %copy.136), channel_id=1, source_target_pairs={{4,0},{8,4},{12,8},{5,1},{9,5},{13,9},{6,2},{10,6},{14,10},{7,3},{... | collective-permute-start | bytes 3010568 | tf_op jit(solution)/shard_map/ppermute | solution.py:21
  2325.8 31.5 %collective-permute-start.37 = (f32[1,1,128,196]{2,3,1,0:T(8,128)}, f32[1,1,128,196]{2,3,1,0:T(8,128)}, u32[]{:S(2)}, u32[]{:S(2)}) collective-permute-start(f32[1,1,128,196]{2,3,1,0:T(8,128)} %get-tuple-element.480), channel_id=1, source_target_pairs={{0,4},{4,8},{8,12},{1,5},{5,9},{9,13},{2,6},{6,10},{10,14},{3,7},{... | collective-permute-start | bytes 301064 | tf_op jit(solution)/shard_map/ppermute | solution.py:18
  2327.7 30.9 %collective-permute-start.38 = (f32[1,1,128,196]{2,3,1,0:T(8,128)}, f32[1,1,128,196]{2,3,1,0:T(8,128)}, u32[]{:S(2)}, u32[]{:S(2)}) collective-permute-start(f32[1,1,128,196]{2,3,1,0:T(8,128)} %get-tuple-element.479), channel_id=1, source_target_pairs={{4,0},{8,4},{12,8},{5,1},{9,5},{13,9},{6,2},{10,6},{14,10},{7,3},{... | collective-permute-start | bytes 301064 | tf_op jit(solution)/shard_map/ppermute | solution.py:21
  2355.8 22.7 collective-permute-start.41
  2541.9 493.8 %all-reduce.88.cloned.1.call-start = ((), (), s32[]{:S(2)}) async-start(), calls=%async_computation.1 | async-start | bytes 26476544 | tf_op jit(solution)/shard_map/psum | solution.py:546
  (529 other events, 10739.2 us)
Sparse Core Ops, SparseCore 0:
  2542.0 104.8 all-reduce.85
  2655.7 380.0 all-reduce.87
where the time goes:
time: 3070 us; the launch traced here: 3060 us
  blocking collectives  1270 us (41%)
  matrix products  727 us (24%)
  waiting for transfers between devices  450 us (15%)
  other arithmetic  247 us (8%)
  local copies, waits for them, and re-layouts  236 us (8%)
  starting transfers between devices  105 us (3%)
    psum x13, blocking collectives, norm_stats(): lax.psum((jnp.concatenate(moments), count_local), ('clip', 'tm'))  668 us
    psum x13, blocking collectives, norm_back(): channel_sums = lax.psum(jnp.concatenate(partial_sums), ('clip', 'tm'))  600 us
    dot_general x126, matrix products, pointwise(): return jnp.einsum('oc,btcp->btop', weight, values, precision=PRECISE)  539 us
    psum x2, waiting for transfers between devices, body(): lax.psum((weight_sums[0], weight_sums[1], weight_sums[2], weight_sums[3],...  439 us
    dot_general x18, matrix products, spatial(): return jnp.einsum('btkcq,koc->btoq', shifted, weight, precision=PRECISE)  137 us
    ppermute x18, starting transfers between devices, padded_2(): lax.ppermute(lax.slice_in_dim(block, block.shape[dim] - width, None, axis...  66.2 us
  transfers between devices with their start and end apart: 46, of which 6 were waited for; matrix products, arithmetic and copies ran while one was open for 17% of the time, Pallas kernels for 0%

commit v1 on v0

v1 whole, which is shorter than its diff:
```python
import math

import jax
import jax.numpy as jnp
from jax import lax
from jax.sharding import PartitionSpec as P

EPSILON = 1e-05
FINE = lax.Precision.HIGH
GROUP = 4
AXES = ("clip", "tm")


def dot_nn(a, b):
    return lax.dot_general(a, b, (((1,), (0,)), ((), ())), precision=FINE)


def dot_nt(a, b):
    return lax.dot_general(a, b, (((1,), (1,)), ((), ())), precision=FINE)


def dot_tn(a, b):
    return lax.dot_general(a, b, (((0,), (0,)), ((), ())), precision=FINE)


def sum_everywhere(vector):
    count = lax.axis_size("clip") * lax.axis_size("tm")
    copies = jnp.broadcast_to(vector[None], (count,) + vector.shape)
    return jnp.sum(lax.all_to_all(copies, AXES, 0, 0), axis=0)


def from_previous(edge):
    count = lax.axis_size("clip")
    return lax.ppermute(edge, "clip", [(i, i + 1) for i in range(count - 1)])


def from_next(edge):
    count = lax.axis_size("clip")
    return lax.ppermute(edge, "clip", [(i + 1, i) for i in range(count - 1)])


def swap(values):
    return lax.ppermute(values, "section", [(0, 1), (1, 0)])


def later(values, edge, frames):
    grid = values.reshape(-1, frames, values.shape[1])
    return jnp.concatenate([edge[:, None], grid[:, :-1]], axis=1).reshape(values.shape)


def earlier(values, edge, frames):
    grid = values.reshape(-1, frames, values.shape[1])
    return jnp.concatenate([grid[:, 1:], edge[:, None]], axis=1).reshape(values.shape)


def first_frame(values, frames):
    return values.reshape(-1, frames, values.shape[1])[:, 0]


def last_frame(values, frames):
    return values.reshape(-1, frames, values.shape[1])[:, -1]


def conv_grid(values, kernel, frames):
    side = math.isqrt(values.shape[0] // frames)
    grid = values.reshape(side, side, frames, values.shape[1])
    out = lax.conv_general_dilated(
        grid, kernel, (1, 1), "SAME", dimension_numbers=("HWNC", "HWIO", "HWNC"), precision=FINE
    )
    return out.reshape(values.shape[0], kernel.shape[3])


def conv_grid_back(values, kernel, grad, frames):
    out, pull = jax.vjp(lambda x, k: conv_grid(x, k, frames), values, kernel)
    return pull(grad)


def silu(v):
    return v * jax.nn.sigmoid(v)


def silu_slope(v):
    s = jax.nn.sigmoid(v)
    return s * (1.0 + v * (1.0 - s))


def fold(vector, channels):
    return jnp.sum(vector.reshape(-1, channels), axis=0)


def spread(vector, width):
    return jnp.tile(vector, width // vector.shape[0])


class Norm:
    def __init__(self, gain, bias):
        self.gain, self.bias, self.channels = gain, bias, gain.shape[0]

    def sums(self, values, mask):
        weighted = values * mask
        return jnp.concatenate(
            [
                fold(jnp.sum(weighted, axis=0), self.channels),
                fold(jnp.sum(weighted * values, axis=0), self.channels),
            ]
        )

    def learn(self, values, totals, count):
        self.values = values
        self.count = count
        self.mean = totals[: self.channels] / count
        square = totals[self.channels :] / count
        self.rstd = lax.rsqrt(square - self.mean * self.mean + EPSILON)

    def normed(self):
        width = self.values.shape[1]
        return (self.values - spread(self.mean, width)) * spread(self.rstd, width)

    def apply(self, mask):
        width = self.values.shape[1]
        return mask * (spread(self.gain, width) * self.normed() + spread(self.bias, width))

    def back_sums(self, grad):
        return jnp.concatenate(
            [
                fold(jnp.sum(grad, axis=0), self.channels),
                fold(jnp.sum(grad * self.normed(), axis=0), self.channels),
            ]
        )

    def back(self, grad, totals, mask):
        width = self.values.shape[1]
        self.bias_grad = totals[: self.channels]
        self.gain_grad = totals[self.channels :]
        scale = spread(self.gain * self.rstd, width)
        low = spread(self.bias_grad / self.count, width)
        slope = spread(self.gain_grad / self.count, width)
        return mask * (scale * (grad - low - self.normed() * slope))


class Section:
    def __init__(self, weights, gain, bias):
        reduce_, spatial, expand, lateral, slow_reduce, slow_spatial, slow_expand, shortcut = weights
        inner, wide = reduce_.shape[1], reduce_.shape[2]
        self.inner, self.wide = inner, wide
        taps = [
            [[float(r == q + k - 1) for k in range(3)] for q in range(GROUP)] for r in range(GROUP)
        ]
        near = jnp.einsum("rqk,koi->riqo", jnp.array(taps, jnp.float32), reduce_, precision="highest")
        far = [
            [[float((r, q, k) in ((3, 0, 0), (0, 3, 2))) for k in range(3)] for q in range(GROUP)]
            for r in range(GROUP)
        ]
        edge = jnp.einsum("rqk,koi->riqo", jnp.array(far, jnp.float32), reduce_, precision="highest")
        self.fast_reduce = jnp.concatenate(
            [near.reshape(GROUP * wide, GROUP * inner), edge.reshape(GROUP * wide, GROUP * inner)], axis=1
        )
        eye = jnp.eye(GROUP, dtype=jnp.float32)
        side = math.isqrt(spatial.shape[0])
        blocks = jnp.einsum("rq,koi->kriqo", eye, spatial, precision="highest")
        self.fast_spatial = blocks.reshape(side, side, GROUP * inner, GROUP * inner)
        self.fast_expand = jnp.einsum("rq,oi->riqo", eye, expand, precision="highest").reshape(
            GROUP * inner, GROUP * wide
        )
        self.lateral_here = lateral[2:5]
        self.lateral_next = lateral[0:2]
        self.joined = jnp.concatenate(
            [slow_reduce.reshape(-1, slow_reduce.shape[2]), shortcut], axis=0
        )
        self.slow_spatial = jnp.swapaxes(slow_spatial, 1, 2).reshape(
            side, side, slow_spatial.shape[2], slow_spatial.shape[1]
        )
        self.slow_expand = slow_expand
        self.depth = slow_reduce.shape[1]
        widths = [
            inner,
            inner,
            wide,
            lateral.shape[1],
            slow_reduce.shape[1],
            slow_spatial.shape[1],
            slow_expand.shape[0],
            shortcut.shape[0],
        ]
        self.norms, cursor = [], 0
        for width in widths:
            self.norms.append(Norm(gain[cursor : cursor + width], bias[cursor : cursor + width]))
            cursor += width


class Block:
    def __init__(self, section, mask, frames):
        self.s, self.mask, self.frames = section, mask, frames
        self.grads = {}

    def fast_forward(self, fast_in, shared):
        s, mask, frames, norms = self.s, self.mask, self.frames, self.s.norms
        self.fast_in = fast_in
        width = GROUP * s.inner
        both = dot_nn(fast_in, s.fast_reduce)
        here, edge = both[:, :width], both[:, width:]
        lane = lax.broadcasted_iota(jnp.int32, (1, width), 1)
        before = later(edge, from_previous(last_frame(edge, frames)), frames)
        after = earlier(edge, from_next(first_frame(edge, frames)), frames)
        first = here + jnp.where(
            lane < s.inner, before, jnp.where(lane >= width - s.inner, after, 0.0)
        )
        totals = yield norms[0].sums(first, mask)
        norms[0].learn(first, totals, 4.0 * shared["count"])
        self.first_act = silu(norms[0].apply(mask))
        second = conv_grid(self.first_act, s.fast_spatial, frames)
        totals = yield norms[1].sums(second, mask)
        norms[1].learn(second, totals, 4.0 * shared["count"])
        self.second_act = silu(norms[1].apply(mask))
        third = dot_nn(self.second_act, s.fast_expand)
        totals = yield norms[2].sums(third, mask)
        norms[2].learn(third, totals, 4.0 * shared["count"])
        self.fast_pre = norms[2].apply(mask) + fast_in
        self.fast_out = silu(self.fast_pre)
        wide = s.wide
        parts = [self.fast_out[:, r * wide : (r + 1) * wide] for r in range(GROUP)]
        here = dot_nt(parts[0], s.lateral_here[0])
        here += dot_nt(parts[1], s.lateral_here[1])
        here += dot_nt(parts[2], s.lateral_here[2])
        onward = dot_nt(parts[2], s.lateral_next[0]) + dot_nt(parts[3], s.lateral_next[1])
        lateral = here + later(onward, from_previous(last_frame(onward, frames)), frames)
        totals = yield norms[3].sums(lateral, mask)
        norms[3].learn(lateral, totals, shared["count"])
        self.lateral_act = silu(norms[3].apply(mask))

    def slow_forward(self, slow_in, shared):
        s, mask, frames, norms = self.s, self.mask, self.frames, self.s.norms
        self.joined = jnp.concatenate([slow_in, self.lateral_act], axis=1)
        depth = s.depth
        reduced = dot_nt(self.joined, s.joined[: 3 * depth])
        skipped = dot_nt(self.joined, s.joined[3 * depth :])
        low, mid, high = reduced[:, :depth], reduced[:, depth : 2 * depth], reduced[:, 2 * depth :]
        inner = (
            mid
            + later(low, from_previous(last_frame(low, frames)), frames)
            + earlier(high, from_next(first_frame(high, frames)), frames)
        )
        sums = [norms[4].sums(inner, mask), norms[7].sums(skipped, mask)]
        totals = yield jnp.concatenate(sums)
        norms[4].learn(inner, totals[: 2 * depth], shared["count"])
        norms[7].learn(skipped, totals[2 * depth :], shared["count"])
        self.inner_act = silu(norms[4].apply(mask))
        middle = conv_grid(self.inner_act, s.slow_spatial, frames)
        totals = yield norms[5].sums(middle, mask)
        norms[5].learn(middle, totals, shared["count"])
        self.middle_act = silu(norms[5].apply(mask))
        expanded = dot_nt(self.middle_act, s.slow_expand)
        totals = yield norms[6].sums(expanded, mask)
        norms[6].learn(expanded, totals, shared["count"])
        self.slow_pre = norms[6].apply(mask) + norms[7].apply(mask)
        self.slow_out = silu(self.slow_pre)

    def slow_backward(self, slow_grad):
        s, mask, frames, norms = self.s, self.mask, self.frames, self.s.norms
        depth = s.depth
        pre = mask * slow_grad * silu_slope(self.slow_pre)
        wide = pre.shape[1]
        totals = yield jnp.concatenate(
            [norms[6].back_sums(pre), jnp.sum(pre * norms[7].normed(), axis=0)]
        )
        expand_grad = norms[6].back(pre, totals[: 2 * wide], mask)
        skip_grad = norms[7].back(
            pre, jnp.concatenate([totals[:wide], totals[2 * wide :]]), mask
        )
        middle_act_grad = dot_nn(expand_grad, s.slow_expand)
        self.grads["slow_expand"] = dot_tn(expand_grad, self.middle_act)
        pre = mask * middle_act_grad * silu_slope(norms[5].apply(mask))
        totals = yield norms[5].back_sums(pre)
        middle_grad = norms[5].back(pre, totals, mask)
        inner_act_grad, kernel_grad = conv_grid_back(
            self.inner_act, s.slow_spatial, middle_grad, frames
        )
        self.grads["slow_spatial"] = jnp.swapaxes(
            kernel_grad.reshape((-1,) + kernel_grad.shape[2:]), 1, 2
        )
        pre = mask * inner_act_grad * silu_slope(norms[4].apply(mask))
        totals = yield norms[4].back_sums(pre)
        inner_grad = norms[4].back(pre, totals, mask)
        low = earlier(inner_grad, from_next(first_frame(inner_grad, frames)), frames)
        high = later(inner_grad, from_previous(last_frame(inner_grad, frames)), frames)
        reduced_grad = jnp.concatenate([low, inner_grad, high], axis=1)
        joined_grad = dot_nn(reduced_grad, s.joined[: 3 * depth]) + dot_nn(
            skip_grad, s.joined[3 * depth :]
        )
        self.grads["slow_reduce"] = dot_tn(reduced_grad, self.joined)
        self.grads["shortcut"] = dot_tn(skip_grad, self.joined)
        self.slow_in_grad = mask * joined_grad[:, :wide]
        self.lateral_act_grad = joined_grad[:, wide:]

    def fast_backward(self, fast_grad):
        s, mask, frames, norms = self.s, self.mask, self.frames, self.s.norms
        wide = s.wide
        pre = mask * self.lateral_act_grad * silu_slope(norms[3].apply(mask))
        totals = yield norms[3].back_sums(pre)
        here = norms[3].back(pre, totals, mask)
        onward = earlier(here, from_next(first_frame(here, frames)), frames)
        parts = [
            dot_nn(here, s.lateral_here[0]),
            dot_nn(here, s.lateral_here[1]),
            dot_nn(here, s.lateral_here[2]) + dot_nn(onward, s.lateral_next[0]),
            dot_nn(onward, s.lateral_next[1]),
        ]
        outs = [self.fast_out[:, r * wide : (r + 1) * wide] for r in range(GROUP)]
        self.grads["lateral"] = jnp.stack(
            [
                dot_tn(onward, outs[2]),
                dot_tn(onward, outs[3]),
                dot_tn(here, outs[0]),
                dot_tn(here, outs[1]),
                dot_tn(here, outs[2]),
            ]
        )
        out_grad = fast_grad() + jnp.concatenate(parts, axis=1)
        fast_pre_grad = mask * out_grad * silu_slope(self.fast_pre)
        totals = yield norms[2].back_sums(fast_pre_grad)
        third_grad = norms[2].back(fast_pre_grad, totals, mask)
        second_act_grad = dot_nt(third_grad, s.fast_expand)
        inner = s.inner
        grid = dot_tn(third_grad, self.second_act).reshape(GROUP, wide, GROUP, inner)
        self.grads["fast_expand"] = sum(grid[r, :, r] for r in range(GROUP))
        pre = mask * second_act_grad * silu_slope(norms[1].apply(mask))
        totals = yield norms[1].back_sums(pre)
        second_grad = norms[1].back(pre, totals, mask)
        first_act_grad, kernel_grad = conv_grid_back(
            self.first_act, s.fast_spatial, second_grad, frames
        )
        grid = kernel_grad.reshape(-1, GROUP, inner, GROUP, inner)
        self.grads["fast_spatial"] = jnp.swapaxes(
            sum(grid[:, r, :, r] for r in range(GROUP)), 1, 2
        )
        pre = mask * first_act_grad * silu_slope(norms[0].apply(mask))
        totals = yield norms[0].back_sums(pre)
        first_grad = norms[0].back(pre, totals, mask)
        width = GROUP * inner
        lane = lax.broadcasted_iota(jnp.int32, (1, width), 1)
        after = earlier(first_grad, from_next(first_frame(first_grad, frames)), frames)
        before = later(first_grad, from_previous(last_frame(first_grad, frames)), frames)
        edge = jnp.where(lane < inner, after, jnp.where(lane >= width - inner, before, 0.0))
        both = jnp.concatenate([first_grad, edge], axis=1)
        self.fast_in_grad = mask * (dot_nt(both, s.fast_reduce) + fast_pre_grad)
        grid = dot_tn(both, self.fast_in).reshape(2, GROUP, inner, GROUP, wide)
        near, far = grid[0], grid[1]
        self.grads["fast_reduce"] = jnp.stack(
            [
                near[1, :, 0] + near[2, :, 1] + near[3, :, 2] + far[0, :, 3],
                near[0, :, 0] + near[1, :, 1] + near[2, :, 2] + near[3, :, 3],
                near[0, :, 1] + near[1, :, 2] + near[2, :, 3] + far[3, :, 0],
            ]
        )


class Task:
    def __init__(self, steps):
        self.steps, self.done = steps, False
        self.wanted = next(steps)

    def resume(self, totals):
        try:
            self.wanted = self.steps.send(totals)
        except StopIteration:
            self.done = True


def advance(*tasks, extra=None):
    wanted = [task.wanted for task in tasks]
    if extra is not None:
        wanted.append(extra)
    totals = sum_everywhere(jnp.concatenate(wanted))
    pieces, cursor = [], 0
    for part in wanted:
        pieces.append(totals[cursor : cursor + part.shape[0]])
        cursor += part.shape[0]
    return pieces


def rows_of(values, own):
    picked = lax.dynamic_index_in_dim(values, own, 0, keepdims=False)[0]
    return jnp.transpose(picked, (2, 0, 1))


def body(
    slow_input,
    fast_input,
    frame_counts,
    fast_reduce,
    fast_spatial,
    fast_expand,
    lateral_conv,
    slow_reduce,
    slow_spatial,
    slow_expand,
    shortcut,
    norm_gain,
    norm_bias,
    slow_cotangent,
    fast_cotangent,
):
    own = lax.axis_index("section")
    lower = own == 0
    frames, positions = slow_input.shape[2], slow_input.shape[4]
    rows = frames * positions
    wide = fast_input.shape[3]

    def slow_rows(values):
        return rows_of(values, own).reshape(rows, -1)

    def fast_rows(values):
        return rows_of(values, own).reshape(rows, GROUP * wide)

    mine = [
        fast_reduce[0],
        fast_spatial[0],
        fast_expand[0],
        lateral_conv[0],
        slow_reduce[0],
        slow_spatial[0],
        slow_expand[0],
        shortcut[0],
        norm_gain[0],
        norm_bias[0],
    ]
    small = [0, 1, 2, 8, 9]
    packed = swap(jnp.concatenate([mine[i].reshape(-1) for i in small]))
    other, cursor = [None] * len(mine), 0
    for i in small:
        other[i] = packed[cursor : cursor + mine[i].size].reshape(mine[i].shape)
        cursor += mine[i].size
    for i in (3, 4, 7, 5, 6):
        other[i] = swap(mine[i])
    sections = []
    for index in range(2):
        both = [jnp.where(own == index, a, b) for a, b in zip(mine, other)]
        sections.append(Section(both[:8], both[8], both[9]))

    count_here = lax.dynamic_index_in_dim(frame_counts, own, 0, keepdims=False)
    frame = lax.axis_index("clip") * frames + lax.broadcasted_iota(jnp.int32, (positions, frames), 1)
    mask = (frame < count_here).astype(jnp.float32).reshape(rows, 1)
    blocks = [Block(section, mask, frames) for section in sections]
    shared = {}

    fast = [Task(blocks[0].fast_forward(mask * fast_rows(fast_input), shared)), None]
    got = advance(fast[0], extra=jnp.sum(mask, axis=0))
    shared["count"] = got[1][0]
    fast[0].resume(got[0])
    for step in range(2):
        fast[0].resume(advance(fast[0])[0])
    fast[1] = Task(blocks[1].fast_forward(blocks[0].fast_out, shared))
    got = advance(fast[0], fast[1])
    fast[0].resume(got[0])
    fast[1].resume(got[1])
    slow = [Task(blocks[0].slow_forward(mask * slow_rows(slow_input), shared)), None]
    for step in range(3):
        got = advance(slow[0], fast[1])
        slow[0].resume(got[0])
        fast[1].resume(got[1])
    slow[1] = Task(blocks[1].slow_forward(blocks[0].slow_out, shared))
    for step in range(3):
        slow[1].resume(advance(slow[1])[0])

    tasks = Task(blocks[1].slow_backward(slow_rows(slow_cotangent)))
    for step in range(3):
        tasks.resume(advance(tasks)[0])
    late = Task(blocks[1].fast_backward(lambda: fast_rows(fast_cotangent)))
    soon = Task(blocks[0].slow_backward(blocks[1].slow_in_grad))
    for step in range(3):
        got = advance(late, soon)
        late.resume(got[0])
        soon.resume(got[1])
    last = Task(blocks[0].fast_backward(lambda: blocks[1].fast_in_grad))
    got = advance(late, last)
    late.resume(got[0])
    last.resume(got[1])
    for step in range(3):
        last.resume(advance(last)[0])

    def assembled(first, second, channels, native):
        to_zero = lax.ppermute(first, "section", [(1, 0)])
        to_one = lax.ppermute(second, "section", [(0, 1)])
        pair = jnp.stack([jnp.where(lower, first, to_one), jnp.where(lower, to_zero, second)])
        grid = pair.reshape(2, positions, native, channels)
        return jnp.transpose(grid, (0, 2, 3, 1))[None, :, None]

    zero, one = blocks
    slow_wide = slow_input.shape[3]
    names = (
        "fast_reduce",
        "fast_spatial",
        "fast_expand",
        "lateral",
        "slow_reduce",
        "slow_spatial",
        "slow_expand",
        "shortcut",
    )
    norm_grads = []
    for block in blocks:
        norm_grads.append(
            jnp.stack(
                [
                    jnp.concatenate([norm.gain_grad for norm in block.s.norms]),
                    jnp.concatenate([norm.bias_grad for norm in block.s.norms]),
                ]
            )
        )
    kept = jnp.where(lower, norm_grads[0], norm_grads[1])
    kept = kept + swap(jnp.where(lower, norm_grads[1], norm_grads[0]))
    sent = [jnp.where(lower, one.grads[n], zero.grads[n]) for n in names]
    held = [jnp.where(lower, zero.grads[n], one.grads[n]) for n in names]
    partial = [h + swap(x) for h, x in zip(held, sent)]
    totals = lax.psum(tuple(partial), AXES)
    shapes = [w.shape for w in mine[:8]]
    totals = [t.reshape((1,) + s) for t, s in zip(totals, shapes)]
    return (
        assembled(zero.slow_out, one.slow_out, slow_wide, frames),
        assembled(zero.fast_out, one.fast_out, wide, GROUP * frames),
        assembled(zero.slow_in_grad, one.slow_in_grad, slow_wide, frames),
        assembled(zero.fast_in_grad, one.fast_in_grad, wide, GROUP * frames),
        *totals,
        kept[None, 0],
        kept[None, 1],
    )


def solution(mesh):
    acts = P(None, "tm", "clip", None, None)
    outs = P("section", None, "tm", "clip", None, None)
    four, three, two = P("section", None, None, None), P("section", None, None), P("section", None)
    weights = (four, four, three, four, four, four, three, three)
    return jax.shard_map(
        body,
        mesh=mesh,
        in_specs=(acts, acts, P(None, "tm"), *weights, two, two, acts, acts),
        out_specs=(outs, outs, outs, outs, *weights, two, two),
        check_vma=False,
    )
```

time: 3070 us -> 1500 us (0.49)
  blocking collectives: 1270 us -> 0 us
  matrix products: 727 us -> 295 us
  starting transfers between devices: 105 us -> 187 us
  local copies, waits for them, and re-layouts: 236 us -> 302 us
  other arithmetic: 247 us -> 209 us
    psum x26 -> x0, blocking collectives: 1270 us -> none  [the longest x13 668 us: norm_stats(): lax.psum((jnp.concatenate(moments), count_local), ('clip', 'tm'))]
    dot_general x156 -> x64, matrix products: 727 us -> 236 us  [the longest x20 87.6 us: dot_tn(): return lax.dot_general(a, b, (((0,), (0,)), ((), ())), precision=FINE)]
    all_to_all x0 -> x20, starting transfers between devices: none -> 112 us  [sum_everywhere(): return jnp.sum(lax.all_to_all(copies, AXES, 0, 0), axis=0)]
    reshape x0 -> x64, local copies, waits for them, and re-layouts: none -> 81.9 us  [the longest x6 11.8 us: later(): jnp.concatenate([edge[:, None], grid[:, :-1]], axis=1).reshape(values.shape)]
    pad x15 -> x0, local copies, waits for them, and re-layouts: 66.4 us -> none  [the longest x12 53.2 us: temporal(): padded[:, offset:offset + reach_span:stride]]
    conv_general_dilated x0 -> x12, matrix products: none -> 58.2 us  [conv_grid(): lax.conv_general_dilated(grid, kernel, (1, 1), 'SAME', dimension_numbers=...]
    all_to_all x0 -> x20, waiting for transfers between devices: none -> 56.8 us  [sum_everywhere(): return jnp.sum(lax.all_to_all(copies, AXES, 0, 0), axis=0)]
    psum x2, waiting for transfers between devices: 439 us -> 394 us  [body(): totals = lax.psum(tuple(partial), AXES)]
  transfers between devices with their start and end apart: 46 -> 65, of which waited for: 6 -> 21; matrix products, arithmetic and copies ran while one was open for 17% -> 51% of each run, Pallas kernels for 0% -> 0%
where the time goes in v1:
time: 1500 us; the launch traced here: 1480 us
  waiting for transfers between devices  468 us (31%)
  local copies, waits for them, and re-layouts  302 us (20%)
  matrix products  295 us (20%)
  other arithmetic  209 us (14%)
  starting transfers between devices  187 us (12%)
  between operations  19.9 us (1%)
    psum x2, waiting for transfers between devices, body(): totals = lax.psum(tuple(partial), AXES)  394 us
    all_to_all x20, starting transfers between devices, sum_everywhere(): return jnp.sum(lax.all_to_all(copies, AXES, 0, 0), axis=0)  112 us
    dot_general x20, matrix products, dot_tn(): return lax.dot_general(a, b, (((0,), (0,)), ((), ())), precision=FINE)  87.6 us
    dot_general x20, matrix products, dot_nn(): return lax.dot_general(a, b, (((1,), (0,)), ((), ())), precision=FINE)  76 us
    dot_general x20, matrix products, dot_nt(): return lax.dot_general(a, b, (((1,), (1,)), ((), ())), precision=FINE)  69.3 us
    conv_general_dilated x12, matrix products, conv_grid(): lax.conv_general_dilated(grid, kernel, (1, 1), 'SAME', dimension_numbers=...  58.2 us
    all_to_all x20, waiting for transfers between devices, sum_everywhere(): return jnp.sum(lax.all_to_all(copies, AXES, 0, 0), axis=0)  56.8 us
    unnamed x647, local copies, waits for them, and re-layouts  48.5 us
  transfers between devices with their start and end apart: 65, of which 21 were waited for; matrix products, arithmetic and copies ran while one was open for 51% of the time, Pallas kernels for 0%

profile of v1, /device:TPU:0, one launch (start us, length us, event | category | flops | bytes accessed | tf_op | source)
XLA Modules:
  0.0 1480.2 jit_solution(9648502324176077127)
XLA Ops:
  57.7 8.4 all-to-all-start
  100.0 7.2 all-to-all-done.2
  200.8 10.0 fusion
  286.9 7.8 all-to-all-done.6
  323.3 10.7 multiply_reduce_fusion.1
  381.0 7.0 all-to-all-start.8
  406.0 7.1 all-to-all-start.9
  421.7 8.4 fusion.262
  444.2 6.9 fusion.269
  451.8 7.1 all-to-all-start.11
  458.9 7.4 all-to-all-done.11
  494.3 14.0 fusion.9
  536.1 9.4 convolution_add_fusion.1
  558.5 9.7 fusion.327
  591.1 10.5 fusion.14
  601.6 16.6 %broadcast_select_fusion.1 = (f32[1024,1280]{1,0:T(8,128)}, f32[1024,1280]{1,0:T(8,128)}) fusion(f32[1024,1280]{1,0:T(8,128)S(1)} %fusion.14, pred[]{:T(512)S(6)} %eq.12, f32[784,256]{1,0:T(8,128)S(1)} %copy-done.45, f32[784,1024]{1,0:T(8,128)S(1)} %fusion.5, f32[784,1024]{1,0:T(8,128)} %get-tuple-element.138, f32[784,1024]{1,0:T(8,128)S(1)} %copy-done.42, ...), kind=kOutput, calls=%fused_computation.47 | convolution fusion | flops 6173560832 | bytes 26188864 | tf_op jit(solution)/shard_map/dot_general | solution.py:23
  624.7 9.8 fusion.7
  651.2 9.1 all-to-all-start.14
  705.6 10.0 broadcast_select_fusion.15
  773.5 10.9 fusion.15
  795.1 7.6 all-to-all-start.16
  802.8 11.2 broadcast_select_fusion.7
  870.2 9.0 all-to-all-start.17
  1068.2 388.8 %all-reduce.7.cloned.1.call-done = (f32[1,5,256,128]{3,2,1,0:T(8,128)}, f32[1,3,256,1280]{3,2,1,0:T(8,128)}, f32[1,9,256,256]{3,2,1,0:T(8,128)}, f32[1,1024,256]{2,1,0:T(8,128)}, f32[1,1024,1280]{2,1,0:T(8,128)}) async-done(((f32[1,5,256,128]{3,2,1,0:T(8,128)}, f32[1,3,256,1280]{3,2,1,0:T(8,128)}, f32[1,9,256,256]{3,2,1,0:T(8,128)}, f32[1,1024,256]{2,1,0:T(8,128)}, f32[1,1024,1280]{2,1,0:T(8,128)}), ...) | async-done | bytes 13238288 | tf_op jit(solution)/shard_map/psum | solution.py:515
  (1352 shorter events, 855.8 us)
Async XLA Ops:
  11.2 111.3 %collective-permute-start.3 = (f32[5,256,128]{2,1,0:T(8,128)}, f32[5,256,128]{2,1,0:T(8,128)}, u32[]{:S(2)}, u32[]{:S(2)}) collective-permute-start(f32[5,256,128]{2,1,0:T(8,128)} %bitcast.751), channel_id=1, source_target_pairs={{0,16},{16,0},{1,17},{17,1},{2,18},{18,2},{3,19},{19,3},{4,20},{20... | collective-permute-start | bytes 1966088 | tf_op jit(solution)/shard_map/ppermute | solution.py:43
  11.3 257.4 %collective-permute-start.12 = (f32[1024,256]{1,0:T(8,128)}, f32[1024,256]{1,0:T(8,128)}, u32[]{:S(2)}, u32[]{:S(2)}) collective-permute-start(f32[1024,256]{1,0:T(8,128)} %bitcast.818), channel_id=1, source_target_pairs={{0,16},{16,0},{1,17},{17,1},{2,18},{18,2},{3,19},{19,3},{4,20},{20... | collective-permute-start | bytes 3145736 | tf_op jit(solution)/shard_map/ppermute | solution.py:43
  11.7 146.8 %collective-permute-start.7 = (f32[3,256,1280]{2,1,0:T(8,128)}, f32[3,256,1280]{2,1,0:T(8,128)}, u32[]{:S(2)}, u32[]{:S(2)}) collective-permute-start(f32[3,256,1280]{2,1,0:T(8,128)} %bitcast.691), channel_id=1, source_target_pairs={{0,16},{16,0},{1,17},{17,1},{2,18},{18,2},{3,19},{19,3},{4,20},{20... | collective-permute-start | bytes 11796488 | tf_op jit(solution)/shard_map/ppermute | solution.py:43
  117.3 99.5 %collective-permute-start.11 = (f32[9,256,256]{2,1,0:T(8,128)}, f32[9,256,256]{2,1,0:T(8,128)}, u32[]{:S(2)}, u32[]{:S(2)}) collective-permute-start(f32[9,256,256]{2,1,0:T(8,128)} %bitcast.72), channel_id=1, source_target_pairs={{0,16},{16,0},{1,17},{17,1},{2,18},{18,2},{3,19},{19,3},{4,20},{20... | collective-permute-start | bytes 7077896 | tf_op jit(solution)/shard_map/ppermute | solution.py:43
  121.6 78.6 %collective-permute-start.10 = (f32[1024,1280]{1,0:T(8,128)}, f32[1024,1280]{1,0:T(8,128)}, u32[]{:S(2)}, u32[]{:S(2)}) collective-permute-start(f32[1024,1280]{1,0:T(8,128)} %bitcast.815), channel_id=1, source_target_pairs={{0,16},{16,0},{1,17},{17,1},{2,18},{18,2},{3,19},{19,3},{4,20},{20... | collective-permute-start | bytes 15728648 | tf_op jit(solution)/shard_map/ppermute | solution.py:43
  188.5 67.2 %collective-permute-start.19 = (f32[784,512]{1,0:T(8,128)S(1)}, f32[784,512]{1,0:T(8,128)}, u32[]{:S(2)}, u32[]{:S(2)}) collective-permute-start(f32[784,512]{1,0:T(8,128)S(1)} %fusion.48), channel_id=1, source_target_pairs={{16,0},{17,1},{18,2},{19,3},{20,4},{21,5},{22,6},{23,7},{24,8},{25... | collective-permute-start | bytes 4816904 | tf_op jit(solution)/shard_map/ppermute | solution.py:482
  301.4 120.3 %collective-permute-start.17 = (f32[784,1024]{1,0:T(8,128)S(1)}, f32[784,1024]{1,0:T(8,128)}, u32[]{:S(2)}, u32[]{:S(2)}) collective-permute-start(f32[784,1024]{1,0:T(8,128)S(1)} %fusion.5), channel_id=1, source_target_pairs={{16,0},{17,1},{18,2},{19,3},{20,4},{21,5},{22,6},{23,7},{24,8},{25... | collective-permute-start | bytes 9633800 | tf_op jit(solution)/shard_map/ppermute | solution.py:482
  314.7 20.4 %collective-permute-start.14 = (f32[196,256]{1,0:T(8,128)}, f32[196,256]{1,0:T(8,128)}, u32[]{:S(2)}, u32[]{:S(2)}) collective-permute-start(f32[196,256]{1,0:T(8,128)} %bitcast.646), channel_id=1, source_target_pairs={{0,4},{4,8},{8,12},{1,5},{5,9},{9,13},{2,6},{6,10},{10,14},{3,7},{... | collective-permute-start | bytes 602120 | tf_op jit(solution)/shard_map/ppermute | solution.py:34
  440.4 207.3 %collective-permute-start.18 = (f32[784,512]{1,0:T(8,128)}, f32[784,512]{1,0:T(8,128)}, u32[]{:S(2)}, u32[]{:S(2)}) collective-permute-start(f32[784,512]{1,0:T(8,128)} %copy-done.17), channel_id=1, source_target_pairs={{0,16},{1,17},{2,18},{3,19},{4,20},{5,21},{6,22},{7,23},{8,24},{9,... | collective-permute-start | bytes 4816904 | tf_op jit(solution)/shard_map/ppermute | solution.py:483
  589.6 49.1 %collective-permute-start.22 = (f32[196,256]{1,0:T(8,128)S(1)}, f32[196,256]{1,0:T(8,128)}, u32[]{:S(2)}, u32[]{:S(2)}) collective-permute-start(f32[196,256]{1,0:T(8,128)S(1)} %bitcast.752), channel_id=1, source_target_pairs={{4,0},{8,4},{12,8},{5,1},{9,5},{13,9},{6,2},{10,6},{14,10},{7,3},{... | collective-permute-start | bytes 602120 | tf_op jit(solution)/shard_map/ppermute | solution.py:39
  590.9 370.2 %collective-permute-start.40 = (f32[1024,256]{1,0:T(8,128)}, f32[1024,256]{1,0:T(8,128)}, u32[]{:S(2)}, u32[]{:S(2)}) collective-permute-start(f32[1024,256]{1,0:T(8,128)} %get-tuple-element.363), channel_id=1, source_target_pairs={{0,16},{16,0},{1,17},{17,1},{2,18},{18,2},{3,19},{19,3},{4,20},{20... | collective-permute-start | bytes 3145736 | tf_op jit(solution)/shard_map/ppermute | solution.py:43
  618.2 356.8 %collective-permute-start.41 = (f32[1024,1280]{1,0:T(8,128)}, f32[1024,1280]{1,0:T(8,128)}, u32[]{:S(2)}, u32[]{:S(2)}) collective-permute-start(f32[1024,1280]{1,0:T(8,128)} %get-tuple-element.365), channel_id=1, source_target_pairs={{0,16},{16,0},{1,17},{17,1},{2,18},{18,2},{3,19},{19,3},{4,20},{20... | collective-permute-start | bytes 15728648 | tf_op jit(solution)/shard_map/ppermute | solution.py:43
  698.6 26.1 %all-to-all-start.15 = ((f32[16,1,576]{2,1,0:T(1,128)}), f32[16,1,576]{2,1,0:T(1,128)S(1)}, u32[]{:S(2)}, u32[]{:S(2)}) async-start(f32[16,1,576]{2,1,0:T(1,128)} %broadcast_in_dim.279), calls=%async_computation.15 | async-start | bytes 81920 | tf_op jit(solution)/shard_map/all_to_all | solution.py:29
  721.7 244.7 %collective-permute-start.39 = (f32[9,256,256]{2,1,0:T(8,128)}, f32[9,256,256]{2,1,0:T(8,128)}, u32[]{:S(2)}, u32[]{:S(2)}) collective-permute-start(f32[9,256,256]{2,1,0:T(8,128)} %bitcast.704), channel_id=1, source_target_pairs={{0,16},{16,0},{1,17},{17,1},{2,18},{18,2},{3,19},{19,3},{4,20},{20... | collective-permute-start | bytes 7077896 | tf_op jit(solution)/shard_map/ppermute | solution.py:43
  739.4 23.4 %collective-permute-start.24 = (f32[196,256]{1,0:T(8,128)}, f32[196,256]{1,0:T(8,128)}, u32[]{:S(2)}, u32[]{:S(2)}) collective-permute-start(f32[196,256]{1,0:T(8,128)} %bitcast.641), channel_id=1, source_target_pairs={{0,4},{4,8},{8,12},{1,5},{5,9},{9,13},{2,6},{6,10},{10,14},{3,7},{... | collective-permute-start | bytes 602120 | tf_op jit(solution)/shard_map/ppermute | solution.py:34
  743.6 20.3 %collective-permute-start.23 = (f32[196,256]{1,0:T(8,128)}, f32[196,256]{1,0:T(8,128)}, u32[]{:S(2)}, u32[]{:S(2)}) collective-permute-start(f32[196,256]{1,0:T(8,128)} %bitcast.642), channel_id=1, source_target_pairs={{4,0},{8,4},{12,8},{5,1},{9,5},{13,9},{6,2},{10,6},{14,10},{7,3},{... | collective-permute-start | bytes 602120 | tf_op jit(solution)/shard_map/ppermute | solution.py:39
  916.1 23.7 %all-to-all-start.19 = ((f32[16,1,64]{2,1,0:T(1,128)}), f32[16,1,64]{2,1,0:T(1,128)S(1)}, u32[]{:S(2)}, u32[]{:S(2)}) async-start(f32[16,1,64]{2,1,0:T(1,128)} %broadcast_in_dim.289), calls=%async_computation.19 | async-start | bytes 16384 | tf_op jit(solution)/shard_map/all_to_all | solution.py:29
  919.6 148.6 %all-reduce.5.cloned.1.call-start = ((), (), s32[]{:S(2)}) async-start(), calls=%async_computation.20 | async-start | bytes 425984 | tf_op jit(solution)/shard_map/psum | solution.py:515
  948.7 21.3 %collective-permute-start.38 = (f32[768,1280]{1,0:T(8,128)}, f32[768,1280]{1,0:T(8,128)}, u32[]{:S(2)}, u32[]{:S(2)}) collective-permute-start(f32[768,1280]{1,0:T(8,128)} %get-tuple-element.361), channel_id=1, source_target_pairs={{0,16},{16,0},{1,17},{17,1},{2,18},{18,2},{3,19},{19,3},{4,20},{20... | collective-permute-start | bytes 11796488 | tf_op jit(solution)/shard_map/ppermute | solution.py:43
  960.6 496.4 %all-reduce.7.cloned.1.call-start = ((), (), s32[]{:S(2)}) async-start(), calls=%async_computation.21 | async-start | bytes 26476544 | tf_op jit(solution)/shard_map/psum | solution.py:515
  984.4 23.6 %collective-permute-start.25 = (f32[784,1024]{1,0:T(8,128)S(1)}, f32[784,1024]{1,0:T(8,128)}, u32[]{:S(2)}, u32[]{:S(2)}) collective-permute-start(f32[784,1024]{1,0:T(8,128)S(1)} %copy-done.27), channel_id=1, source_target_pairs={{0,16},{1,17},{2,18},{3,19},{4,20},{5,21},{6,22},{7,23},{8,24},{9,... | collective-permute-start | bytes 9633800 | tf_op jit(solution)/shard_map/ppermute | solution.py:483
  988.0 31.1 %collective-permute-start.16 = (f32[784,1024]{1,0:T(8,128)}, f32[784,1024]{1,0:T(8,128)}, u32[]{:S(2)}, u32[]{:S(2)}) collective-permute-start(f32[784,1024]{1,0:T(8,128)} %get-tuple-element.150), channel_id=1, source_target_pairs={{0,16},{1,17},{2,18},{3,19},{4,20},{5,21},{6,22},{7,23},{8,24},{9,... | collective-permute-start | bytes 9633800 | tf_op jit(solution)/shard_map/ppermute | solution.py:483
  1005.1 28.1 %collective-permute-start.32 = (f32[784,512]{1,0:T(8,128)}, f32[784,512]{1,0:T(8,128)}, u32[]{:S(2)}, u32[]{:S(2)}) collective-permute-start(f32[784,512]{1,0:T(8,128)} %get-tuple-element.359), channel_id=1, source_target_pairs={{0,16},{1,17},{2,18},{3,19},{4,20},{5,21},{6,22},{7,23},{8,24},{9,... | collective-permute-start | bytes 4816904 | tf_op jit(solution)/shard_map/ppermute | solution.py:483
  1013.2 33.2 %collective-permute-start.26 = (f32[784,1024]{1,0:T(8,128)}, f32[784,1024]{1,0:T(8,128)}, u32[]{:S(2)}, u32[]{:S(2)}) collective-permute-start(f32[784,1024]{1,0:T(8,128)} %get-tuple-element.113), channel_id=1, source_target_pairs={{16,0},{17,1},{18,2},{19,3},{20,4},{21,5},{22,6},{23,7},{24,8},{25... | collective-permute-start | bytes 9633800 | tf_op jit(solution)/shard_map/ppermute | solution.py:482
  (347 other events, 4115.7 us)
Sparse Core Ops, SparseCore 0:
  960.7 107.4 all-reduce.4
  1076.9 380.0 all-reduce.6

commit v2 on v1

v2 whole, which is shorter than its diff:
```python
from functools import partial
import math

import jax
import jax.numpy as jnp
from jax import lax
from jax.experimental import pallas as pl
from jax.experimental.pallas import tpu as pltpu
from jax.sharding import PartitionSpec as P

EPSILON = 1e-05
FINE = lax.Precision.HIGH
GROUP = 4
AXES = ("clip", "tm")


def dot_nn(a, b):
    return lax.dot_general(a, b, (((1,), (0,)), ((), ())), precision=FINE)


def dot_nt(a, b):
    return lax.dot_general(a, b, (((1,), (1,)), ((), ())), precision=FINE)


def dot_tn(a, b):
    return lax.dot_general(a, b, (((0,), (0,)), ((), ())), precision=FINE)


def sums_everywhere(vector):
    count = lax.axis_size("clip") * lax.axis_size("tm")
    copies = jnp.broadcast_to(vector, (count, vector.shape[1]))
    return lax.all_to_all(copies, AXES, 0, 0)


def from_previous(edge):
    count = lax.axis_size("clip")
    return lax.ppermute(edge, "clip", [(i, i + 1) for i in range(count - 1)])


def from_next(edge):
    count = lax.axis_size("clip")
    return lax.ppermute(edge, "clip", [(i + 1, i) for i in range(count - 1)])


def swap(values):
    return lax.ppermute(values, "section", [(0, 1), (1, 0)])


def silu(v):
    return v * jax.nn.sigmoid(v)


def silu_slope(v):
    s = jax.nn.sigmoid(v)
    return s * (1.0 + v * (1.0 - s))


VMEM_BYTES = 56 * 2**20


def rowwise(mask, width):
    return jnp.concatenate([mask] * (width // mask.shape[1]), axis=1)


def moments(r_ref, offset, width, count, fold=0):
    total = jnp.sum(r_ref[:, offset : offset + width], axis=0, keepdims=True)
    square = jnp.sum(r_ref[:, offset + width : offset + 2 * width], axis=0, keepdims=True)
    if fold:
        total, square = around(total, fold), around(square, fold)
    mean = total / count
    return mean, lax.rsqrt(square / count - mean * mean + EPSILON)


def around(row, fold):
    out = row
    for step in range(fold, row.shape[1], fold):
        out = out + pltpu.roll(row, step, 1)
    return out


def repeat(row, times):
    return row if times == 1 else jnp.concatenate([row] * times, axis=1)


def store_sums(st_ref, values, mask, fold=1):
    weighted = values * mask
    total = jnp.sum(weighted, axis=0, keepdims=True)
    square = jnp.sum(weighted * values, axis=0, keepdims=True)
    width = total.shape[1] // fold
    st_ref[:, :width] = sum(total[:, k * width : (k + 1) * width] for k in range(fold))
    st_ref[:, width:] = sum(square[:, k * width : (k + 1) * width] for k in range(fold))


class Stacked:
    def __init__(self, both, index):
        self.both, self.index, self.shape = both, index, both.shape[1:]

    def block(self, shape, place):
        def where(*step):
            return (self.index,) + place(*step)

        return pl.BlockSpec((None,) + shape, where)

    def whole(self):
        zeros = (0,) * len(self.shape)
        return self.block(self.shape, lambda *step: zeros)


def array_of(value):
    return value.both if isinstance(value, Stacked) else value


def call(kernel, outs, ins, scratch=(), **static):
    vmem = pl.BlockSpec(memory_space=pltpu.VMEM)
    return pl.pallas_call(
        partial(kernel, **static),
        grid=(1,),
        out_shape=[jax.ShapeDtypeStruct(s, jnp.float32) for s in outs],
        in_specs=[x.whole() if isinstance(x, Stacked) else vmem for x in ins],
        out_specs=[vmem] * len(outs),
        scratch_shapes=[pltpu.VMEM(s, jnp.float32) for s in scratch],
        compiler_params=pltpu.CompilerParams(vmem_limit_bytes=VMEM_BYTES),
    )(*[array_of(x) for x in ins])


def fixed(shape):
    return pl.BlockSpec(shape, lambda j: (0,) * len(shape))


def columns(rows, width):
    return pl.BlockSpec((rows, width), lambda j: (0, j))


def bands(height, width):
    return pl.BlockSpec((height, width), lambda j: (j, 0))


def call_steps(kernel, steps, outs, out_specs, ins, in_specs, scratch=(), **static):
    return pl.pallas_call(
        partial(kernel, **static),
        grid=(steps,),
        out_shape=[jax.ShapeDtypeStruct(s, jnp.float32) for s in outs],
        in_specs=in_specs,
        out_specs=out_specs,
        scratch_shapes=[pltpu.VMEM(s, jnp.float32) for s in scratch],
        compiler_params=pltpu.CompilerParams(
            dimension_semantics=("arbitrary",), vmem_limit_bytes=VMEM_BYTES
        ),
    )(*[array_of(x) for x in ins])


def take_rows(out_ref, values, first, frames, scratch):
    for k in range(out_ref.shape[1] // 128):
        scratch[k] = values[:, k * 128 : (k + 1) * 128]
        out_ref[:, k * 128 : (k + 1) * 128] = scratch[k, pl.ds(first, out_ref.shape[0], stride=frames), :]


def put_rows(values, first, frames, edge, scratch):
    pieces = []
    for k in range(edge.shape[1] // 128):
        scratch[k] = values[:, k * 128 : (k + 1) * 128]
        scratch[k, pl.ds(first, edge.shape[0], stride=frames), :] = edge[:, k * 128 : (k + 1) * 128]
        pieces.append(scratch[k])
    return jnp.concatenate(pieces, axis=1) if len(pieces) > 1 else pieces[0]


def before_rows(scratch, values, edge, frames):
    return put_rows(pltpu.roll(values, 1, 0), 0, frames, edge, scratch)


def after_rows(scratch, values, edge, frames):
    return put_rows(pltpu.roll(values, values.shape[0] - 1, 0), frames - 1, frames, edge, scratch)


def banded(w_ref, matrix):
    taps, inner, wide = w_ref.shape
    matrix[...] = jnp.zeros(matrix.shape, jnp.float32)
    for q in range(GROUP):
        for k in range(taps):
            r = q + k - 1
            start = q * inner + (0 if 0 <= r < GROUP else GROUP * inner)
            r = r % GROUP
            matrix[start : start + inner, r * wide : (r + 1) * wide] = w_ref[k]
    return matrix[...]


def fast_first_kernel(
    own_ref, x_ref, m_ref, w_ref, x_out, y_ref, low_ref, high_ref, scratch, matrix, *, frames
):
    rows, wide = m_ref.shape[0], x_ref.shape[1]
    for r in range(GROUP):
        x_out[:, r * wide : (r + 1) * wide] = (
            x_ref[pl.ds(r, rows, stride=GROUP), :] * rowwise(m_ref[...], wide)
        )
    y = dot_nt(x_out[...], banded(w_ref, matrix))
    y_ref[...] = y
    take_rows(low_ref, y[:, y.shape[1] // 2 :], 0, frames, scratch)
    take_rows(high_ref, y[:, y.shape[1] // 2 :], frames - 1, frames, scratch)


def fast_join_kernel(y_ref, p_ref, n_ref, m_ref, o_ref, st_ref, sp_ref, sn_ref, *, frames, inner):
    width = o_ref.shape[1]
    edge = y_ref[:, width:]
    before = before_rows(sp_ref, edge, p_ref[...], frames)
    after = after_rows(sn_ref, edge, n_ref[...], frames)
    lane = lax.broadcasted_iota(jnp.int32, (1, width), 1)
    out = y_ref[:, :width] + jnp.where(
        lane < inner, before, jnp.where(lane >= width - inner, after, 0.0)
    )
    o_ref[...] = out
    store_sums(st_ref, out, m_ref[...])


def fill_shifts(values, x0, xl, xr, side, frames):
    rows, width = values.shape
    pad = (x0.shape[0] - rows) // 2
    blank = jnp.zeros((pad + 8, width), jnp.float32)
    for ref in (x0, xl, xr):
        ref[0 : pad + 8] = blank
        ref[pad + rows - 8 : 2 * pad + rows] = blank
    row = lax.broadcasted_iota(jnp.int32, (rows, 1), 0)
    column = lax.rem(lax.div(row, frames), side)
    x0[pad : pad + rows] = values
    xl[pad + frames : pad + frames + rows] = jnp.where(column == side - 1, 0.0, values)
    xr[pad - frames : pad - frames + rows] = jnp.where(column == 0, 0.0, values)


def shifted(k, x0, xl, xr, rows, side, frames):
    pad = (x0.shape[0] - rows) // 2
    start = pad + (k // 3 - 1) * side * frames
    return (xl, x0, xr)[k % 3][start : start + rows]


def conv_kernel(
    v_ref, r_ref, c_ref, g_ref, b_ref, m_ref, k_ref, o_ref, act_ref, st_ref, x0, xl, xr,
    *, offset, fold, side, frames
):
    rows, width = v_ref.shape
    mean, rstd = moments(r_ref, offset, width, c_ref[...], fold)
    mask = rowwise(m_ref[...], width)
    act = mask * silu(g_ref[...] * ((v_ref[...] - mean) * rstd) + b_ref[...])
    act_ref[...] = act
    fill_shifts(act, x0, xl, xr, side, frames)
    total = dot_nt(shifted(0, x0, xl, xr, rows, side, frames), k_ref[0])
    for k in range(1, k_ref.shape[0]):
        total += dot_nt(shifted(k, x0, xl, xr, rows, side, frames), k_ref[k])
    o_ref[...] = total
    store_sums(st_ref, total, rowwise(m_ref[...], total.shape[1]))


def fast_expand_kernel(
    v_ref, r_ref, c_ref, g_ref, b_ref, m_ref, w_ref, o_ref, act_ref, st_ref, *, offset, fold
):
    width = v_ref.shape[1]
    mean, rstd = moments(r_ref, offset, width, c_ref[...], fold)
    act = rowwise(m_ref[...], width) * silu(g_ref[...] * ((v_ref[...] - mean) * rstd) + b_ref[...])
    act_ref[...] = act
    out = dot_nn(act, w_ref[...])
    o_ref[...] = out
    store_sums(st_ref, out, rowwise(m_ref[...], out.shape[1]), GROUP)


def fast_out_kernel(
    v_ref, x_ref, r_ref, c_ref, g_ref, b_ref, m_ref, l_ref, w_ref,
    out_ref, here_ref, next_ref, edge_ref, y_ref, low_ref, high_ref, scratch, matrix, *, offset, frames, more
):
    width = v_ref.shape[1]
    wide = width // GROUP
    mean, rstd = moments(r_ref, offset, wide, c_ref[...])
    mean, rstd = repeat(mean, GROUP), repeat(rstd, GROUP)
    pre = g_ref[...] * ((v_ref[...] - mean) * rstd) + b_ref[...] + x_ref[...]
    out = rowwise(m_ref[...], width) * silu(pre)
    out_ref[...] = out
    one, two, three, four = [out[:, r * wide : (r + 1) * wide] for r in range(GROUP)]
    here_ref[...] = dot_nt(one, l_ref[2]) + dot_nt(two, l_ref[3]) + dot_nt(three, l_ref[4])
    onward = dot_nt(three, l_ref[0]) + dot_nt(four, l_ref[1])
    next_ref[...] = onward
    take_rows(edge_ref, onward, frames - 1, frames, scratch)
    if more:
        y = dot_nt(out, banded(w_ref, matrix))
        y_ref[...] = y
        half = y.shape[1] // 2
        take_rows(low_ref, y[:, half:], 0, frames, scratch)
        take_rows(high_ref, y[:, half:], frames - 1, frames, scratch)
    else:
        for ref in (y_ref, low_ref, high_ref):
            ref[...] = jnp.zeros(ref.shape, jnp.float32)


def lateral_join_kernel(h_ref, n_ref, e_ref, m_ref, o_ref, st_ref, sp_ref, *, frames):
    out = h_ref[...] + before_rows(sp_ref, n_ref[...], e_ref[...], frames)
    o_ref[...] = out
    store_sums(st_ref, out, rowwise(m_ref[...], out.shape[1]))


def reduce_kernel(
    x_ref, v_ref, r_ref, c_ref, g_ref, b_ref, m_ref, w_ref, y_ref, low_ref, high_ref, act_ref, joined,
    scratch, *, offset, frames
):
    step = pl.program_id(0)
    wide, lateral = x_ref.shape[1], v_ref.shape[1]

    @pl.when(step == 0)
    def _():
        mean, rstd = moments(r_ref, offset, lateral, c_ref[...])
        joined[:, :wide] = x_ref[...]
        act = silu(g_ref[...] * ((v_ref[...] - mean) * rstd) + b_ref[...])
        act = act * rowwise(m_ref[...], lateral)
        joined[:, wide:] = act
        act_ref[...] = act

    y = dot_nt(joined[...], w_ref[...])
    y_ref[...] = y

    @pl.when(step == 0)
    def _():
        take_rows(high_ref, y, frames - 1, frames, scratch)

    @pl.when(step == 2)
    def _():
        take_rows(low_ref, y, 0, frames, scratch)


def shortcut_kernel(x_ref, a_ref, m_ref, w_ref, y_ref, s_ref, q_ref):
    wide = x_ref.shape[1]
    out = dot_nt(x_ref[...], w_ref[:, :wide])
    out += dot_nt(a_ref[...], w_ref[:, wide:])
    y_ref[...] = out
    weighted = out * rowwise(m_ref[...], out.shape[1])
    s_ref[...] = jnp.sum(weighted, axis=0, keepdims=True)
    q_ref[...] = jnp.sum(weighted * out, axis=0, keepdims=True)


def inner_join_kernel(y_ref, p_ref, n_ref, m_ref, o_ref, st_ref, sp_ref, sn_ref, *, frames):
    depth = o_ref.shape[1]
    out = y_ref[:, depth : 2 * depth]
    out += before_rows(sp_ref, y_ref[:, :depth], p_ref[...], frames)
    out += after_rows(sn_ref, y_ref[:, 2 * depth : 3 * depth], n_ref[...], frames)
    o_ref[...] = out
    store_sums(st_ref, out, rowwise(m_ref[...], depth))


def expand_kernel(
    v_ref, r_ref, c_ref, g_ref, b_ref, m_ref, w_ref, o_ref, act_ref, s_ref, q_ref, *, offset
):
    width = v_ref.shape[1]

    @pl.when(pl.program_id(0) == 0)
    def _():
        mean, rstd = moments(r_ref, offset, width, c_ref[...])
        act = silu(g_ref[...] * ((v_ref[...] - mean) * rstd) + b_ref[...])
        act_ref[...] = act * rowwise(m_ref[...], width)

    out = dot_nt(act_ref[...], w_ref[...])
    o_ref[...] = out
    weighted = out * rowwise(m_ref[...], out.shape[1])
    s_ref[...] = jnp.sum(weighted, axis=0, keepdims=True)
    q_ref[...] = jnp.sum(weighted * out, axis=0, keepdims=True)


def slow_out_kernel(
    e_ref, k_ref, r6_ref, r7_ref, c_ref, g6_ref, b6_ref, g7_ref, b7_ref, m_ref, o_ref,
    *, offset6, offset7, total
):
    pre, _, _ = slow_pre(
        e_ref, k_ref, r6_ref, r7_ref, c_ref, g6_ref, b6_ref, g7_ref, b7_ref, offset6, offset7, total
    )
    o_ref[...] = rowwise(m_ref[...], pre.shape[1]) * silu(pre)


def part(r_ref, offset, width):
    start = pl.multiple_of(offset + pl.program_id(0) * width, 128)
    return jnp.sum(r_ref[:, pl.ds(start, width)], axis=0, keepdims=True)


def moments_part(r_ref, offset, total, width, count):
    mean = part(r_ref, offset, width) / count
    square = part(r_ref, offset + total, width) / count
    return mean, lax.rsqrt(square - mean * mean + EPSILON)


def slow_pre(
    e_ref, k_ref, r6_ref, r7_ref, c_ref, g6_ref, b6_ref, g7_ref, b7_ref, offset6, offset7, total
):
    width = e_ref.shape[1]
    mean6, rstd6 = moments_part(r6_ref, offset6, total, width, c_ref[...])
    mean7, rstd7 = moments_part(r7_ref, offset7, total, width, c_ref[...])
    n6 = (e_ref[...] - mean6) * rstd6
    n7 = (k_ref[...] - mean7) * rstd7
    pre = (g6_ref[...] * n6 + b6_ref[...]) + (g7_ref[...] * n7 + b7_ref[...])
    return pre, (n6, rstd6), (n7, rstd7)


def slow_slope_kernel(
    d_ref, e_ref, k_ref, r6_ref, r7_ref, c_ref, g6_ref, b6_ref, g7_ref, b7_ref, m_ref,
    p_ref, s_ref, q6_ref, q7_ref, *, offset6, offset7, total
):
    pre, (n6, _), (n7, _) = slow_pre(
        e_ref, k_ref, r6_ref, r7_ref, c_ref, g6_ref, b6_ref, g7_ref, b7_ref, offset6, offset7, total
    )
    grad = rowwise(m_ref[...], pre.shape[1]) * d_ref[...] * silu_slope(pre)
    p_ref[...] = grad
    s_ref[...] = jnp.sum(grad, axis=0, keepdims=True)
    q6_ref[...] = jnp.sum(grad * n6, axis=0, keepdims=True)
    q7_ref[...] = jnp.sum(grad * n7, axis=0, keepdims=True)


def expand_back_kernel(
    p_ref, e_ref, k_ref, r6_ref, r7_ref, rb_ref, c_ref, g6_ref, g7_ref, m_ref, w_ref, act_ref,
    v_ref, r5_ref, g5_ref, b5_ref,
    skip_ref, dw_ref, o_ref, st_ref, acc, *, offset6, offset7, offsetb, offset5, total
):
    step, steps = pl.program_id(0), pl.num_programs(0)
    width, depth = p_ref.shape[1], v_ref.shape[1]
    count, mask = c_ref[...], rowwise(m_ref[...], width)
    mean6, rstd6 = moments_part(r6_ref, offset6, total, width, count)
    mean7, rstd7 = moments_part(r7_ref, offset7, total, width, count)
    low = part(rb_ref, offsetb, width) / count
    q6 = part(rb_ref, offsetb + total, width) / count
    q7 = part(rb_ref, offsetb + 2 * total, width) / count
    pre = p_ref[...]
    grad = mask * ((g6_ref[...] * rstd6) * (pre - low - (e_ref[...] - mean6) * rstd6 * q6))
    skip_ref[...] = mask * ((g7_ref[...] * rstd7) * (pre - low - (k_ref[...] - mean7) * rstd7 * q7))
    dw_ref[...] = dot_tn(grad, act_ref[...])
    product = dot_nn(grad, w_ref[...])

    @pl.when(step == 0)
    def _():
        acc[...] = product

    @pl.when(step > 0)
    def _():
        acc[...] += product

    @pl.when(step == steps - 1)
    def _():
        mean, rstd = moments(r5_ref, offset5, depth, count)
        normed = (v_ref[...] - mean) * rstd
        out = rowwise(m_ref[...], depth) * acc[...]
        out = out * silu_slope(g5_ref[...] * normed + b5_ref[...])
        o_ref[...] = out
        st_ref[:, :depth] = jnp.sum(out, axis=0, keepdims=True)
        st_ref[:, depth:] = jnp.sum(out * normed, axis=0, keepdims=True)


def store_weight(dw_ref, grad, x_ref, a_ref):
    count, _, width = dw_ref.shape
    for k in range(count - 1):
        dw_ref[k] = dot_tn(grad, x_ref[:, k * width : (k + 1) * width])
    dw_ref[count - 1] = dot_tn(grad, a_ref[...])


def shortcut_back_kernel(d_ref, w_ref, x_ref, a_ref, dw_ref, o_ref):
    step = pl.program_id(0)
    grad = d_ref[...]
    store_weight(dw_ref, grad, x_ref, a_ref)

    @pl.when(step == 0)
    def _():
        o_ref[...] = dot_nn(grad, w_ref[...])

    @pl.when(step > 0)
    def _():
        o_ref[...] += dot_nn(grad, w_ref[...])


def back_sums(rb_ref, offset, width, count, fold=0):
    low = jnp.sum(rb_ref[:, offset : offset + width], axis=0, keepdims=True)
    slope = jnp.sum(rb_ref[:, offset + width : offset + 2 * width], axis=0, keepdims=True)
    if fold:
        low, slope = around(low, fold), around(slope, fold)
    return low / count, slope / count


def norm_back(pre, values, mean, rstd, gain, low, slope, mask):
    return mask * ((gain * rstd) * (pre - low - (values - mean) * rstd * slope))


def store_back_sums(st_ref, grad, normed, fold=1):
    low = jnp.sum(grad, axis=0, keepdims=True)
    slope = jnp.sum(grad * normed, axis=0, keepdims=True)
    width = low.shape[1] // fold
    st_ref[:, :width] = sum(low[:, k * width : (k + 1) * width] for k in range(fold))
    st_ref[:, width:] = sum(slope[:, k * width : (k + 1) * width] for k in range(fold))


def conv_back_kernel(
    p_ref, v_ref, r_ref, rb_ref, c_ref, g_ref, u_ref, ru_ref, gu_ref, bu_ref, m_ref, k_ref,
    d_ref, o_ref, st_ref, x0, xl, xr, *, offset, offsetb, offsetu, fold, side, frames
):
    rows, width = v_ref.shape
    count, mask = c_ref[...], rowwise(m_ref[...], width)
    mean, rstd = moments(r_ref, offset, width, count, fold)
    low, slope = back_sums(rb_ref, offsetb, width, count, fold)
    grad = norm_back(p_ref[...], v_ref[...], mean, rstd, g_ref[...], low, slope, mask)
    d_ref[...] = grad
    fill_shifts(grad, x0, xl, xr, side, frames)
    last = k_ref.shape[0] - 1
    total = dot_nn(shifted(0, x0, xl, xr, rows, side, frames), k_ref[last])
    for k in range(1, last + 1):
        total += dot_nn(shifted(k, x0, xl, xr, rows, side, frames), k_ref[last - k])
    mean, rstd = moments(ru_ref, offsetu, u_ref.shape[1], count, fold)
    normed = (u_ref[...] - mean) * rstd
    out = rowwise(m_ref[...], u_ref.shape[1]) * total
    out = out * silu_slope(gu_ref[...] * normed + bu_ref[...])
    o_ref[...] = out
    store_back_sums(st_ref, out, normed)


def conv_weight_kernel(x_ref, d_ref, dw_ref, x0, xl, xr, *, side, frames):
    rows = x_ref.shape[0]
    fill_shifts(x_ref[...], x0, xl, xr, side, frames)
    grad = d_ref[...]
    for k in range(dw_ref.shape[0]):
        dw_ref[k] = dot_tn(grad, shifted(k, x0, xl, xr, rows, side, frames))


def norm_back_kernel(
    p_ref, v_ref, r_ref, rb_ref, c_ref, g_ref, m_ref, o_ref, low_ref, high_ref, scratch,
    *, offset, offsetb, fold, frames
):
    width = v_ref.shape[1]
    count = c_ref[...]
    mean, rstd = moments(r_ref, offset, width, count, fold)
    low, slope = back_sums(rb_ref, offsetb, width, count, fold)
    mask = rowwise(m_ref[...], width)
    out = norm_back(p_ref[...], v_ref[...], mean, rstd, g_ref[...], low, slope, mask)
    o_ref[...] = out
    take_rows(low_ref, out, 0, frames, scratch)
    take_rows(high_ref, out, frames - 1, frames, scratch)


def joined_back_kernel(
    d_ref, p_ref, n_ref, j_ref, w_ref, m_ref, v_ref, r_ref, c_ref, g_ref, b_ref,
    x_ref, o_ref, all_ref, st_ref, scratch, *, offset, frames
):
    step, steps = pl.program_id(0), pl.num_programs(0)
    depth = d_ref.shape[1]

    @pl.when(step == 0)
    def _():
        grad = d_ref[...]
        all_ref[:, :depth] = after_rows(scratch, grad, n_ref[...], frames)
        all_ref[:, depth : 2 * depth] = grad
        all_ref[:, 2 * depth :] = before_rows(scratch, grad, p_ref[...], frames)

    mask = rowwise(m_ref[...], o_ref.shape[1])
    out = mask * (dot_nn(all_ref[...], w_ref[...]) + j_ref[...])

    @pl.when(step < steps - 1)
    def _():
        x_ref[...] = out

    @pl.when(step == steps - 1)
    def _():
        mean, rstd = moments(r_ref, offset, v_ref.shape[1], c_ref[...])
        normed = (v_ref[...] - mean) * rstd
        grad = out * silu_slope(g_ref[...] * normed + b_ref[...])
        o_ref[...] = grad
        store_back_sums(st_ref, grad, normed)


def reduce_weight_kernel(d_ref, x_ref, a_ref, dw_ref):
    store_weight(dw_ref, d_ref[...], x_ref, a_ref)


def lateral_back_kernel(
    d_ref, n_ref, f_ref, v_ref, x_ref, r_ref, c_ref, g_ref, b_ref, m_ref, l_ref,
    o_ref, on_ref, st_ref, scratch, *, offset, frames
):
    width = v_ref.shape[1]
    wide = width // GROUP
    here = d_ref[...]
    onward = after_rows(scratch, here, n_ref[...], frames)
    on_ref[...] = onward
    back = jnp.concatenate(
        [
            dot_nn(here, l_ref[2]),
            dot_nn(here, l_ref[3]),
            dot_nn(here, l_ref[4]) + dot_nn(onward, l_ref[0]),
            dot_nn(onward, l_ref[1]),
        ],
        axis=1,
    )
    mean, rstd = moments(r_ref, offset, wide, c_ref[...])
    normed = (v_ref[...] - repeat(mean, GROUP)) * repeat(rstd, GROUP)
    mask = rowwise(m_ref[...], width)
    pre = g_ref[...] * normed + b_ref[...] + x_ref[...]
    grad = mask * (f_ref[...] + back) * silu_slope(pre)
    o_ref[...] = grad
    store_back_sums(st_ref, grad, normed, GROUP)


def lateral_weight_kernel(d_ref, on_ref, x_ref, dw_ref):
    wide = dw_ref.shape[2]
    here, onward = d_ref[...], on_ref[...]
    for k, (grad, r) in enumerate(((onward, 2), (onward, 3), (here, 0), (here, 1), (here, 2))):
        dw_ref[k] = dot_tn(grad, x_ref[:, r * wide : (r + 1) * wide])


def fast_expand_back_kernel(
    p_ref, v_ref, r_ref, rb_ref, c_ref, g_ref, u_ref, ru_ref, gu_ref, bu_ref, m_ref, w_ref,
    d_ref, o_ref, st_ref, *, offset, offsetb, offsetu, fold
):
    width = v_ref.shape[1]
    wide, inner = width // GROUP, u_ref.shape[1]
    count = c_ref[...]
    mean, rstd = moments(r_ref, offset, wide, count)
    low, slope = back_sums(rb_ref, offsetb, wide, count)
    mean, rstd, low, slope = [repeat(row, GROUP) for row in (mean, rstd, low, slope)]
    mask = rowwise(m_ref[...], width)
    grad = norm_back(p_ref[...], v_ref[...], mean, rstd, g_ref[...], low, slope, mask)
    d_ref[...] = grad
    mean, rstd = moments(ru_ref, offsetu, inner, count, fold)
    normed = (u_ref[...] - mean) * rstd
    out = rowwise(m_ref[...], inner) * dot_nt(grad, w_ref[...])
    out = out * silu_slope(gu_ref[...] * normed + bu_ref[...])
    o_ref[...] = out
    store_back_sums(st_ref, out, normed)


def transposed_product_kernel(d_ref, x_ref, dw_ref):
    dw_ref[...] = dot_tn(d_ref[...], x_ref[...])


def fast_first_back_kernel(
    d_ref, p_ref, n_ref, res_ref, w_ref, m_ref, x_ref, o_ref, dw_ref, sp_ref, sn_ref,
    matrix, *, frames, inner
):
    grad = d_ref[...]
    width = grad.shape[1]
    before = before_rows(sp_ref, grad, p_ref[...], frames)
    after = after_rows(sn_ref, grad, n_ref[...], frames)
    lane = lax.broadcasted_iota(jnp.int32, (1, width), 1)
    edge = jnp.where(lane < inner, after, jnp.where(lane >= width - inner, before, 0.0))
    both = jnp.concatenate([grad, edge], axis=1)
    mask = rowwise(m_ref[...], o_ref.shape[1])
    o_ref[...] = mask * (dot_nn(both, banded(w_ref, matrix)) + res_ref[...])
    dw_ref[...] = dot_tn(both, x_ref[...])


def load_rows_kernel(own_ref, x_ref, m_ref, o_ref):
    o_ref[...] = x_ref[...].reshape(o_ref.shape) * rowwise(m_ref[...], o_ref.shape[1])


def load_packed_kernel(own_ref, x_ref, o_ref):
    wide = x_ref.shape[1]
    for r in range(GROUP):
        o_ref[:, r * wide : (r + 1) * wide] = x_ref[pl.ds(r, o_ref.shape[0], stride=GROUP), :]


def place_rows_kernel(own_ref, a_ref, b_ref, c_ref, d_ref, o_ref):
    for slot, refs in ((0, (a_ref, c_ref)), (1, (b_ref, d_ref))):
        for own in range(2):

            @pl.when((pl.program_id(0) == slot) & (own_ref[0] == own))
            def _():
                o_ref[...] = refs[own][...].reshape(o_ref.shape)


def place_packed_kernel(own_ref, a_ref, b_ref, c_ref, d_ref, o_ref):
    wide = o_ref.shape[1]
    for slot, refs in ((0, (a_ref, c_ref)), (1, (b_ref, d_ref))):
        for own in range(2):

            @pl.when((pl.program_id(0) == slot) & (own_ref[0] == own))
            def _():
                for r in range(GROUP):
                    o_ref[pl.ds(r, refs[own].shape[0], stride=GROUP), :] = refs[own][
                        :, r * wide : (r + 1) * wide
                    ]


def chosen(kernel, own, grid, ins, in_specs, out, out_spec):
    return pl.pallas_call(
        kernel,
        out_shape=jax.ShapeDtypeStruct(out, jnp.float32),
        grid_spec=pltpu.PrefetchScalarGridSpec(
            num_scalar_prefetch=1, grid=grid, in_specs=in_specs, out_specs=out_spec
        ),
        compiler_params=pltpu.CompilerParams(vmem_limit_bytes=VMEM_BYTES),
    )(own, *ins)


def place_weight_kernel(own_ref, a_ref, b_ref, c_ref, d_ref, o_ref):
    count, rows, width = a_ref.shape
    for own, refs in enumerate(((a_ref, b_ref), (c_ref, d_ref))):

        @pl.when(own_ref[0] == own)
        def _():
            for half, ref in enumerate(refs):
                for k in range(count):
                    o_ref[half * rows : (half + 1) * rows, k * width : (k + 1) * width] = ref[k]


def place_weight(low, high, own):
    to_zero, to_one = cross(low, high)
    count, rows, width = low.shape
    return chosen(
        place_weight_kernel,
        own,
        (1,),
        [low, to_zero, to_one, high],
        [pl.BlockSpec(low.shape, lambda j, o: (0, 0, 0))] * 4,
        (2 * rows, count * width),
        pl.BlockSpec((2 * rows, count * width), lambda j, o: (0, 0)),
    )


def pieces_of(places):
    return max(n for n in range(1, 9) if places % (4 * n) == 0 or n == 1)


def load_rows(values, mask, own):
    grid = jnp.transpose(values[:, 0], (0, 3, 1, 2))
    _, places, frames, wide = grid.shape
    steps = pieces_of(places)
    size = places // steps
    return chosen(
        load_rows_kernel,
        own,
        (steps,),
        [grid, mask],
        [
            pl.BlockSpec((None, size, frames, wide), lambda j, o: (o[0], j, 0, 0)),
            pl.BlockSpec((size * frames, 128), lambda j, o: (j, 0)),
        ],
        (places * frames, wide),
        pl.BlockSpec((size * frames, wide), lambda j, o: (j, 0)),
    )


def packed_view(values):
    grid = jnp.transpose(values[:, 0], (0, 3, 1, 2))
    return grid.reshape(grid.shape[0], -1, grid.shape[3])


def load_packed(values, own):
    grid = packed_view(values)
    _, rows, wide = grid.shape
    out = (rows // GROUP, GROUP * wide)
    return chosen(
        load_packed_kernel,
        own,
        (1,),
        [grid],
        [pl.BlockSpec((None, rows, wide), lambda j, o: (o[0], 0, 0))],
        out,
        pl.BlockSpec(out, lambda j, o: (0, 0)),
    )


def cross(first, second):
    return (
        lax.ppermute(first, "section", [(1, 0)]),
        lax.ppermute(second, "section", [(0, 1)]),
    )


def place_rows(first, second, own, frames):
    to_zero, to_one = cross(first, second)
    rows, wide = first.shape
    places = rows // frames
    steps = pieces_of(places)
    size = places // steps

    def spec(slot, core):
        def where(t, j, o):
            used = (t == slot) & (o[0] == core)
            return (jnp.where(used, j, jnp.where(t > slot, steps - 1, 0)), 0)

        return pl.BlockSpec((size * frames, wide), where)

    out = chosen(
        place_rows_kernel,
        own,
        (2, steps),
        [first, to_zero, to_one, second],
        [spec(0, 0), spec(1, 0), spec(0, 1), spec(1, 1)],
        (2, places, frames, wide),
        pl.BlockSpec((None, size, frames, wide), lambda t, j, o: (t, j, 0, 0)),
    )
    return jnp.transpose(out, (0, 2, 3, 1))[None, :, None]


def place_packed(first, second, own, frames):
    to_zero, to_one = cross(first, second)
    rows, full = first.shape
    wide = full // GROUP
    out = chosen(
        place_packed_kernel,
        own,
        (2,),
        [first, to_zero, to_one, second],
        [pl.BlockSpec((rows, full), lambda t, o: (0, 0))] * 4,
        (2, rows * GROUP, wide),
        pl.BlockSpec((None, rows * GROUP, wide), lambda t, o: (t, 0, 0)),
    )
    grid = out.reshape(2, rows // frames, GROUP * frames, wide)
    return jnp.transpose(grid, (0, 2, 3, 1))[None, :, None]


def bits_of(axis):
    size, stride, found = lax.axis_size(axis), 1, []
    while stride < size:
        found.append((axis, stride))
        stride *= 2
    return found


def routes():
    near, far, deep = bits_of("tm"), [], bits_of("clip")
    middle = len(near) // 2
    near, far = near[:middle], near[middle:]
    one, two, three = near + far + deep, far + deep + near, deep + near + far
    return [list(zip(one, two)), list(zip(two, three)), list(zip(three, one))]


def halves(values, bit, axis=0):
    rows = values.shape[axis] // 2
    kept = lax.dynamic_slice_in_dim(values, bit * rows, rows, axis)
    return kept, lax.dynamic_slice_in_dim(values, (1 - bit) * rows, rows, axis)


def core_half(arrays):
    core = lax.axis_index("section")
    pairs = [halves(x, core, 1) for x in arrays]
    kept, sent = [
        jnp.concatenate([p[k].reshape(-1, p[k].shape[2]) for p in pairs]) for k in range(2)
    ]
    return kept + swap(sent)


def half_pieces(total, arrays):
    pieces, cursor = [], 0
    for x in arrays:
        shape = (x.shape[0], x.shape[1] // 2, x.shape[2])
        rows = shape[0] * shape[1]
        pieces.append(total[cursor : cursor + rows].reshape(shape))
        cursor += rows
    return pieces


def reduction(arrays, route):
    arrays = yield arrays
    total = core_half(arrays)
    bits = [side_of(pair) for pair in route]
    for pair, bit in zip(route, bits):
        (total,) = yield (total,)
        kept, sent = halves(total, bit)
        total = kept + trade(sent, pair)
    for pair, bit in reversed(list(zip(route, bits))):
        (total,) = yield (total,)
        taken = trade(total, pair)
        low, high = jnp.where(bit == 0, total, taken), jnp.where(bit == 0, taken, total)
        total = jnp.concatenate([low, high], axis=0)
    return half_pieces(total, arrays)


def summed(arrays):
    arrays = yield arrays
    total = core_half(arrays)
    (total,) = yield (total,)
    return half_pieces(lax.psum(total, AXES), arrays)


def held_grads(block, names):
    found = yield [block.grads[n] for n in names]
    for name, value in zip(names, found):
        block.grads[name] = value


def side_of(pair):
    sides = [(lax.axis_index(axis) // stride) % 2 for axis, stride in pair]
    return jnp.where(lax.axis_index("section") == 0, sides[0], sides[1])


def trade(values, pair):
    sizes = {axis: lax.axis_size(axis) for axis in AXES}
    partners = []
    for core, (axis, stride) in enumerate(pair):
        for clip in range(sizes["clip"]):
            for tm in range(sizes["tm"]):
                to = {"clip": clip, "tm": tm}
                to[axis] ^= stride
                partners.append(
                    tuple(
                        (core * sizes["clip"] + c) * sizes["tm"] + t
                        for c, t in ((clip, tm), (to["clip"], to["tm"]))
                    )
                )
    return lax.ppermute(values, ("section",) + AXES, partners)


def small_reduction(values):
    axes = ("section",) + AXES
    count = lax.axis_size("section") * lax.axis_size("clip") * lax.axis_size("tm")
    rows = -(-values.shape[0] // count) * count
    shares = jnp.pad(values, ((0, rows - values.shape[0]), (0, 0))).reshape(count, -1, values.shape[1])
    (shares,) = yield (shares,)
    share = jnp.sum(lax.all_to_all(shares, axes, 0, 0), axis=0)
    (share,) = yield (share,)
    copies = jnp.broadcast_to(share[None], (count,) + share.shape)
    out = lax.all_to_all(copies, axes, 0, 0).reshape(rows, -1)
    return out[: values.shape[0]]


class Job:
    def __init__(self, steps, paces=(1,)):
        self.steps, self.paces, self.result = steps, list(paces), None
        self.held = next(steps)

    def resume(self, held):
        for _ in range(self.paces.pop(0) if len(self.paces) > 1 else self.paces[0]):
            try:
                held = self.steps.send(held)
            except StopIteration as end:
                self.held, self.result = None, end.value
                return
        self.held = held

    def finish(self):
        while self.held is not None:
            self.resume(self.held)
        return self.result


class Section:
    def __init__(self, index, small, large):
        self.fast_reduce, spatial, expand, gain, bias = [x[index] for x in small]
        inner, wide = self.fast_reduce.shape[1], self.fast_reduce.shape[2]
        self.lateral, self.slow_reduce, self.slow_spatial, self.slow_expand, self.shortcut = [
            Stacked(x, index) for x in large
        ]
        self.inner, self.wide, self.depth = inner, wide, self.slow_expand.shape[1]
        eye = jnp.eye(GROUP, dtype=jnp.float32)
        self.fast_spatial = jnp.einsum("rq,koi->kqori", eye, spatial, precision="highest").reshape(
            spatial.shape[0], GROUP * inner, GROUP * inner
        )
        self.fast_expand = jnp.einsum("rq,oi->riqo", eye, expand, precision="highest").reshape(
            GROUP * inner, GROUP * wide
        )
        widths = [
            inner, inner, wide, self.lateral.shape[1], self.depth, self.depth,
            self.slow_expand.shape[0], self.shortcut.shape[0],
        ]
        repeats = [GROUP, GROUP, GROUP, 1, 1, 1, 1, 1]
        self.widths, self.gains, self.biases, cursor = widths, [], [], 0
        for width, times in zip(widths, repeats):
            self.gains.append(jnp.tile(gain[None, cursor : cursor + width], (1, times)))
            self.biases.append(jnp.tile(bias[None, cursor : cursor + width], (1, times)))
            cursor += width


class Block:
    def __init__(self, section, mask, frames, shared):
        self.s, self.mask, self.frames, self.shared = section, mask, frames, shared
        self.rows = mask.shape[0]
        self.places = self.rows // frames
        self.side = math.isqrt(self.places)
        self.pad = -(-(self.side + 1) * frames // 8) * 8
        self.grads, self.sums, self.back = {}, {}, {}

    def window(self, width):
        return [(self.rows + 2 * self.pad, width)] * 3

    def lanes(self, width):
        return (width // 128, self.rows, 128)

    def fast_first(self, fast_input, own):
        rows, places, width = self.rows, self.places, GROUP * self.s.inner
        grid, full = packed_view(fast_input), GROUP * self.s.wide
        outs = [(rows, full), (rows, 2 * width), (places, width), (places, width)]
        return pl.pallas_call(
            partial(fast_first_kernel, frames=self.frames),
            out_shape=[jax.ShapeDtypeStruct(s, jnp.float32) for s in outs],
            grid_spec=pltpu.PrefetchScalarGridSpec(
                num_scalar_prefetch=1,
                grid=(1,),
                in_specs=[
                    pl.BlockSpec((None,) + grid.shape[1:], lambda j, o: (o[0], 0, 0)),
                    pl.BlockSpec((rows, 128), lambda j, o: (0, 0)),
                    pl.BlockSpec(self.s.fast_reduce.shape, lambda j, o: (0, 0, 0)),
                ],
                out_specs=[pl.BlockSpec(s, lambda j, o: (0, 0)) for s in outs],
                scratch_shapes=[
                    pltpu.VMEM(self.lanes(width), jnp.float32),
                    pltpu.VMEM((2 * width, full), jnp.float32),
                ],
            ),
            compiler_params=pltpu.CompilerParams(vmem_limit_bytes=VMEM_BYTES),
        )(own, grid, self.mask, self.s.fast_reduce)

    def fast_forward(self, fast_in, parts):
        s, mask, frames, rows, places = self.s, self.mask, self.frames, self.rows, self.places
        c4 = self.shared
        self.fast_in = fast_in
        width, full = GROUP * s.inner, GROUP * s.wide
        both, low, high = parts
        self.first, sums = call(
            fast_join_kernel,
            [(rows, width), (1, 2 * width)],
            [both, from_previous(high), from_next(low), mask],
            [self.lanes(width)] * 2,
            frames=frames,
            inner=s.inner,
        )
        self.sums[0] = yield sums
        second, self.first_act, sums = call(
            conv_kernel,
            [(rows, width), (rows, width), (1, 2 * width)],
            [self.first, self.sums[0][0], c4["fast"], s.gains[0], s.biases[0], mask, s.fast_spatial],
            self.window(width),
            offset=self.sums[0][1], fold=s.inner, side=self.side, frames=frames,
        )
        self.second = second
        self.sums[1] = yield sums
        self.third, self.second_act, sums = call(
            fast_expand_kernel,
            [(rows, full), (rows, width), (1, 2 * s.wide)],
            [second, self.sums[1][0], c4["fast"], s.gains[1], s.biases[1], mask, s.fast_expand],
            offset=self.sums[1][1], fold=s.inner,
        )
        self.sums[2] = yield sums
        following = (self.following or self).s.fast_reduce
        lateral = s.widths[3]
        shapes = [(rows, full), (rows, lateral), (rows, lateral), (places, lateral)]
        if self.following:
            shapes += [(rows, 2 * width), (places, width), (places, width)]
        else:
            shapes += [(8, 256), (8, 128), (8, 128)]
        self.fast_out, here, onward, edge, *self.parts = call(
            fast_out_kernel,
            shapes,
            [
                self.third, fast_in, self.sums[2][0], c4["fast"], s.gains[2], s.biases[2], mask,
                s.lateral, following,
            ],
            [self.lanes(lateral), (2 * width, full)],
            offset=self.sums[2][1], frames=frames, more=self.following is not None,
        )
        self.lateral, sums = call(
            lateral_join_kernel,
            [(rows, lateral), (1, 2 * lateral)],
            [here, onward, from_previous(edge), mask],
            [self.lanes(lateral)],
            frames=frames,
        )
        self.sums[3] = yield sums

    def slow_forward(self, slow_in):
        s, mask, frames, rows, places = self.s, self.mask, self.frames, self.rows, self.places
        count = self.shared["slow"]
        depth, lateral, wide, out_wide = s.depth, s.widths[3], slow_in.shape[1], s.widths[7]
        full = wide + lateral
        self.slow_in = slow_in
        r3, offset = self.sums[3]
        reduced, low, high, self.lateral_act = call_steps(
            reduce_kernel,
            3,
            [(rows, 3 * depth), (places, depth), (places, depth), (rows, lateral)],
            [columns(rows, depth), fixed((places, depth)), fixed((places, depth)), fixed((rows, lateral))],
            [slow_in, self.lateral, r3, count, s.gains[3], s.biases[3], mask, s.slow_reduce],
            [
                fixed((rows, wide)), fixed((rows, lateral)), fixed(r3.shape), fixed((1, 1)),
                fixed((1, lateral)), fixed((1, lateral)), fixed((rows, 128)),
                s.slow_reduce.block((depth, full), lambda j: (j, 0)),
            ],
            [(rows, full), self.lanes(depth)],
            offset=offset, frames=frames,
        )
        steps = out_wide // depth
        self.skipped, skip_sum, skip_square = call_steps(
            shortcut_kernel,
            steps,
            [(rows, out_wide), (1, out_wide), (1, out_wide)],
            [columns(rows, depth), columns(1, depth), columns(1, depth)],
            [slow_in, self.lateral_act, mask, s.shortcut],
            [
                fixed((rows, wide)), fixed((rows, lateral)), fixed((rows, 128)),
                s.shortcut.block((depth, full), lambda j: (j, 0)),
            ],
        )
        self.inner, sums = call(
            inner_join_kernel,
            [(rows, depth), (1, 2 * depth)],
            [reduced, from_previous(high), from_next(low), mask],
            [self.lanes(depth)] * 2,
            frames=frames,
        )
        r, offset = yield jnp.concatenate([sums, skip_sum, skip_square], axis=1)
        self.sums[4], self.sums[7] = (r, offset), (r, offset + 2 * depth)
        self.middle, self.inner_act, sums = call(
            conv_kernel,
            [(rows, depth), (rows, depth), (1, 2 * depth)],
            [self.inner, r, count, s.gains[4], s.biases[4], mask, s.slow_spatial],
            self.window(depth),
            offset=offset, fold=0, side=self.side, frames=frames,
        )
        self.sums[5] = yield sums
        r5, offset = self.sums[5]
        self.expanded, self.middle_act, total, square = call_steps(
            expand_kernel,
            steps,
            [(rows, out_wide), (rows, depth), (1, out_wide), (1, out_wide)],
            [columns(rows, depth), fixed((rows, depth)), columns(1, depth), columns(1, depth)],
            [self.middle, r5, count, s.gains[5], s.biases[5], mask, s.slow_expand],
            [
                fixed((rows, depth)), fixed(r5.shape), fixed((1, 1)), fixed((1, depth)),
                fixed((1, depth)), fixed((rows, 128)),
                s.slow_expand.block((depth, depth), lambda j: (j, 0)),
            ],
            offset=offset,
        )
        self.sums[6] = yield jnp.concatenate([total, square], axis=1)
        self.slow_out = call_steps(
            slow_out_kernel,
            steps,
            [(rows, out_wide)],
            [columns(rows, depth)],
            *self.slow_pre_inputs(),
            offset6=self.sums[6][1], offset7=self.sums[7][1], total=out_wide,
        )[0]

    def slow_pre_inputs(self):
        s, rows, depth = self.s, self.rows, self.s.depth
        r6, r7 = self.sums[6][0], self.sums[7][0]
        wide, row = columns(rows, depth), columns(1, depth)
        return (
            [
                self.expanded, self.skipped, r6, r7, self.shared["slow"], s.gains[6], s.biases[6],
                s.gains[7], s.biases[7], self.mask,
            ],
            [
                wide, wide, fixed(r6.shape), fixed(r7.shape), fixed((1, 1)), row, row, row, row,
                fixed((rows, 128)),
            ],
        )

    def slow_backward(self, slow_grad):
        s, mask, frames, rows, places = self.s, self.mask, self.frames, self.rows, self.places
        count = self.shared["slow"]
        depth, lateral, out_wide, wide = s.depth, s.widths[3], s.widths[7], self.slow_in.shape[1]
        full, steps = wide + lateral, out_wide // depth
        (r6, offset6), (r7, offset7) = self.sums[6], self.sums[7]
        ins, specs = self.slow_pre_inputs()
        pre, low, slope6, slope7 = call_steps(
            slow_slope_kernel,
            steps,
            [(rows, out_wide)] + [(1, out_wide)] * 3,
            [columns(rows, depth)] + [columns(1, depth)] * 3,
            [slow_grad] + ins,
            [columns(rows, depth)] + specs,
            offset6=offset6, offset7=offset7, total=out_wide,
        )
        rb, offsetb = yield jnp.concatenate([low, slope6, slope7], axis=1)
        self.back[6], self.back[7] = (rb, offsetb, offsetb + out_wide), (rb, offsetb, offsetb + 2 * out_wide)
        r5, offset5 = self.sums[5]
        skip_grad, self.grads["slow_expand"], pre, sums = call_steps(
            expand_back_kernel,
            steps,
            [(rows, out_wide), (out_wide, depth), (rows, depth), (1, 2 * depth)],
            [columns(rows, depth), bands(depth, depth), fixed((rows, depth)), fixed((1, 2 * depth))],
            [
                pre, self.expanded, self.skipped, r6, r7, rb, count, s.gains[6], s.gains[7], mask,
                s.slow_expand, self.middle_act, self.middle, r5, s.gains[5], s.biases[5],
            ],
            [columns(rows, depth)] * 3
            + [fixed(r6.shape), fixed(r7.shape), fixed(rb.shape), fixed((1, 1))]
            + [columns(1, depth)] * 2
            + [fixed((rows, 128)), s.slow_expand.block((depth, depth), lambda j: (j, 0))]
            + [fixed((rows, depth)), fixed((rows, depth))]
            + [fixed(r5.shape), fixed((1, depth)), fixed((1, depth))],
            [(rows, depth)],
            offset6=offset6, offset7=offset7, offsetb=offsetb, offset5=offset5, total=out_wide,
        )
        self.grads["shortcut"], joined_grad = call_steps(
            shortcut_back_kernel,
            steps,
            [(full // lateral, out_wide, lateral), (rows, full)],
            [pl.BlockSpec((full // lateral, depth, lateral), lambda j: (0, j, 0)), fixed((rows, full))],
            [skip_grad, s.shortcut, self.slow_in, self.lateral_act],
            [
                columns(rows, depth), s.shortcut.block((depth, full), lambda j: (j, 0)),
                fixed((rows, wide)), fixed((rows, lateral)),
            ],
        )
        rb, offsetb = yield sums
        self.back[5] = (rb, offsetb, offsetb + depth)
        r4, offset4 = self.sums[4]
        middle_grad, pre, sums = call(
            conv_back_kernel,
            [(rows, depth), (rows, depth), (1, 2 * depth)],
            [
                pre, self.middle, r5, rb, count, s.gains[5], self.inner, r4, s.gains[4], s.biases[4],
                mask, s.slow_spatial,
            ],
            self.window(depth),
            offset=offset5, offsetb=offsetb, offsetu=offset4, fold=0, side=self.side, frames=frames,
        )
        self.grads["slow_spatial"] = call(
            conv_weight_kernel,
            [s.slow_spatial.shape],
            [self.inner_act, middle_grad],
            self.window(depth),
            side=self.side, frames=frames,
        )[0]
        rb, offsetb = yield sums
        self.back[4] = (rb, offsetb, offsetb + depth)
        inner_grad, low, high = call(
            norm_back_kernel,
            [(rows, depth), (places, depth), (places, depth)],
            [pre, self.inner, r4, rb, count, s.gains[4], mask],
            [self.lanes(depth)],
            offset=offset4, offsetb=offsetb, fold=0, frames=frames,
        )
        r3, offset3 = self.sums[3]
        last = wide // lateral
        self.slow_in_grad, self.lateral_pre, reduced_grad, self.lateral_sums = call_steps(
            joined_back_kernel,
            last + 1,
            [(rows, wide), (rows, lateral), (rows, 3 * depth), (1, 2 * lateral)],
            [
                pl.BlockSpec((rows, lateral), lambda j: (0, jnp.minimum(j, last - 1))),
                fixed((rows, lateral)), fixed((rows, 3 * depth)), fixed((1, 2 * lateral)),
            ],
            [
                inner_grad, from_previous(high), from_next(low), joined_grad, s.slow_reduce, mask,
                self.lateral, r3, count, s.gains[3], s.biases[3],
            ],
            [
                fixed((rows, depth)), fixed((places, depth)), fixed((places, depth)),
                columns(rows, lateral), s.slow_reduce.block((3 * depth, lateral), lambda j: (0, j)),
                fixed((rows, 128)),
                fixed((rows, lateral)), fixed(r3.shape), fixed((1, 1)), fixed((1, lateral)),
                fixed((1, lateral)),
            ],
            [self.lanes(depth)],
            offset=offset3, frames=frames,
        )
        self.grads["slow_reduce"] = call_steps(
            reduce_weight_kernel,
            3,
            [(full // lateral, 3 * depth, lateral)],
            [pl.BlockSpec((full // lateral, depth, lateral), lambda j: (0, j, 0))],
            [reduced_grad, self.slow_in, self.lateral_act],
            [columns(rows, depth), fixed((rows, wide)), fixed((rows, lateral))],
        )[0]

    def fast_backward(self, fast_grad):
        s, mask, frames, rows, places = self.s, self.mask, self.frames, self.rows, self.places
        count, count4 = self.shared["slow"], self.shared["fast"]
        wide, inner, lateral = s.wide, s.inner, s.widths[3]
        width, full = GROUP * inner, GROUP * wide
        rb, offsetb = yield self.lateral_sums
        self.back[3] = (rb, offsetb, offsetb + lateral)
        r3, offset3 = self.sums[3]
        here, low, _ = call(
            norm_back_kernel,
            [(rows, lateral), (places, lateral), (places, lateral)],
            [self.lateral_pre, self.lateral, r3, rb, count, s.gains[3], mask],
            [self.lanes(lateral)],
            offset=offset3, offsetb=offsetb, fold=0, frames=frames,
        )
        r2, offset2 = self.sums[2]
        residual, onward, sums = call(
            lateral_back_kernel,
            [(rows, full), (rows, lateral), (1, 2 * wide)],
            [
                here, from_next(low), fast_grad(), self.third, self.fast_in, r2, count4, s.gains[2],
                s.biases[2], mask, s.lateral,
            ],
            [self.lanes(lateral)],
            offset=offset2, frames=frames,
        )
        self.grads["lateral"] = call(
            lateral_weight_kernel, [(5, lateral, wide)], [here, onward, self.fast_out]
        )[0]
        rb, offsetb = yield sums
        self.back[2] = (rb, offsetb, offsetb + wide)
        r1, offset1 = self.sums[1]
        third_grad, pre, sums = call(
            fast_expand_back_kernel,
            [(rows, full), (rows, width), (1, 2 * width)],
            [
                residual, self.third, r2, rb, count4, s.gains[2], self.second, r1, s.gains[1],
                s.biases[1], mask, s.fast_expand,
            ],
            offset=offset2, offsetb=offsetb, offsetu=offset1, fold=inner,
        )
        grid = call(transposed_product_kernel, [(full, width)], [third_grad, self.second_act])[0]
        grid = grid.reshape(GROUP, wide, GROUP, inner)
        self.grads["fast_expand"] = sum(grid[r, :, r] for r in range(GROUP))
        rb, offsetb = yield sums
        self.back[1] = (rb, offsetb, offsetb + width)
        r0, offset0 = self.sums[0]
        second_grad, pre, sums = call(
            conv_back_kernel,
            [(rows, width), (rows, width), (1, 2 * width)],
            [
                pre, self.second, r1, rb, count4, s.gains[1], self.first, r0, s.gains[0], s.biases[0],
                mask, s.fast_spatial,
            ],
            self.window(width),
            offset=offset1, offsetb=offsetb, offsetu=offset0, fold=inner, side=self.side,
            frames=frames,
        )
        grid = call(
            conv_weight_kernel,
            [s.fast_spatial.shape],
            [self.first_act, second_grad],
            self.window(width),
            side=self.side, frames=frames,
        )[0]
        grid = grid.reshape(-1, GROUP, inner, GROUP, inner)
        self.grads["fast_spatial"] = sum(grid[:, r, :, r] for r in range(GROUP))
        rb, offsetb = yield sums
        self.back[0] = (rb, offsetb, offsetb + width)
        first_grad, low, high = call(
            norm_back_kernel,
            [(rows, width), (places, width), (places, width)],
            [pre, self.first, r0, rb, count4, s.gains[0], mask],
            [self.lanes(width)],
            offset=offset0, offsetb=offsetb, fold=inner, frames=frames,
        )
        self.fast_in_grad, grid = call(
            fast_first_back_kernel,
            [(rows, full), (2 * width, full)],
            [
                first_grad, from_previous(high), from_next(low), residual, s.fast_reduce, mask,
                self.fast_in,
            ],
            [self.lanes(width)] * 2 + [(2 * width, full)],
            frames=frames, inner=inner,
        )
        grid = grid.reshape(2, GROUP, inner, GROUP, wide)
        near, far = grid[0], grid[1]
        self.grads["fast_reduce"] = jnp.stack(
            [
                near[1, :, 0] + near[2, :, 1] + near[3, :, 2] + far[0, :, 3],
                near[0, :, 0] + near[1, :, 1] + near[2, :, 2] + near[3, :, 3],
                near[0, :, 1] + near[1, :, 2] + near[2, :, 3] + far[3, :, 0],
            ]
        )

    def blocked(self, name):
        grad = self.grads[name]
        if name == "lateral":
            taps, depth, wide = grad.shape
            grad = jnp.pad(grad, ((0, taps % 2), (0, 0), (0, 0))).reshape(-1, 2, depth, wide)
            return jnp.swapaxes(grad, 1, 2).reshape(-1, depth, 2 * wide)
        return grad if grad.ndim == 3 else grad[None]

    def fast_flat(self):
        names = ("fast_reduce", "fast_spatial", "fast_expand")
        flat = jnp.concatenate([self.grads[n].reshape(-1) for n in names])
        return jnp.pad(flat, (0, -flat.shape[0] % 1024)).reshape(-1, 128)

    def norm_grads(self):
        gains, biases = [], []
        for j, width in enumerate(self.s.widths):
            rb, low, slope = self.back[j]
            span = GROUP * width if j < 2 else width
            for start, found in ((slope, gains), (low, biases)):
                total = jnp.sum(rb[:, start : start + span], axis=0)
                found.append(jnp.sum(total.reshape(-1, width), axis=0))
        return jnp.stack([jnp.concatenate(gains), jnp.concatenate(biases)])


class Task:
    def __init__(self, steps):
        self.steps = steps
        self.wanted = next(steps)

    def resume(self, totals):
        self.wanted = next(self.steps, None) if totals is None else self.send(totals)

    def send(self, totals):
        try:
            return self.steps.send(totals)
        except StopIteration:
            return None


def advance(*tasks, extra=None, jobs=()):
    wanted = [task.wanted for task in tasks] + ([] if extra is None else [extra])
    r = sums_everywhere(jnp.concatenate(wanted, axis=1))
    jobs = [job for job in jobs if job.held is not None]
    if jobs:
        r, held = lax.optimization_barrier((r, [job.held for job in jobs]))
        for job, values in zip(jobs, held):
            job.resume(values)
    offsets = [sum(w.shape[1] for w in wanted[:k]) for k in range(len(wanted))]
    return [(r, offset) for offset in offsets]


def body(
    slow_input,
    fast_input,
    frame_counts,
    fast_reduce,
    fast_spatial,
    fast_expand,
    lateral_conv,
    slow_reduce,
    slow_spatial,
    slow_expand,
    shortcut,
    norm_gain,
    norm_bias,
    slow_cotangent,
    fast_cotangent,
):
    own = lax.axis_index("section")
    lower = own == 0
    frames, positions = slow_input.shape[2], slow_input.shape[4]
    rows = frames * positions
    wide = fast_input.shape[3]

    which = jnp.reshape(own, (1,)).astype(jnp.int32)
    small = [fast_reduce[0], fast_spatial[0], fast_expand[0], norm_gain[0], norm_bias[0]]
    flat = jnp.concatenate([x.reshape(-1) for x in small])
    flat = jnp.pad(flat, (0, -flat.shape[0] % 1024)).reshape(-1, 128)
    flat = lax.all_gather(flat, "section").reshape(2, -1)
    gathered, cursor = [], 0
    for x in small:
        gathered.append(flat[:, cursor : cursor + x.size].reshape((2,) + x.shape))
        cursor += x.size
    large = [
        lateral_conv[0],
        slow_reduce[0].reshape(-1, slow_reduce.shape[3]),
        slow_spatial[0],
        slow_expand[0],
        shortcut[0],
    ]
    large = [lax.all_gather(x, "section") for x in large]
    sections = [Section(index, gathered, large) for index in range(2)]

    count_here = lax.dynamic_index_in_dim(frame_counts, own, 0, keepdims=False)
    frame = lax.axis_index("clip") * frames + lax.broadcasted_iota(
        jnp.int32, (positions, frames, 128), 1
    )
    mask = (frame < count_here).astype(jnp.float32).reshape(rows, 128)
    shared = {}
    blocks = [Block(section, mask, frames, shared) for section in sections]
    blocks[0].following, blocks[1].following = blocks[1], None

    fast_in, *parts = blocks[0].fast_first(fast_input, which)
    fast = [Task(blocks[0].fast_forward(fast_in, parts)), None]
    got = advance(fast[0], extra=jnp.sum(mask, axis=0, keepdims=True))
    r, offset = got[1]
    shared["slow"] = jnp.sum(r[:, offset : offset + 1], axis=0, keepdims=True)
    shared["fast"] = GROUP * shared["slow"]
    fast[0].resume(got[0])
    for step in range(2):
        fast[0].resume(advance(fast[0])[0])
    fast[1] = Task(blocks[1].fast_forward(blocks[0].fast_out, blocks[0].parts))
    got = advance(fast[0], fast[1])
    fast[0].resume(got[0])
    fast[1].resume(got[1])
    slow = [Task(blocks[0].slow_forward(load_rows(slow_input, mask, which))), None]
    for step in range(3):
        got = advance(slow[0], fast[1])
        slow[0].resume(got[0])
        fast[1].resume(got[1])
    slow[1] = Task(blocks[1].slow_forward(blocks[0].slow_out))
    for step in range(3):
        slow[1].resume(advance(slow[1])[0])

    zero, one = blocks
    ways = routes()
    jobs = []

    def start(steps, paces=(1,)):
        jobs.append(Job(steps, paces))
        return jobs[-1]

    tasks = Task(one.slow_backward(load_rows(slow_cotangent, mask, which)))
    tasks.resume(advance(tasks)[0])
    soonest = start(
        reduction([one.blocked(n) for n in ("shortcut", "slow_expand")], ways[0]), (2, 2, 2, 2, 1)
    )
    tasks.resume(advance(tasks, jobs=jobs)[0])
    start(held_grads(one, ("slow_spatial",)))
    tasks.resume(advance(tasks, jobs=jobs)[0])
    start(held_grads(one, ("slow_reduce",)))
    late = Task(one.fast_backward(lambda: load_packed(fast_cotangent, which)))
    soon = Task(zero.slow_backward(one.slow_in_grad))
    for step in range(3):
        got = advance(late, soon, jobs=jobs)
        late.resume(got[0])
        soon.resume(got[1])
        if step == 0:
            whole = start(
                reduction(
                    [one.blocked(n) for n in ("slow_spatial", "slow_reduce", "lateral")], ways[1]
                ),
                (2, 2, 2, 2, 1),
            )
            early = start(
                reduction([zero.blocked(n) for n in ("shortcut", "slow_expand")], ways[2]),
                (1, 1, 2, 2, 2, 1),
            )
        if step == 1:
            start(held_grads(zero, ("slow_spatial",)))
        if step == 2:
            start(held_grads(zero, ("slow_reduce",)))
    last = Task(zero.fast_backward(lambda: one.fast_in_grad))
    got = advance(late, last, jobs=jobs)
    late.resume(got[0])
    last.resume(got[1])
    middle = start(
        reduction([zero.blocked(n) for n in ("slow_spatial", "slow_reduce", "lateral")], ways[0]),
        (2, 2, 2, 1),
    )
    middle.resume(middle.held)
    for step in range(3):
        last.resume(advance(last, jobs=jobs)[0])
    rest = Job(small_reduction(jnp.concatenate([zero.fast_flat(), one.fast_flat()]))).finish()

    totals = {}
    halves_one = dict(zip(("shortcut", "slow_expand"), soonest.finish()))
    halves_one.update(zip(("slow_spatial", "slow_reduce", "lateral"), whole.finish()))
    halves_zero = dict(zip(("shortcut", "slow_expand"), early.finish()))
    halves_zero.update(zip(("slow_spatial", "slow_reduce", "lateral"), middle.finish()))
    for name in ("shortcut", "slow_reduce", "slow_expand"):
        totals[name] = place_weight(halves_zero[name], halves_one[name], which)
    for name in ("slow_spatial", "lateral"):
        low, high = halves_zero[name], halves_one[name]
        to_zero, to_one = cross(low, high)
        totals[name] = jnp.concatenate(
            [jnp.where(lower, low, to_one), jnp.where(lower, to_zero, high)], axis=1
        )
    pairs, depth, double = totals["lateral"].shape
    lateral = totals["lateral"].reshape(pairs, depth, 2, double // 2)
    lateral = jnp.swapaxes(lateral, 1, 2).reshape(2 * pairs, depth, -1)
    totals["lateral"] = lateral[: lateral_conv.shape[1]]
    rows = rest.shape[0] // 2
    flat, cursor = jnp.where(lower, rest[:rows], rest[rows:]).reshape(-1), 0
    for name, x in zip(("fast_reduce", "fast_spatial", "fast_expand"), small):
        totals[name] = flat[cursor : cursor + x.size]
        cursor += x.size
    names = (
        "fast_reduce",
        "fast_spatial",
        "fast_expand",
        "lateral",
        "slow_reduce",
        "slow_spatial",
        "slow_expand",
        "shortcut",
    )
    norm_grads = [block.norm_grads() for block in blocks]
    kept = jnp.where(lower, norm_grads[0], norm_grads[1])
    kept = kept + swap(jnp.where(lower, norm_grads[1], norm_grads[0]))
    shapes = [
        x.shape
        for x in (
            fast_reduce, fast_spatial, fast_expand, lateral_conv, slow_reduce, slow_spatial,
            slow_expand, shortcut,
        )
    ]
    totals = [totals[name].reshape(shape) for name, shape in zip(names, shapes)]
    return (
        place_rows(zero.slow_out, one.slow_out, which, frames),
        place_packed(zero.fast_out, one.fast_out, which, frames),
        place_rows(zero.slow_in_grad, one.slow_in_grad, which, frames),
        place_packed(zero.fast_in_grad, one.fast_in_grad, which, frames),
        *totals,
        kept[None, 0],
        kept[None, 1],
    )


def solution(mesh):
    acts = P(None, "tm", "clip", None, None)
    outs = P("section", None, "tm", "clip", None, None)
    four, three, two = P("section", None, None, None), P("section", None, None), P("section", None)
    weights = (four, four, three, four, four, four, three, three)
    return jax.shard_map(
        body,
        mesh=mesh,
        in_specs=(acts, acts, P(None, "tm"), *weights, two, two, acts, acts),
        out_specs=(outs, outs, outs, outs, *weights, two, two),
        check_vma=False,
    )
```

time: 1500 us -> 1170 us (0.78)
  Pallas kernels: 0 us -> 432 us
  waiting for transfers between devices: 468 us -> 171 us
  matrix products: 295 us -> 0 us
  local copies, waits for them, and re-layouts: 302 us -> 142 us
  other arithmetic: 209 us -> 103 us
  starting transfers between devices: 187 us -> 238 us
  blocking collectives: 0 us -> 46 us
    pallas_call x0 -> x67, Pallas kernels: none -> 432 us  [the longest x18 202 us: call_steps(): pl.pallas_call(partial(kernel, **static), grid=(steps,), out_shape=[jax.S...]
    psum x2 -> x0, waiting for transfers between devices: 394 us -> none  [body(): totals = lax.psum(tuple(partial), AXES)]
    dot_general x64 -> x0, matrix products: 236 us -> none  [the longest x20 87.6 us: dot_tn(): return lax.dot_general(a, b, (((0,), (0,)), ((), ())), precision=FINE)]
    ppermute x8 -> x50, waiting for transfers between devices: 0.02 us -> 100 us  [the longest x32 100 us: trade(): return lax.ppermute(values, ('section',) + AXES, partners)]
    ppermute x8 -> x50, starting transfers between devices: 17.2 us -> 92.5 us  [the longest x32 52.3 us: trade(): return lax.ppermute(values, ('section',) + AXES, partners)]
    conv_general_dilated x12 -> x0, matrix products: 58.2 us -> none  [conv_grid(): lax.conv_general_dilated(grid, kernel, (1, 1), 'SAME', dimension_numbers=...]
    reshape x64 -> x25, local copies, waits for them, and re-layouts: 81.9 us -> 24.2 us  [the longest x2 6.48 us: fast_backward(): grid = grid.reshape(-1, GROUP, inner, GROUP, inner)]
    all_to_all x0 -> x4, blocking collectives: none -> 43.9 us  [sums_everywhere(): return lax.all_to_all(copies, AXES, 0, 0)]
  transfers between devices with their start and end apart: 65 -> 98, of which waited for: 21 -> 31; matrix products, arithmetic and copies ran while one was open for 51% -> 17% of each run, Pallas kernels for 0% -> 32%
where the time goes in v2:
time: 1170 us; the launch traced here: 1150 us
  Pallas kernels  432 us (37%)
  starting transfers between devices  238 us (20%)
  waiting for transfers between devices  171 us (15%)
  local copies, waits for them, and re-layouts  142 us (12%)
  other arithmetic  103 us (9%)
  blocking collectives  46 us (4%)
  between operations  17.2 us (1%)
    pallas_call x18, Pallas kernels, call_steps(): pl.pallas_call(partial(kernel, **static), grid=(steps,), out_shape=[jax.S...  202 us
    pallas_call x38, Pallas kernels, call(): pl.pallas_call(partial(kernel, **static), grid=(1,), out_shape=[jax.Shape...  167 us
    ppermute x32, waiting for transfers between devices, trade(): return lax.ppermute(values, ('section',) + AXES, partners)  100 us
    all_to_all x16, starting transfers between devices, sums_everywhere(): return lax.all_to_all(copies, AXES, 0, 0)  88 us
    pallas_call x10, Pallas kernels, chosen(): pl.pallas_call(kernel, out_shape=jax.ShapeDtypeStruct(out, jnp.float32),...  60.2 us
    ppermute x32, starting transfers between devices, trade(): return lax.ppermute(values, ('section',) + AXES, partners)  52.3 us
    all_to_all x4, blocking collectives, sums_everywhere(): return lax.all_to_all(copies, AXES, 0, 0)  43.9 us
    ppermute x10, starting transfers between devices, from_previous(): return lax.ppermute(edge, 'clip', [(i, i + 1) for i in range(count - 1)])  33.4 us
  transfers between devices with their start and end apart: 98, of which 31 were waited for; matrix products, arithmetic and copies ran while one was open for 17% of the time, Pallas kernels for 32%

profile of v2, /device:TPU:0, one launch (start us, length us, event | category | flops | bytes accessed | tf_op | source)
XLA Modules:
  0.0 1149.2 jit_solution(5228977686223958262)
XLA Ops:
  122.8 10.7 shard_map.262
  148.8 10.7 shard_map.264
  188.7 10.4 all_to_all.179
  239.2 10.7 shard_map.272
  256.1 10.8 shard_map.274
  271.7 10.5 all_to_all.180
  290.5 10.2 all_to_all.181
  330.8 12.8 %all_to_all.182 = f32[16,1,3072]{2,1,0:T(1,128)S(1)} all-to-all(f32[16,1,3072]{2,1,0:T(1,128)S(1)} %broadcast_in_dim.69), channel_id=1, replica_groups=mesh['section'=2,'clip'=4,'tm'=4] {'clip','tm'}, dimensions={0} | all-to-all | bytes 393216 | tf_op jit(solution)/shard_map/all_to_all | solution.py:32
  344.4 11.5 shard_map.282
  360.8 21.8 %shard_map.283 = (f32[5,1024,256]{2,1,0:T(8,128)}, f32[784,1280]{1,0:T(8,128)}) custom-call(f32[784,1024]{1,0:T(8,128)} %get-tuple-element.255.d_ref, f32[2,1024,1280]{2,1,0:T(8,128)} %all-gather.10.cloned.1.call-done.w_ref, f32[784,1024]{1,0:T(8,128)} %shard_map.271.x_ref.a_ref, f32[784,256]{1,0:T(8,128)} %get-tuple-element.238.a_ref), custom_call_target="tpu_custom_call" | custom-call | tf_op jit(solution)/shard_map/pallas_call | solution.py:139
  443.7 12.9 %shard_map.287 = (f32[784,1024]{1,0:T(8,128)}, f32[784,256]{1,0:T(8,128)}, f32[784,768]{1,0:T(8,128)}, f32[1,512]{1,0:T(1,128)}) custom-call(f32[784,256]{1,0:T(8,128)} %get-tuple-element.266.d_ref, f32[196,256]{1,0:T(8,128)} %copy-done.58, f32[196,256]{1,0:T(8,128)} %copy-done.59, f32[784,1280]{1,0:T(8,128)} %get-tuple-element.269.j_ref, ...), custom_call_target="tpu_custom_call" | custom-call | tf_op jit(solution)/shard_map/pallas_call | solution.py:139
  474.5 10.7 shard_map.289
  498.9 11.4 shard_map.290
  524.9 22.0 %shard_map.295 = (f32[5,1024,256]{2,1,0:T(8,128)}, f32[784,1280]{1,0:T(8,128)}) custom-call(f32[784,1024]{1,0:T(8,128)} %get-tuple-element.290.d_ref, f32[2,1024,1280]{2,1,0:T(8,128)} %all-gather.10.cloned.1.call-done.w_ref, f32[784,1024]{1,0:T(8,128)} %shard_map.254.x_ref, f32[784,256]{1,0:T(8,128)} %get-tuple-element.213.a_ref), custom_call_target="tpu_custom_call" | custom-call | tf_op jit(solution)/shard_map/pallas_call | solution.py:139
  682.7 12.8 %shard_map.300 = (f32[784,1024]{1,0:T(8,128)}, f32[784,256]{1,0:T(8,128)}, f32[784,768]{1,0:T(8,128)}, f32[1,512]{1,0:T(1,128)}) custom-call(f32[784,256]{1,0:T(8,128)} %get-tuple-element.307.d_ref, f32[196,256]{1,0:T(8,128)} %copy-done.48, f32[196,256]{1,0:T(8,128)} %copy-done.49, f32[784,1280]{1,0:T(8,128)} %get-tuple-element.310.j_ref, ...), custom_call_target="tpu_custom_call" | custom-call | tf_op jit(solution)/shard_map/pallas_call | solution.py:139
  696.9 12.9 %all-to-all-start.16 = ((f32[16,1,768]{2,1,0:T(1,128)}), f32[16,1,768]{2,1,0:T(1,128)S(1)}, u32[]{:S(2)}, u32[]{:S(2)}) async-start(f32[16,1,768]{2,1,0:T(1,128)} %broadcast_in_dim.78), calls=%async_computation.16 | async-start | bytes 98304 | tf_op jit(solution)/shard_map/all_to_all | solution.py:32
  711.2 11.1 shard_map.303
  787.3 10.8 shard_map.278
  850.8 11.8 %collective-permute-done.38 = f32[216,256]{1,0:T(8,128)} collective-permute-done((f32[216,256]{1,0:T(8,128)}, f32[216,256]{1,0:T(8,128)}, u32[]{:S(2)}, u32[]{:S(2)}) %collective-permute-start.38) | collective-permute-done | bytes 221216 | tf_op jit(solution)/shard_map/ppermute | solution.py:892
  886.4 10.6 collective-permute-done.44
  913.5 10.7 shard_map.301
  981.7 17.6 %collective-permute-done.53 = f32[216,256]{1,0:T(8,128)S(1)} collective-permute-done((f32[216,256]{1,0:T(8,128)S(1)}, f32[216,256]{1,0:T(8,128)S(1)}, u32[]{:S(2)}, u32[]{:S(2)}) %collective-permute-start.53) | collective-permute-done | bytes 221216 | tf_op jit(solution)/shard_map/ppermute | solution.py:892
  1023.5 27.7 %collective-permute-done.58 = f32[432,256]{1,0:T(8,128)S(1)} collective-permute-done((f32[432,256]{1,0:T(8,128)S(1)}, f32[432,256]{1,0:T(8,128)S(1)}, u32[]{:S(2)}, u32[]{:S(2)}) %collective-permute-start.58) | collective-permute-done | bytes 442400 | tf_op jit(solution)/shard_map/ppermute | solution.py:892
  1061.1 10.6 all-to-all-done.20
  (750 shorter events, 818.7 us)
Async XLA Ops:
  7.2 77.4 %all-gather.6.cloned.1.call-start = ((), (), s32[]{:S(2)}) async-start(), calls=%async_computation.22 | async-start | bytes 1966080 | tf_op jit(solution)/shard_map/all_gather | solution.py:1436
  7.9 114.9 %all-gather.8.cloned.1.call-start = ((), (), s32[]{:S(2)}) async-start(), calls=%async_computation.23 | async-start | bytes 11796480 | tf_op jit(solution)/shard_map/all_gather | solution.py:1436
  8.7 140.1 %all-gather.10.cloned.1.call-start = ((), (), s32[]{:S(2)}) async-start(), calls=%async_computation.24 | async-start | bytes 15728640 | tf_op jit(solution)/shard_map/all_gather | solution.py:1436
  9.5 171.5 %all-gather.12.cloned.1.call-start = ((), (), s32[]{:S(2)}) async-start(), calls=%async_computation.25 | async-start | bytes 7077888 | tf_op jit(solution)/shard_map/all_gather | solution.py:1436
  10.0 198.6 %all-gather.14.cloned.1.call-start = ((), (), s32[]{:S(2)}) async-start(), calls=%async_computation.26 | async-start | bytes 3145728 | tf_op jit(solution)/shard_map/all_gather | solution.py:1436
  426.5 45.8 %collective-permute-start.18 = (f32[768,256]{1,0:T(8,128)S(1)}, f32[768,256]{1,0:T(8,128)S(1)}, u32[]{:S(2)}, u32[]{:S(2)}) collective-permute-start(f32[768,256]{1,0:T(8,128)S(1)} %constant_dynamic-slice_fusion.28), channel_id=1, source_target_pairs={{0,2},{1,3},{2,0},{3,1},{4,6},{5,7},{6,4},{7,5},{8,10},{9,11},{10,... | collective-permute-start | bytes 2359304 | tf_op jit(solution)/shard_map/ppermute | solution.py:892
  495.0 59.6 %collective-permute-start.22 = (f32[192,256]{1,0:T(8,128)S(1)}, f32[192,256]{1,0:T(8,128)}, u32[]{:S(2)}, u32[]{:S(2)}) collective-permute-start(f32[192,256]{1,0:T(8,128)S(1)} %dynamic-slice_add_fusion.15), channel_id=1, source_target_pairs={{0,8},{1,9},{2,10},{3,11},{4,12},{5,13},{6,14},{7,15},{8,0},{9,1},... | collective-permute-start | bytes 589832 | tf_op jit(solution)/shard_map/ppermute | solution.py:892
  569.1 54.5 %collective-permute-start.27 = (f32[3072,256]{1,0:T(8,128)}, f32[3072,256]{1,0:T(8,128)}, u32[]{:S(2)}, u32[]{:S(2)}) collective-permute-start(f32[3072,256]{1,0:T(8,128)} %pad_maximum_fusion.3), channel_id=1, source_target_pairs={{0,16},{16,0},{1,17},{17,1},{2,18},{18,2},{3,19},{19,3},{4,20},{20... | collective-permute-start | bytes 9437192 | tf_op jit(solution)/shard_map/ppermute | solution.py:46
  636.8 88.0 %collective-permute-start.34 = (f32[1536,256]{1,0:T(8,128)}, f32[1536,256]{1,0:T(8,128)}, u32[]{:S(2)}, u32[]{:S(2)}) collective-permute-start(f32[1536,256]{1,0:T(8,128)} %constant_dynamic-slice_fusion.14), channel_id=1, source_target_pairs={{0,4},{1,5},{2,6},{3,7},{4,0},{5,1},{6,2},{7,3},{8,12},{9,13},{10,... | collective-permute-start | bytes 4718600 | tf_op jit(solution)/shard_map/ppermute | solution.py:892
  657.1 65.8 %collective-permute-start.33 = (f32[432,256]{1,0:T(8,128)}, f32[432,256]{1,0:T(8,128)}, u32[]{:S(2)}, u32[]{:S(2)}) collective-permute-start(f32[432,256]{1,0:T(8,128)} %constant_dynamic-slice_fusion.15), channel_id=1, source_target_pairs={{0,8},{1,9},{2,10},{3,11},{4,12},{5,13},{6,14},{7,15},{8,0},{9,1},... | collective-permute-start | bytes 1327112 | tf_op jit(solution)/shard_map/ppermute | solution.py:892
  662.7 124.6 %collective-permute-start.8 = (f32[784,1024]{1,0:T(8,128)S(1)}, f32[784,1024]{1,0:T(8,128)}, u32[]{:S(2)}, u32[]{:S(2)}) collective-permute-start(f32[784,1024]{1,0:T(8,128)S(1)} %copy-done.2), channel_id=1, source_target_pairs={{16,0},{17,1},{18,2},{19,3},{20,4},{21,5},{22,6},{23,7},{24,8},{25... | collective-permute-start | bytes 9633800 | tf_op jit(solution)/shard_map/ppermute | solution.py:755
  674.4 112.9 %collective-permute-start.11 = (f32[784,1024]{1,0:T(8,128)}, f32[784,1024]{1,0:T(8,128)}, u32[]{:S(2)}, u32[]{:S(2)}) collective-permute-start(f32[784,1024]{1,0:T(8,128)} %shard_map.277.d_ref), channel_id=1, source_target_pairs={{0,16},{1,17},{2,18},{3,19},{4,20},{5,21},{6,22},{7,23},{8,24},{9,... | collective-permute-start | bytes 9633800 | tf_op jit(solution)/shard_map/ppermute | solution.py:756
  709.9 70.0 %collective-permute-start.12 = (f32[784,512]{1,0:T(8,128)}, f32[784,512]{1,0:T(8,128)}, u32[]{:S(2)}, u32[]{:S(2)}) collective-permute-start(f32[784,512]{1,0:T(8,128)} %get-tuple-element.227.x_ref.a_ref), channel_id=1, source_target_pairs={{16,0},{17,1},{18,2},{19,3},{20,4},{21,5},{22,6},{23,7},{24,8},{25... | collective-permute-start | bytes 4816904 | tf_op jit(solution)/shard_map/ppermute | solution.py:755
  779.8 52.6 %collective-permute-start.42 = (f32[3456,256]{1,0:T(8,128)}, f32[3456,256]{1,0:T(8,128)}, u32[]{:S(2)}, u32[]{:S(2)}) collective-permute-start(f32[3456,256]{1,0:T(8,128)} %pad_maximum_fusion.1), channel_id=1, source_target_pairs={{0,16},{16,0},{1,17},{17,1},{2,18},{18,2},{3,19},{19,3},{4,20},{20... | collective-permute-start | bytes 10616840 | tf_op jit(solution)/shard_map/ppermute | solution.py:46
  784.6 42.8 %collective-permute-start.70 = (f32[1536,256]{1,0:T(8,128)}, f32[1536,256]{1,0:T(8,128)}, u32[]{:S(2)}, u32[]{:S(2)}) collective-permute-start(f32[1536,256]{1,0:T(8,128)} %pad_maximum_fusion.10), channel_id=1, source_target_pairs={{0,1},{1,0},{2,3},{3,2},{4,5},{5,4},{6,7},{7,6},{8,9},{9,8},{10,11... | collective-permute-start | bytes 4718600 | tf_op jit(solution)/shard_map/ppermute | solution.py:892
  798.7 110.0 %collective-permute-start.31 = (f32[784,1024]{1,0:T(8,128)}, f32[784,1024]{1,0:T(8,128)}, u32[]{:S(2)}, u32[]{:S(2)}) collective-permute-start(f32[784,1024]{1,0:T(8,128)} %get-tuple-element.270.d_ref), channel_id=1, source_target_pairs={{0,16},{1,17},{2,18},{3,19},{4,20},{5,21},{6,22},{7,23},{8,24},{9,... | collective-permute-start | bytes 9633800 | tf_op jit(solution)/shard_map/ppermute | solution.py:756
  819.5 91.4 %collective-permute-start.30 = (f32[784,1024]{1,0:T(8,128)}, f32[784,1024]{1,0:T(8,128)}, u32[]{:S(2)}, u32[]{:S(2)}) collective-permute-start(f32[784,1024]{1,0:T(8,128)} %get-tuple-element.311.a_ref), channel_id=1, source_target_pairs={{16,0},{17,1},{18,2},{19,3},{20,4},{21,5},{22,6},{23,7},{24,8},{25... | collective-permute-start | bytes 9633800 | tf_op jit(solution)/shard_map/ppermute | solution.py:755
  821.7 44.2 %collective-permute-start.40 = (f32[768,256]{1,0:T(8,128)}, f32[768,256]{1,0:T(8,128)}, u32[]{:S(2)}, u32[]{:S(2)}) collective-permute-start(f32[768,256]{1,0:T(8,128)} %constant_dynamic-slice_fusion.12), channel_id=1, source_target_pairs={{0,8},{1,9},{2,10},{3,11},{4,12},{5,13},{6,14},{7,15},{8,0},{9,1},... | collective-permute-start | bytes 2359304 | tf_op jit(solution)/shard_map/ppermute | solution.py:892
  882.6 47.5 %collective-permute-start.48 = (f32[864,256]{1,0:T(8,128)}, f32[864,256]{1,0:T(8,128)}, u32[]{:S(2)}, u32[]{:S(2)}) collective-permute-start(f32[864,256]{1,0:T(8,128)} %constant_dynamic-slice_fusion.2), channel_id=1, source_target_pairs={{0,2},{1,3},{2,0},{3,1},{4,6},{5,7},{6,4},{7,5},{8,10},{9,11},{10,... | collective-permute-start | bytes 2654216 | tf_op jit(solution)/shard_map/ppermute | solution.py:892
  885.8 44.3 %collective-permute-start.47 = (f32[192,256]{1,0:T(8,128)S(1)}, f32[192,256]{1,0:T(8,128)S(1)}, u32[]{:S(2)}, u32[]{:S(2)}) collective-permute-start(f32[192,256]{1,0:T(8,128)S(1)} %dynamic-slice_add_fusion.14), channel_id=1, source_target_pairs={{0,2},{1,3},{2,0},{3,1},{4,6},{5,7},{6,4},{7,5},{8,10},{9,11},{10,... | collective-permute-start | bytes 589832 | tf_op jit(solution)/shard_map/ppermute | solution.py:892
  908.8 184.8 %collective-permute-start.71 = (f32[1,512,256]{2,1,0:T(8,128)}, f32[1,512,256]{2,1,0:T(8,128)}, u32[]{:S(2)}, u32[]{:S(2)}) collective-permute-start(f32[1,512,256]{2,1,0:T(8,128)} %slice_bitcast_fusion.1.d_ref), channel_id=1, source_target_pairs={{0,16},{1,17},{2,18},{3,19},{4,20},{5,21},{6,22},{7,23},{8,24},{9,... | collective-permute-start | bytes 1572872 | tf_op jit(solution)/shard_map/ppermute | solution.py:756
  910.9 185.7 %collective-permute-start.57 = (f32[784,512]{1,0:T(8,128)}, f32[784,512]{1,0:T(8,128)}, u32[]{:S(2)}, u32[]{:S(2)}) collective-permute-start(f32[784,512]{1,0:T(8,128)} %get-tuple-element.326.f_ref.d_ref), channel_id=1, source_target_pairs={{0,16},{1,17},{2,18},{3,19},{4,20},{5,21},{6,22},{7,23},{8,24},{9,... | collective-permute-start | bytes 4816904 | tf_op jit(solution)/shard_map/ppermute | solution.py:756
  961.9 118.0 %collective-permute-start.61 = (f32[1728,256]{1,0:T(8,128)S(1)}, f32[1728,256]{1,0:T(8,128)}, u32[]{:S(2)}, u32[]{:S(2)}) collective-permute-start(f32[1728,256]{1,0:T(8,128)S(1)} %pad_maximum_fusion.8), channel_id=1, source_target_pairs={{0,2},{1,3},{2,0},{3,1},{4,6},{5,7},{6,4},{7,5},{8,10},{9,11},{10,... | collective-permute-start | bytes 5308424 | tf_op jit(solution)/shard_map/ppermute | solution.py:892
  1011.1 77.6 %collective-permute-start.68 = (f32[1536,256]{1,0:T(8,128)}, f32[1536,256]{1,0:T(8,128)}, u32[]{:S(2)}, u32[]{:S(2)}) collective-permute-start(f32[1536,256]{1,0:T(8,128)} %pad_maximum_fusion.11), channel_id=1, source_target_pairs={{0,4},{1,5},{2,6},{3,7},{4,0},{5,1},{6,2},{7,3},{8,12},{9,13},{10,... | collective-permute-start | bytes 4718600 | tf_op jit(solution)/shard_map/ppermute | solution.py:892
  (180 other events, 2124.2 us)
Sparse Core Ops, SparseCore 0:
  9.6 12.1 all-gather.5
  23.3 20.2 all-gather.7
  45.1 24.0 all-gather.9
  70.6 15.6 all-gather.11
  87.7 11.7 all-gather.13

commit v3 on v2

--- a/solution.py
+++ b/solution.py
@@ -9,9 +9,11 @@
 from jax.sharding import PartitionSpec as P
 
 EPSILON = 1e-05
+PLANS = ((0, 0, 0, 0, 0, 0), (1, 2, 2, 2, 2, 0), (2, 3, 3, 0))
 FINE = lax.Precision.HIGH
 GROUP = 4
 AXES = ("clip", "tm")
+NORM_ORDER = (2, 0, 1, 3, 4, 5, 6, 7)
 
 
 def dot_nn(a, b):
@@ -27,9 +29,7 @@
 
 
 def sums_everywhere(vector):
-    count = lax.axis_size("clip") * lax.axis_size("tm")
-    copies = jnp.broadcast_to(vector, (count, vector.shape[1]))
-    return lax.all_to_all(copies, AXES, 0, 0)
+    return lax.all_to_all(vector, AXES, 0, 0)
 
 
 def from_previous(edge):
@@ -55,7 +55,7 @@
     return s * (1.0 + v * (1.0 - s))
 
 
-VMEM_BYTES = 56 * 2**20
+VMEM_BYTES = 36 * 2**20
 
 
 def rowwise(mask, width):
@@ -82,13 +82,27 @@
     return row if times == 1 else jnp.concatenate([row] * times, axis=1)
 
 
+def put_sums(st_ref, start, row):
+    st_ref[:, start : start + row.shape[1]] = jnp.broadcast_to(row, (st_ref.shape[0], row.shape[1]))
+
+
+def put_part(st_ref, offset, row):
+    width = row.shape[1]
+    start = pl.multiple_of(offset + pl.program_id(0) * width, 128)
+    st_ref[:, pl.ds(start, width)] = jnp.broadcast_to(row, (st_ref.shape[0], width))
+
+
+def folded(row, fold):
+    width = row.shape[1] // fold
+    return sum(row[:, k * width : (k + 1) * width] for k in range(fold))
+
+
 def store_sums(st_ref, values, mask, fold=1):
     weighted = values * mask
-    total = jnp.sum(weighted, axis=0, keepdims=True)
-    square = jnp.sum(weighted * values, axis=0, keepdims=True)
-    width = total.shape[1] // fold
-    st_ref[:, :width] = sum(total[:, k * width : (k + 1) * width] for k in range(fold))
-    st_ref[:, width:] = sum(square[:, k * width : (k + 1) * width] for k in range(fold))
+    total = folded(jnp.sum(weighted, axis=0, keepdims=True), fold)
+    put_sums(st_ref, 0, total)
+    square = folded(jnp.sum(weighted * values, axis=0, keepdims=True), fold)
+    put_sums(st_ref, total.shape[1], square)
 
 
 class Stacked:
@@ -106,8 +120,28 @@
         return self.block(self.shape, lambda *step: zeros)
 
 
+class Window:
+    def __init__(self, both, place, offset, shape):
+        self.both, self.place, self.offset, self.shape = both, place, offset, shape
+
+    def whole(self):
+        lead = (None,) * len(self.place)
+        if self.shape[0] == 1:
+            where = self.place + (0, self.offset // self.shape[1])
+        else:
+            where = self.place + (self.offset // self.shape[0], 0)
+        return pl.BlockSpec(lead + self.shape, lambda *step: where)
+
+    def parts(self, width):
+        lead = (None,) * len(self.place)
+        first = self.offset // width
+        return pl.BlockSpec(lead + (1, width), lambda j: self.place + (0, first + j))
+
+
 def array_of(value):
-    return value.both if isinstance(value, Stacked) else value
+    if isinstance(value, Stacked):
+        return pltpu.with_memory_space_constraint(value.both, pltpu.HBM)
+    return value.both if isinstance(value, Window) else value
 
 
 def call(kernel, outs, ins, scratch=(), **static):
@@ -116,7 +150,7 @@
         partial(kernel, **static),
         grid=(1,),
         out_shape=[jax.ShapeDtypeStruct(s, jnp.float32) for s in outs],
-        in_specs=[x.whole() if isinstance(x, Stacked) else vmem for x in ins],
+        in_specs=[x.whole() if isinstance(x, (Stacked, Window)) else vmem for x in ins],
         out_specs=[vmem] * len(outs),
         scratch_shapes=[pltpu.VMEM(s, jnp.float32) for s in scratch],
         compiler_params=pltpu.CompilerParams(vmem_limit_bytes=VMEM_BYTES),
@@ -133,6 +167,14 @@
 
 def bands(height, width):
     return pl.BlockSpec((height, width), lambda j: (j, 0))
+
+
+def streamed(value, spec):
+    value = array_of(value)
+    pieces = [n for n in spec.block_shape if n is not None]
+    if math.prod(pieces) < value.size and value.size * 4 > 2**20:
+        return pltpu.with_memory_space_constraint(value, pltpu.HBM)
+    return value
 
 
 def call_steps(kernel, steps, outs, out_specs, ins, in_specs, scratch=(), **static):
@@ -146,7 +188,7 @@
         compiler_params=pltpu.CompilerParams(
             dimension_semantics=("arbitrary",), vmem_limit_bytes=VMEM_BYTES
         ),
-    )(*[array_of(x) for x in ins])
+    )(*[streamed(x, spec) for x, spec in zip(ins, in_specs)])
 
 
 def take_rows(out_ref, values, first, frames, scratch):
@@ -173,15 +215,40 @@
 
 
 def banded(w_ref, matrix):
-    taps, inner, wide = w_ref.shape
+    taps, wide = 3, w_ref.shape[1]
+    inner = w_ref.shape[0] // taps
     matrix[...] = jnp.zeros(matrix.shape, jnp.float32)
     for q in range(GROUP):
         for k in range(taps):
             r = q + k - 1
             start = q * inner + (0 if 0 <= r < GROUP else GROUP * inner)
             r = r % GROUP
-            matrix[start : start + inner, r * wide : (r + 1) * wide] = w_ref[k]
+            matrix[start : start + inner, r * wide : (r + 1) * wide] = w_ref[k * inner : (k + 1) * inner]
     return matrix[...]
+
+
+def diagonal(tile, inner):
+    frame = lax.broadcasted_iota(jnp.int32, (1, tile.shape[1]), 1) // inner
+    return jnp.concatenate([jnp.where(frame == r, tile, 0.0) for r in range(GROUP)], axis=0)
+
+
+def undiagonal(square, inner):
+    count = square.shape[0] // GROUP
+    frame = lax.broadcasted_iota(jnp.int32, (1, square.shape[1]), 1) // inner
+    total = sum(
+        jnp.where(frame == r, square[r * count : (r + 1) * count], 0.0) for r in range(GROUP)
+    )
+    total = around(total, inner)
+    count = count // GROUP
+    return sum(
+        jnp.where(frame == r, total[r * count : (r + 1) * count], 0.0) for r in range(GROUP)
+    )
+
+
+def tap(k_ref, k, inner):
+    if not inner:
+        return k_ref[k]
+    return diagonal(k_ref[k * inner : (k + 1) * inner], inner)
 
 
 def fast_first_kernel(
@@ -209,6 +276,7 @@
     )
     o_ref[...] = out
     store_sums(st_ref, out, m_ref[...])
+    put_sums(st_ref, 2 * width, jnp.sum(m_ref[...], axis=0, keepdims=True))
 
 
 def fill_shifts(values, x0, xl, xr, side, frames):
@@ -241,9 +309,9 @@
     act = mask * silu(g_ref[...] * ((v_ref[...] - mean) * rstd) + b_ref[...])
     act_ref[...] = act
     fill_shifts(act, x0, xl, xr, side, frames)
-    total = dot_nt(shifted(0, x0, xl, xr, rows, side, frames), k_ref[0])
-    for k in range(1, k_ref.shape[0]):
-        total += dot_nt(shifted(k, x0, xl, xr, rows, side, frames), k_ref[k])
+    total = dot_nt(shifted(0, x0, xl, xr, rows, side, frames), tap(k_ref, 0, fold))
+    for k in range(1, 9):
+        total += dot_nt(shifted(k, x0, xl, xr, rows, side, frames), tap(k_ref, k, fold))
     o_ref[...] = total
     store_sums(st_ref, total, rowwise(m_ref[...], total.shape[1]))
 
@@ -255,7 +323,7 @@
     mean, rstd = moments(r_ref, offset, width, c_ref[...], fold)
     act = rowwise(m_ref[...], width) * silu(g_ref[...] * ((v_ref[...] - mean) * rstd) + b_ref[...])
     act_ref[...] = act
-    out = dot_nn(act, w_ref[...])
+    out = dot_nt(act, diagonal(w_ref[...], fold))
     o_ref[...] = out
     store_sums(st_ref, out, rowwise(m_ref[...], out.shape[1]), GROUP)
 
@@ -321,14 +389,14 @@
         take_rows(low_ref, y, 0, frames, scratch)
 
 
-def shortcut_kernel(x_ref, a_ref, m_ref, w_ref, y_ref, s_ref, q_ref):
+def shortcut_kernel(x_ref, a_ref, m_ref, w_ref, y_ref, st_ref):
     wide = x_ref.shape[1]
     out = dot_nt(x_ref[...], w_ref[:, :wide])
     out += dot_nt(a_ref[...], w_ref[:, wide:])
     y_ref[...] = out
     weighted = out * rowwise(m_ref[...], out.shape[1])
-    s_ref[...] = jnp.sum(weighted, axis=0, keepdims=True)
-    q_ref[...] = jnp.sum(weighted * out, axis=0, keepdims=True)
+    put_part(st_ref, 0, jnp.sum(weighted, axis=0, keepdims=True))
+    put_part(st_ref, st_ref.shape[1] // 2, jnp.sum(weighted * out, axis=0, keepdims=True))
 
 
 def inner_join_kernel(y_ref, p_ref, n_ref, m_ref, o_ref, st_ref, sp_ref, sn_ref, *, frames):
@@ -341,7 +409,7 @@
 
 
 def expand_kernel(
-    v_ref, r_ref, c_ref, g_ref, b_ref, m_ref, w_ref, o_ref, act_ref, s_ref, q_ref, *, offset
+    v_ref, r_ref, c_ref, g_ref, b_ref, m_ref, w_ref, o_ref, act_ref, st_ref, *, offset
 ):
     width = v_ref.shape[1]
 
@@ -354,8 +422,8 @@
     out = dot_nt(act_ref[...], w_ref[...])
     o_ref[...] = out
     weighted = out * rowwise(m_ref[...], out.shape[1])
-    s_ref[...] = jnp.sum(weighted, axis=0, keepdims=True)
-    q_ref[...] = jnp.sum(weighted * out, axis=0, keepdims=True)
+    put_part(st_ref, 0, jnp.sum(weighted, axis=0, keepdims=True))
+    put_part(st_ref, st_ref.shape[1] // 2, jnp.sum(weighted * out, axis=0, keepdims=True))
 
 
 def slow_out_kernel(
@@ -393,16 +461,16 @@
 
 def slow_slope_kernel(
     d_ref, e_ref, k_ref, r6_ref, r7_ref, c_ref, g6_ref, b6_ref, g7_ref, b7_ref, m_ref,
-    p_ref, s_ref, q6_ref, q7_ref, *, offset6, offset7, total
+    p_ref, st_ref, *, offset6, offset7, total
 ):
     pre, (n6, _), (n7, _) = slow_pre(
         e_ref, k_ref, r6_ref, r7_ref, c_ref, g6_ref, b6_ref, g7_ref, b7_ref, offset6, offset7, total
     )
     grad = rowwise(m_ref[...], pre.shape[1]) * d_ref[...] * silu_slope(pre)
     p_ref[...] = grad
-    s_ref[...] = jnp.sum(grad, axis=0, keepdims=True)
-    q6_ref[...] = jnp.sum(grad * n6, axis=0, keepdims=True)
-    q7_ref[...] = jnp.sum(grad * n7, axis=0, keepdims=True)
+    put_part(st_ref, 0, jnp.sum(grad, axis=0, keepdims=True))
+    put_part(st_ref, total, jnp.sum(grad * n6, axis=0, keepdims=True))
+    put_part(st_ref, 2 * total, jnp.sum(grad * n7, axis=0, keepdims=True))
 
 
 def expand_back_kernel(
@@ -439,8 +507,7 @@
         out = rowwise(m_ref[...], depth) * acc[...]
         out = out * silu_slope(g5_ref[...] * normed + b5_ref[...])
         o_ref[...] = out
-        st_ref[:, :depth] = jnp.sum(out, axis=0, keepdims=True)
-        st_ref[:, depth:] = jnp.sum(out * normed, axis=0, keepdims=True)
+        store_back_sums(st_ref, out, normed)
 
 
 def store_weight(dw_ref, grad, x_ref, a_ref):
@@ -448,20 +515,6 @@
     for k in range(count - 1):
         dw_ref[k] = dot_tn(grad, x_ref[:, k * width : (k + 1) * width])
     dw_ref[count - 1] = dot_tn(grad, a_ref[...])
-
-
-def shortcut_back_kernel(d_ref, w_ref, x_ref, a_ref, dw_ref, o_ref):
-    step = pl.program_id(0)
-    grad = d_ref[...]
-    store_weight(dw_ref, grad, x_ref, a_ref)
-
-    @pl.when(step == 0)
-    def _():
-        o_ref[...] = dot_nn(grad, w_ref[...])
-
-    @pl.when(step > 0)
-    def _():
-        o_ref[...] += dot_nn(grad, w_ref[...])
 
 
 def back_sums(rb_ref, offset, width, count, fold=0):
@@ -477,11 +530,9 @@
 
 
 def store_back_sums(st_ref, grad, normed, fold=1):
-    low = jnp.sum(grad, axis=0, keepdims=True)
-    slope = jnp.sum(grad * normed, axis=0, keepdims=True)
-    width = low.shape[1] // fold
-    st_ref[:, :width] = sum(low[:, k * width : (k + 1) * width] for k in range(fold))
-    st_ref[:, width:] = sum(slope[:, k * width : (k + 1) * width] for k in range(fold))
+    low = folded(jnp.sum(grad, axis=0, keepdims=True), fold)
+    put_sums(st_ref, 0, low)
+    put_sums(st_ref, low.shape[1], folded(jnp.sum(grad * normed, axis=0, keepdims=True), fold))
 
 
 def conv_back_kernel(
@@ -495,10 +546,9 @@
     grad = norm_back(p_ref[...], v_ref[...], mean, rstd, g_ref[...], low, slope, mask)
     d_ref[...] = grad
     fill_shifts(grad, x0, xl, xr, side, frames)
-    last = k_ref.shape[0] - 1
-    total = dot_nn(shifted(0, x0, xl, xr, rows, side, frames), k_ref[last])
-    for k in range(1, last + 1):
-        total += dot_nn(shifted(k, x0, xl, xr, rows, side, frames), k_ref[last - k])
+    total = dot_nn(shifted(0, x0, xl, xr, rows, side, frames), tap(k_ref, 8, fold))
+    for k in range(1, 9):
+        total += dot_nn(shifted(k, x0, xl, xr, rows, side, frames), tap(k_ref, 8 - k, fold))
     mean, rstd = moments(ru_ref, offsetu, u_ref.shape[1], count, fold)
     normed = (u_ref[...] - mean) * rstd
     out = rowwise(m_ref[...], u_ref.shape[1]) * total
@@ -507,12 +557,17 @@
     store_back_sums(st_ref, out, normed)
 
 
-def conv_weight_kernel(x_ref, d_ref, dw_ref, x0, xl, xr, *, side, frames):
+def conv_weight_kernel(x_ref, d_ref, dw_ref, x0, xl, xr, *, fold, side, frames):
     rows = x_ref.shape[0]
     fill_shifts(x_ref[...], x0, xl, xr, side, frames)
     grad = d_ref[...]
-    for k in range(dw_ref.shape[0]):
-        dw_ref[k] = dot_tn(grad, shifted(k, x0, xl, xr, rows, side, frames))
+    for k in range(9):
+        out = dot_tn(grad, shifted(k, x0, xl, xr, rows, side, frames))
+        if fold:
+            out = undiagonal(out, fold)
+            dw_ref[k * out.shape[0] : (k + 1) * out.shape[0]] = out
+        else:
+            dw_ref[k] = out
 
 
 def norm_back_kernel(
@@ -531,7 +586,7 @@
 
 
 def joined_back_kernel(
-    d_ref, p_ref, n_ref, j_ref, w_ref, m_ref, v_ref, r_ref, c_ref, g_ref, b_ref,
+    d_ref, p_ref, n_ref, k_ref, w_ref, wk_ref, m_ref, v_ref, r_ref, c_ref, g_ref, b_ref,
     x_ref, o_ref, all_ref, st_ref, scratch, *, offset, frames
 ):
     step, steps = pl.program_id(0), pl.num_programs(0)
@@ -545,7 +600,7 @@
         all_ref[:, 2 * depth :] = before_rows(scratch, grad, p_ref[...], frames)
 
     mask = rowwise(m_ref[...], o_ref.shape[1])
-    out = mask * (dot_nn(all_ref[...], w_ref[...]) + j_ref[...])
+    out = mask * (dot_nn(all_ref[...], w_ref[...]) + dot_nn(k_ref[...], wk_ref[...]))
 
     @pl.when(step < steps - 1)
     def _():
@@ -560,7 +615,7 @@
         store_back_sums(st_ref, grad, normed)
 
 
-def reduce_weight_kernel(d_ref, x_ref, a_ref, dw_ref):
+def joined_weight_kernel(d_ref, x_ref, a_ref, dw_ref):
     store_weight(dw_ref, d_ref[...], x_ref, a_ref)
 
 
@@ -592,10 +647,12 @@
 
 
 def lateral_weight_kernel(d_ref, on_ref, x_ref, dw_ref):
-    wide = dw_ref.shape[2]
+    wide = dw_ref.shape[2] // 2
     here, onward = d_ref[...], on_ref[...]
     for k, (grad, r) in enumerate(((onward, 2), (onward, 3), (here, 0), (here, 1), (here, 2))):
-        dw_ref[k] = dot_tn(grad, x_ref[:, r * wide : (r + 1) * wide])
+        side = (k % 2) * wide
+        dw_ref[k // 2, :, side : side + wide] = dot_tn(grad, x_ref[:, r * wide : (r + 1) * wide])
+    dw_ref[2, :, wide:] = jnp.zeros((dw_ref.shape[1], wide), jnp.float32)
 
 
 def fast_expand_back_kernel(
@@ -613,14 +670,14 @@
     d_ref[...] = grad
     mean, rstd = moments(ru_ref, offsetu, inner, count, fold)
     normed = (u_ref[...] - mean) * rstd
-    out = rowwise(m_ref[...], inner) * dot_nt(grad, w_ref[...])
+    out = rowwise(m_ref[...], inner) * dot_nn(grad, diagonal(w_ref[...], fold))
     out = out * silu_slope(gu_ref[...] * normed + bu_ref[...])
     o_ref[...] = out
     store_back_sums(st_ref, out, normed)
 
 
-def transposed_product_kernel(d_ref, x_ref, dw_ref):
-    dw_ref[...] = dot_tn(d_ref[...], x_ref[...])
+def fast_expand_weight_kernel(d_ref, x_ref, dw_ref, *, fold):
+    dw_ref[...] = undiagonal(dot_tn(d_ref[...], x_ref[...]), fold)
 
 
 def fast_first_back_kernel(
@@ -636,7 +693,17 @@
     both = jnp.concatenate([grad, edge], axis=1)
     mask = rowwise(m_ref[...], o_ref.shape[1])
     o_ref[...] = mask * (dot_nn(both, banded(w_ref, matrix)) + res_ref[...])
-    dw_ref[...] = dot_tn(both, x_ref[...])
+    full = dot_tn(both, x_ref[...])
+    wide = full.shape[1] // GROUP
+    for k in range(3):
+        total = None
+        for q in range(GROUP):
+            r = q + k - 1
+            start = q * inner + (0 if 0 <= r < GROUP else GROUP * inner)
+            r = r % GROUP
+            piece = full[start : start + inner, r * wide : (r + 1) * wide]
+            total = piece if total is None else total + piece
+        dw_ref[k * inner : (k + 1) * inner] = total
 
 
 def load_rows_kernel(own_ref, x_ref, m_ref, o_ref):
@@ -682,29 +749,63 @@
     )(own, *ins)
 
 
-def place_weight_kernel(own_ref, a_ref, b_ref, c_ref, d_ref, o_ref):
+def place_early_kernel(own_ref, a_ref, b_ref, c_ref, d_ref, shortcut_ref, expand_ref):
     count, rows, width = a_ref.shape
     for own, refs in enumerate(((a_ref, b_ref), (c_ref, d_ref))):
 
         @pl.when(own_ref[0] == own)
         def _():
             for half, ref in enumerate(refs):
-                for k in range(count):
-                    o_ref[half * rows : (half + 1) * rows, k * width : (k + 1) * width] = ref[k]
-
-
-def place_weight(low, high, own):
-    to_zero, to_one = cross(low, high)
-    count, rows, width = low.shape
-    return chosen(
-        place_weight_kernel,
-        own,
-        (1,),
-        [low, to_zero, to_one, high],
-        [pl.BlockSpec(low.shape, lambda j, o: (0, 0, 0))] * 4,
-        (2 * rows, count * width),
-        pl.BlockSpec((2 * rows, count * width), lambda j, o: (0, 0)),
-    )
+                start = half * rows
+                for k in range(count - 1):
+                    shortcut_ref[start : start + rows, k * width : (k + 1) * width] = ref[k]
+                expand_ref[start : start + rows] = ref[count - 1]
+
+
+def place_late_kernel(own_ref, a_ref, b_ref, c_ref, d_ref, spatial_ref, reduce_ref, lateral_ref):
+    _, rows, width = a_ref.shape
+    taps, blocks = spatial_ref.shape[0], reduce_ref.shape[1] // width
+    runs = reduce_ref.shape[0] // (2 * rows)
+    wide = lateral_ref.shape[2]
+    for own, refs in enumerate(((a_ref, b_ref), (c_ref, d_ref))):
+
+        @pl.when(own_ref[0] == own)
+        def _():
+            for half, ref in enumerate(refs):
+                start = half * rows
+                for k in range(taps):
+                    spatial_ref[k, start : start + rows] = ref[k]
+                for k in range(blocks):
+                    for j in range(runs):
+                        first = (half * runs + j) * rows
+                        reduce_ref[first : first + rows, k * width : (k + 1) * width] = ref[
+                            taps + k * runs + j
+                        ]
+                for k in range(lateral_ref.shape[0]):
+                    side = (k % 2) * wide
+                    lateral_ref[k, start : start + rows] = ref[
+                        taps + blocks * runs + k // 2, :, side : side + wide
+                    ]
+
+
+def place_weights(kernel, low, high, rows, own, outs):
+    views = [x.reshape(-1, rows, x.shape[1]) for x in (low, *cross(low, high), high)]
+
+    def whole(shape):
+        zeros = (0,) * len(shape)
+        return pl.BlockSpec(shape, lambda j, o: zeros, pipeline_mode=pl.Buffered(1))
+
+    return pl.pallas_call(
+        kernel,
+        out_shape=[jax.ShapeDtypeStruct(shape, jnp.float32) for shape in outs],
+        grid_spec=pltpu.PrefetchScalarGridSpec(
+            num_scalar_prefetch=1,
+            grid=(1,),
+            in_specs=[whole(x.shape) for x in views],
+            out_specs=[pl.BlockSpec(memory_space=pltpu.VMEM)] * len(outs),
+        ),
+        compiler_params=pltpu.CompilerParams(vmem_limit_bytes=VMEM_BYTES),
+    )(own, *views)
 
 
 def pieces_of(places):
@@ -831,16 +932,6 @@
     return kept + swap(sent)
 
 
-def half_pieces(total, arrays):
-    pieces, cursor = [], 0
-    for x in arrays:
-        shape = (x.shape[0], x.shape[1] // 2, x.shape[2])
-        rows = shape[0] * shape[1]
-        pieces.append(total[cursor : cursor + rows].reshape(shape))
-        cursor += rows
-    return pieces
-
-
 def reduction(arrays, route):
     arrays = yield arrays
     total = core_half(arrays)
@@ -854,7 +945,7 @@
         taken = trade(total, pair)
         low, high = jnp.where(bit == 0, total, taken), jnp.where(bit == 0, taken, total)
         total = jnp.concatenate([low, high], axis=0)
-    return half_pieces(total, arrays)
+    return total
 
 
 def summed(arrays):
@@ -862,6 +953,17 @@
     total = core_half(arrays)
     (total,) = yield (total,)
     return half_pieces(lax.psum(total, AXES), arrays)
+
+
+def summed(groups):
+    totals = lax.psum(tuple(core_half(arrays) for arrays in groups), AXES)
+    totals = yield totals
+    return totals
+
+
+def worked(values):
+    values = yield values
+    return values
 
 
 def held_grads(block, names):
@@ -919,37 +1021,49 @@
                 return
         self.held = held
 
+    def waits(self):
+        if self.paces[0] == 0 and len(self.paces) > 1:
+            self.paces.pop(0)
+            return True
+        return self.paces[0] == 0
+
     def finish(self):
+        self.paces = [1]
         while self.held is not None:
             self.resume(self.held)
         return self.result
 
 
 class Section:
-    def __init__(self, index, small, large):
-        self.fast_reduce, spatial, expand, gain, bias = [x[index] for x in small]
-        inner, wide = self.fast_reduce.shape[1], self.fast_reduce.shape[2]
+    def __init__(self, index, small, norms, sizes, large):
         self.lateral, self.slow_reduce, self.slow_spatial, self.slow_expand, self.shortcut = [
             Stacked(x, index) for x in large
         ]
-        self.inner, self.wide, self.depth = inner, wide, self.slow_expand.shape[1]
-        eye = jnp.eye(GROUP, dtype=jnp.float32)
-        self.fast_spatial = jnp.einsum("rq,koi->kqori", eye, spatial, precision="highest").reshape(
-            spatial.shape[0], GROUP * inner, GROUP * inner
-        )
-        self.fast_expand = jnp.einsum("rq,oi->riqo", eye, expand, precision="highest").reshape(
-            GROUP * inner, GROUP * wide
-        )
-        widths = [
-            inner, inner, wide, self.lateral.shape[1], self.depth, self.depth,
+        self.inner, self.wide, self.depth = sizes["inner"], sizes["wide"], self.slow_expand.shape[1]
+        start = 0
+        for name in ("fast_spatial", "fast_reduce", "fast_expand"):
+            setattr(self, name, Window(small, (index,), start, (sizes[name], 128)))
+            start += sizes[name]
+        self.widths = [
+            self.inner, self.inner, self.wide, self.lateral.shape[1], self.depth, self.depth,
             self.slow_expand.shape[0], self.shortcut.shape[0],
         ]
-        repeats = [GROUP, GROUP, GROUP, 1, 1, 1, 1, 1]
-        self.widths, self.gains, self.biases, cursor = widths, [], [], 0
-        for width, times in zip(widths, repeats):
-            self.gains.append(jnp.tile(gain[None, cursor : cursor + width], (1, times)))
-            self.biases.append(jnp.tile(bias[None, cursor : cursor + width], (1, times)))
+        self.gains, self.biases = [None] * 8, [None] * 8
+        cursor = 0
+        for j in NORM_ORDER:
+            width = self.widths[j] * (GROUP if j < 3 else 1)
+            self.gains[j] = Window(norms, (index, 0), cursor, (1, width))
+            self.biases[j] = Window(norms, (index, 1), cursor, (1, width))
             cursor += width
+
+
+def norm_row(vector, widths):
+    starts = [sum(widths[:j]) for j in range(8)]
+    pieces = []
+    for j in NORM_ORDER:
+        piece = vector[starts[j] : starts[j] + widths[j]]
+        pieces += [piece] * (GROUP if j < 3 else 1)
+    return jnp.concatenate(pieces)
 
 
 class Block:
@@ -960,6 +1074,7 @@
         self.side = math.isqrt(self.places)
         self.pad = -(-(self.side + 1) * frames // 8) * 8
         self.grads, self.sums, self.back = {}, {}, {}
+        self.copies = lax.axis_size("clip") * lax.axis_size("tm")
 
     def window(self, width):
         return [(self.rows + 2 * self.pad, width)] * 3
@@ -980,7 +1095,7 @@
                 in_specs=[
                     pl.BlockSpec((None,) + grid.shape[1:], lambda j, o: (o[0], 0, 0)),
                     pl.BlockSpec((rows, 128), lambda j, o: (0, 0)),
-                    pl.BlockSpec(self.s.fast_reduce.shape, lambda j, o: (0, 0, 0)),
+                    self.s.fast_reduce.whole(),
                 ],
                 out_specs=[pl.BlockSpec(s, lambda j, o: (0, 0)) for s in outs],
                 scratch_shapes=[
@@ -989,7 +1104,7 @@
                 ],
             ),
             compiler_params=pltpu.CompilerParams(vmem_limit_bytes=VMEM_BYTES),
-        )(own, grid, self.mask, self.s.fast_reduce)
+        )(own, grid, self.mask, array_of(self.s.fast_reduce))
 
     def fast_forward(self, fast_in, parts):
         s, mask, frames, rows, places = self.s, self.mask, self.frames, self.rows, self.places
@@ -999,7 +1114,7 @@
         both, low, high = parts
         self.first, sums = call(
             fast_join_kernel,
-            [(rows, width), (1, 2 * width)],
+            [(rows, width), (self.copies, 2 * width + 128)],
             [both, from_previous(high), from_next(low), mask],
             [self.lanes(width)] * 2,
             frames=frames,
@@ -1008,7 +1123,7 @@
         self.sums[0] = yield sums
         second, self.first_act, sums = call(
             conv_kernel,
-            [(rows, width), (rows, width), (1, 2 * width)],
+            [(rows, width), (rows, width), (self.copies, 2 * width)],
             [self.first, self.sums[0][0], c4["fast"], s.gains[0], s.biases[0], mask, s.fast_spatial],
             self.window(width),
             offset=self.sums[0][1], fold=s.inner, side=self.side, frames=frames,
@@ -1017,7 +1132,7 @@
         self.sums[1] = yield sums
         self.third, self.second_act, sums = call(
             fast_expand_kernel,
-            [(rows, full), (rows, width), (1, 2 * s.wide)],
+            [(rows, full), (rows, width), (self.copies, 2 * s.wide)],
             [second, self.sums[1][0], c4["fast"], s.gains[1], s.biases[1], mask, s.fast_expand],
             offset=self.sums[1][1], fold=s.inner,
         )
@@ -1041,7 +1156,7 @@
         )
         self.lateral, sums = call(
             lateral_join_kernel,
-            [(rows, lateral), (1, 2 * lateral)],
+            [(rows, lateral), (self.copies, 2 * lateral)],
             [here, onward, from_previous(edge), mask],
             [self.lanes(lateral)],
             frames=frames,
@@ -1063,18 +1178,18 @@
             [slow_in, self.lateral, r3, count, s.gains[3], s.biases[3], mask, s.slow_reduce],
             [
                 fixed((rows, wide)), fixed((rows, lateral)), fixed(r3.shape), fixed((1, 1)),
-                fixed((1, lateral)), fixed((1, lateral)), fixed((rows, 128)),
+                s.gains[3].whole(), s.biases[3].whole(), fixed((rows, 128)),
                 s.slow_reduce.block((depth, full), lambda j: (j, 0)),
             ],
             [(rows, full), self.lanes(depth)],
             offset=offset, frames=frames,
         )
         steps = out_wide // depth
-        self.skipped, skip_sum, skip_square = call_steps(
+        self.skipped, skip_sums = call_steps(
             shortcut_kernel,
             steps,
-            [(rows, out_wide), (1, out_wide), (1, out_wide)],
-            [columns(rows, depth), columns(1, depth), columns(1, depth)],
+            [(rows, out_wide), (self.copies, 2 * out_wide)],
+            [columns(rows, depth), fixed((self.copies, 2 * out_wide))],
             [slow_in, self.lateral_act, mask, s.shortcut],
             [
                 fixed((rows, wide)), fixed((rows, lateral)), fixed((rows, 128)),
@@ -1083,36 +1198,36 @@
         )
         self.inner, sums = call(
             inner_join_kernel,
-            [(rows, depth), (1, 2 * depth)],
+            [(rows, depth), (self.copies, 2 * depth)],
             [reduced, from_previous(high), from_next(low), mask],
             [self.lanes(depth)] * 2,
             frames=frames,
         )
-        r, offset = yield jnp.concatenate([sums, skip_sum, skip_square], axis=1)
+        r, offset = yield jnp.concatenate([sums, skip_sums], axis=1)
         self.sums[4], self.sums[7] = (r, offset), (r, offset + 2 * depth)
         self.middle, self.inner_act, sums = call(
             conv_kernel,
-            [(rows, depth), (rows, depth), (1, 2 * depth)],
+            [(rows, depth), (rows, depth), (self.copies, 2 * depth)],
             [self.inner, r, count, s.gains[4], s.biases[4], mask, s.slow_spatial],
             self.window(depth),
             offset=offset, fold=0, side=self.side, frames=frames,
         )
         self.sums[5] = yield sums
         r5, offset = self.sums[5]
-        self.expanded, self.middle_act, total, square = call_steps(
+        self.expanded, self.middle_act, sums = call_steps(
             expand_kernel,
             steps,
-            [(rows, out_wide), (rows, depth), (1, out_wide), (1, out_wide)],
-            [columns(rows, depth), fixed((rows, depth)), columns(1, depth), columns(1, depth)],
+            [(rows, out_wide), (rows, depth), (self.copies, 2 * out_wide)],
+            [columns(rows, depth), fixed((rows, depth)), fixed((self.copies, 2 * out_wide))],
             [self.middle, r5, count, s.gains[5], s.biases[5], mask, s.slow_expand],
             [
-                fixed((rows, depth)), fixed(r5.shape), fixed((1, 1)), fixed((1, depth)),
-                fixed((1, depth)), fixed((rows, 128)),
+                fixed((rows, depth)), fixed(r5.shape), fixed((1, 1)), s.gains[5].whole(),
+                s.biases[5].whole(), fixed((rows, 128)),
                 s.slow_expand.block((depth, depth), lambda j: (j, 0)),
             ],
             offset=offset,
         )
-        self.sums[6] = yield jnp.concatenate([total, square], axis=1)
+        self.sums[6] = yield sums
         self.slow_out = call_steps(
             slow_out_kernel,
             steps,
@@ -1125,14 +1240,15 @@
     def slow_pre_inputs(self):
         s, rows, depth = self.s, self.rows, self.s.depth
         r6, r7 = self.sums[6][0], self.sums[7][0]
-        wide, row = columns(rows, depth), columns(1, depth)
+        wide = columns(rows, depth)
+        gains = [x.parts(depth) for x in (s.gains[6], s.biases[6], s.gains[7], s.biases[7])]
         return (
             [
                 self.expanded, self.skipped, r6, r7, self.shared["slow"], s.gains[6], s.biases[6],
                 s.gains[7], s.biases[7], self.mask,
             ],
             [
-                wide, wide, fixed(r6.shape), fixed(r7.shape), fixed((1, 1)), row, row, row, row,
+                wide, wide, fixed(r6.shape), fixed(r7.shape), fixed((1, 1)), *gains,
                 fixed((rows, 128)),
             ],
         )
@@ -1144,53 +1260,50 @@
         full, steps = wide + lateral, out_wide // depth
         (r6, offset6), (r7, offset7) = self.sums[6], self.sums[7]
         ins, specs = self.slow_pre_inputs()
-        pre, low, slope6, slope7 = call_steps(
+        pre, sums = call_steps(
             slow_slope_kernel,
             steps,
-            [(rows, out_wide)] + [(1, out_wide)] * 3,
-            [columns(rows, depth)] + [columns(1, depth)] * 3,
+            [(rows, out_wide), (self.copies, 3 * out_wide)],
+            [columns(rows, depth), fixed((self.copies, 3 * out_wide))],
             [slow_grad] + ins,
             [columns(rows, depth)] + specs,
             offset6=offset6, offset7=offset7, total=out_wide,
         )
-        rb, offsetb = yield jnp.concatenate([low, slope6, slope7], axis=1)
+        rb, offsetb = yield sums
         self.back[6], self.back[7] = (rb, offsetb, offsetb + out_wide), (rb, offsetb, offsetb + 2 * out_wide)
         r5, offset5 = self.sums[5]
         skip_grad, self.grads["slow_expand"], pre, sums = call_steps(
             expand_back_kernel,
             steps,
-            [(rows, out_wide), (out_wide, depth), (rows, depth), (1, 2 * depth)],
-            [columns(rows, depth), bands(depth, depth), fixed((rows, depth)), fixed((1, 2 * depth))],
+            [(rows, out_wide), (out_wide, depth), (rows, depth), (self.copies, 2 * depth)],
+            [columns(rows, depth), bands(depth, depth), fixed((rows, depth)), fixed((self.copies, 2 * depth))],
             [
                 pre, self.expanded, self.skipped, r6, r7, rb, count, s.gains[6], s.gains[7], mask,
                 s.slow_expand, self.middle_act, self.middle, r5, s.gains[5], s.biases[5],
             ],
             [columns(rows, depth)] * 3
             + [fixed(r6.shape), fixed(r7.shape), fixed(rb.shape), fixed((1, 1))]
-            + [columns(1, depth)] * 2
+            + [s.gains[6].parts(depth), s.gains[7].parts(depth)]
             + [fixed((rows, 128)), s.slow_expand.block((depth, depth), lambda j: (j, 0))]
             + [fixed((rows, depth)), fixed((rows, depth))]
-            + [fixed(r5.shape), fixed((1, depth)), fixed((1, depth))],
+            + [fixed(r5.shape), s.gains[5].whole(), s.biases[5].whole()],
             [(rows, depth)],
             offset6=offset6, offset7=offset7, offsetb=offsetb, offset5=offset5, total=out_wide,
         )
-        self.grads["shortcut"], joined_grad = call_steps(
-            shortcut_back_kernel,
+        self.grads["shortcut"] = call_steps(
+            joined_weight_kernel,
             steps,
-            [(full // lateral, out_wide, lateral), (rows, full)],
-            [pl.BlockSpec((full // lateral, depth, lateral), lambda j: (0, j, 0)), fixed((rows, full))],
-            [skip_grad, s.shortcut, self.slow_in, self.lateral_act],
-            [
-                columns(rows, depth), s.shortcut.block((depth, full), lambda j: (j, 0)),
-                fixed((rows, wide)), fixed((rows, lateral)),
-            ],
-        )
+            [(full // lateral, out_wide, lateral)],
+            [pl.BlockSpec((full // lateral, depth, lateral), lambda j: (0, j, 0))],
+            [skip_grad, self.slow_in, self.lateral_act],
+            [columns(rows, depth), fixed((rows, wide)), fixed((rows, lateral))],
+        )[0]
         rb, offsetb = yield sums
         self.back[5] = (rb, offsetb, offsetb + depth)
         r4, offset4 = self.sums[4]
         middle_grad, pre, sums = call(
             conv_back_kernel,
-            [(rows, depth), (rows, depth), (1, 2 * depth)],
+            [(rows, depth), (rows, depth), (self.copies, 2 * depth)],
             [
                 pre, self.middle, r5, rb, count, s.gains[5], self.inner, r4, s.gains[4], s.biases[4],
                 mask, s.slow_spatial,
@@ -1203,7 +1316,7 @@
             [s.slow_spatial.shape],
             [self.inner_act, middle_grad],
             self.window(depth),
-            side=self.side, frames=frames,
+            fold=0, side=self.side, frames=frames,
         )[0]
         rb, offsetb = yield sums
         self.back[4] = (rb, offsetb, offsetb + depth)
@@ -1219,27 +1332,28 @@
         self.slow_in_grad, self.lateral_pre, reduced_grad, self.lateral_sums = call_steps(
             joined_back_kernel,
             last + 1,
-            [(rows, wide), (rows, lateral), (rows, 3 * depth), (1, 2 * lateral)],
+            [(rows, wide), (rows, lateral), (rows, 3 * depth), (self.copies, 2 * lateral)],
             [
                 pl.BlockSpec((rows, lateral), lambda j: (0, jnp.minimum(j, last - 1))),
-                fixed((rows, lateral)), fixed((rows, 3 * depth)), fixed((1, 2 * lateral)),
+                fixed((rows, lateral)), fixed((rows, 3 * depth)), fixed((self.copies, 2 * lateral)),
             ],
             [
-                inner_grad, from_previous(high), from_next(low), joined_grad, s.slow_reduce, mask,
+                inner_grad, from_previous(high), from_next(low), skip_grad, s.slow_reduce,
+                s.shortcut, mask,
                 self.lateral, r3, count, s.gains[3], s.biases[3],
             ],
             [
                 fixed((rows, depth)), fixed((places, depth)), fixed((places, depth)),
-                columns(rows, lateral), s.slow_reduce.block((3 * depth, lateral), lambda j: (0, j)),
-                fixed((rows, 128)),
-                fixed((rows, lateral)), fixed(r3.shape), fixed((1, 1)), fixed((1, lateral)),
-                fixed((1, lateral)),
+                fixed((rows, out_wide)), s.slow_reduce.block((3 * depth, lateral), lambda j: (0, j)),
+                s.shortcut.block((out_wide, lateral), lambda j: (0, j)), fixed((rows, 128)),
+                fixed((rows, lateral)), fixed(r3.shape), fixed((1, 1)), s.gains[3].whole(),
+                s.biases[3].whole(),
             ],
             [self.lanes(depth)],
             offset=offset3, frames=frames,
         )
         self.grads["slow_reduce"] = call_steps(
-            reduce_weight_kernel,
+            joined_weight_kernel,
             3,
             [(full // lateral, 3 * depth, lateral)],
             [pl.BlockSpec((full // lateral, depth, lateral), lambda j: (0, j, 0))],
@@ -1265,7 +1379,7 @@
         r2, offset2 = self.sums[2]
         residual, onward, sums = call(
             lateral_back_kernel,
-            [(rows, full), (rows, lateral), (1, 2 * wide)],
+            [(rows, full), (rows, lateral), (self.copies, 2 * wide)],
             [
                 here, from_next(low), fast_grad(), self.third, self.fast_in, r2, count4, s.gains[2],
                 s.biases[2], mask, s.lateral,
@@ -1274,29 +1388,32 @@
             offset=offset2, frames=frames,
         )
         self.grads["lateral"] = call(
-            lateral_weight_kernel, [(5, lateral, wide)], [here, onward, self.fast_out]
+            lateral_weight_kernel, [(3, lateral, 2 * wide)], [here, onward, self.fast_out]
         )[0]
         rb, offsetb = yield sums
         self.back[2] = (rb, offsetb, offsetb + wide)
         r1, offset1 = self.sums[1]
         third_grad, pre, sums = call(
             fast_expand_back_kernel,
-            [(rows, full), (rows, width), (1, 2 * width)],
+            [(rows, full), (rows, width), (self.copies, 2 * width)],
             [
                 residual, self.third, r2, rb, count4, s.gains[2], self.second, r1, s.gains[1],
                 s.biases[1], mask, s.fast_expand,
             ],
             offset=offset2, offsetb=offsetb, offsetu=offset1, fold=inner,
         )
-        grid = call(transposed_product_kernel, [(full, width)], [third_grad, self.second_act])[0]
-        grid = grid.reshape(GROUP, wide, GROUP, inner)
-        self.grads["fast_expand"] = sum(grid[r, :, r] for r in range(GROUP))
+        self.grads["fast_expand"] = call(
+            fast_expand_weight_kernel,
+            [(wide // GROUP, width)],
+            [third_grad, self.second_act],
+            fold=inner,
+        )[0]
         rb, offsetb = yield sums
         self.back[1] = (rb, offsetb, offsetb + width)
         r0, offset0 = self.sums[0]
         second_grad, pre, sums = call(
             conv_back_kernel,
-            [(rows, width), (rows, width), (1, 2 * width)],
+            [(rows, width), (rows, width), (self.copies, 2 * width)],
             [
                 pre, self.second, r1, rb, count4, s.gains[1], self.first, r0, s.gains[0], s.biases[0],
                 mask, s.fast_spatial,
@@ -1305,15 +1422,13 @@
             offset=offset1, offsetb=offsetb, offsetu=offset0, fold=inner, side=self.side,
             frames=frames,
         )
-        grid = call(
+        self.grads["fast_spatial"] = call(
             conv_weight_kernel,
-            [s.fast_spatial.shape],
+            [(9 * inner // GROUP, width)],
             [self.first_act, second_grad],
             self.window(width),
-            side=self.side, frames=frames,
+            fold=inner, side=self.side, frames=frames,
         )[0]
-        grid = grid.reshape(-1, GROUP, inner, GROUP, inner)
-        self.grads["fast_spatial"] = sum(grid[:, r, :, r] for r in range(GROUP))
         rb, offsetb = yield sums
         self.back[0] = (rb, offsetb, offsetb + width)
         first_grad, low, high = call(
@@ -1323,9 +1438,9 @@
             [self.lanes(width)],
             offset=offset0, offsetb=offsetb, fold=inner, frames=frames,
         )
-        self.fast_in_grad, grid = call(
+        self.fast_in_grad, self.grads["fast_reduce"] = call(
             fast_first_back_kernel,
-            [(rows, full), (2 * width, full)],
+            [(rows, full), (3 * inner, wide)],
             [
                 first_grad, from_previous(high), from_next(low), residual, s.fast_reduce, mask,
                 self.fast_in,
@@ -1333,28 +1448,13 @@
             [self.lanes(width)] * 2 + [(2 * width, full)],
             frames=frames, inner=inner,
         )
-        grid = grid.reshape(2, GROUP, inner, GROUP, wide)
-        near, far = grid[0], grid[1]
-        self.grads["fast_reduce"] = jnp.stack(
-            [
-                near[1, :, 0] + near[2, :, 1] + near[3, :, 2] + far[0, :, 3],
-                near[0, :, 0] + near[1, :, 1] + near[2, :, 2] + near[3, :, 3],
-                near[0, :, 1] + near[1, :, 2] + near[2, :, 3] + far[3, :, 0],
-            ]
-        )
 
     def blocked(self, name):
         grad = self.grads[name]
-        if name == "lateral":
-            taps, depth, wide = grad.shape
-            grad = jnp.pad(grad, ((0, taps % 2), (0, 0), (0, 0))).reshape(-1, 2, depth, wide)
-            return jnp.swapaxes(grad, 1, 2).reshape(-1, depth, 2 * wide)
         return grad if grad.ndim == 3 else grad[None]
 
     def fast_flat(self):
-        names = ("fast_reduce", "fast_spatial", "fast_expand")
-        flat = jnp.concatenate([self.grads[n].reshape(-1) for n in names])
-        return jnp.pad(flat, (0, -flat.shape[0] % 1024)).reshape(-1, 128)
+        return jnp.concatenate([self.grads[n] for n in ("fast_spatial", "fast_reduce", "fast_expand")])
 
     def norm_grads(self):
         gains, biases = [], []
@@ -1382,10 +1482,10 @@
             return None
 
 
-def advance(*tasks, extra=None, jobs=()):
-    wanted = [task.wanted for task in tasks] + ([] if extra is None else [extra])
-    r = sums_everywhere(jnp.concatenate(wanted, axis=1))
-    jobs = [job for job in jobs if job.held is not None]
+def advance(*tasks, jobs=()):
+    wanted = [task.wanted for task in tasks]
+    r = sums_everywhere(jnp.concatenate(wanted, axis=1) if len(wanted) > 1 else wanted[0])
+    jobs = [job for job in jobs if job.held is not None and not job.waits()]
     if jobs:
         r, held = lax.optimization_barrier((r, [job.held for job in jobs]))
         for job, values in zip(jobs, held):
@@ -1418,14 +1518,21 @@
     wide = fast_input.shape[3]
 
     which = jnp.reshape(own, (1,)).astype(jnp.int32)
-    small = [fast_reduce[0], fast_spatial[0], fast_expand[0], norm_gain[0], norm_bias[0]]
-    flat = jnp.concatenate([x.reshape(-1) for x in small])
-    flat = jnp.pad(flat, (0, -flat.shape[0] % 1024)).reshape(-1, 128)
-    flat = lax.all_gather(flat, "section").reshape(2, -1)
-    gathered, cursor = [], 0
-    for x in small:
-        gathered.append(flat[:, cursor : cursor + x.size].reshape((2,) + x.shape))
-        cursor += x.size
+    inner, depth = fast_reduce.shape[2], slow_expand.shape[2]
+    widths = [
+        inner, inner, wide, lateral_conv.shape[2], depth, depth, slow_expand.shape[1], shortcut.shape[1]
+    ]
+    rows_of = {
+        "fast_spatial": jnp.tile(fast_spatial[0], (1, 1, GROUP)).reshape(-1, 128),
+        "fast_reduce": fast_reduce[0].reshape(-1, 128),
+        "fast_expand": jnp.tile(fast_expand[0], (1, GROUP)),
+    }
+    sizes = {name: x.shape[0] for name, x in rows_of.items()}
+    sizes.update(inner=inner, wide=wide)
+    norms = jnp.concatenate([norm_row(norm_gain[0], widths), norm_row(norm_bias[0], widths)])
+    small = jnp.concatenate(list(rows_of.values()) + [norms.reshape(-1, 128)])
+    small = lax.all_gather(small, "section")
+    norms = small[:, small.shape[1] - norms.size // 128 :].reshape(2, 2, 1, -1)
     large = [
         lateral_conv[0],
         slow_reduce[0].reshape(-1, slow_reduce.shape[3]),
@@ -1434,7 +1541,7 @@
         shortcut[0],
     ]
     large = [lax.all_gather(x, "section") for x in large]
-    sections = [Section(index, gathered, large) for index in range(2)]
+    sections = [Section(index, small, norms, sizes, large) for index in range(2)]
 
     count_here = lax.dynamic_index_in_dim(frame_counts, own, 0, keepdims=False)
     frame = lax.axis_index("clip") * frames + lax.broadcasted_iota(
@@ -1447,9 +1554,9 @@
 
     fast_in, *parts = blocks[0].fast_first(fast_input, which)
     fast = [Task(blocks[0].fast_forward(fast_in, parts)), None]
-    got = advance(fast[0], extra=jnp.sum(mask, axis=0, keepdims=True))
-    r, offset = got[1]
-    shared["slow"] = jnp.sum(r[:, offset : offset + 1], axis=0, keepdims=True)
+    got = advance(fast[0])
+    r = got[0][0]
+    shared["slow"] = jnp.sum(r[:, r.shape[1] - 128 : r.shape[1] - 127], axis=0, keepdims=True)
     shared["fast"] = GROUP * shared["slow"]
     fast[0].resume(got[0])
     for step in range(2):
@@ -1464,12 +1571,14 @@
         slow[0].resume(got[0])
         fast[1].resume(got[1])
     slow[1] = Task(blocks[1].slow_forward(blocks[0].slow_out))
+    out_fast = Job(worked([place_packed(blocks[0].fast_out, blocks[1].fast_out, which, frames)]))
     for step in range(3):
-        slow[1].resume(advance(slow[1])[0])
+        slow[1].resume(advance(slow[1], jobs=[out_fast] if step == 0 else [])[0])
 
     zero, one = blocks
     ways = routes()
     jobs = []
+    early_names, late_names = ("shortcut", "slow_expand"), ("slow_spatial", "slow_reduce", "lateral")
 
     def start(steps, paces=(1,)):
         jobs.append(Job(steps, paces))
@@ -1477,9 +1586,7 @@
 
     tasks = Task(one.slow_backward(load_rows(slow_cotangent, mask, which)))
     tasks.resume(advance(tasks)[0])
-    soonest = start(
-        reduction([one.blocked(n) for n in ("shortcut", "slow_expand")], ways[0]), (2, 2, 2, 2, 1)
-    )
+    start(held_grads(one, early_names))
     tasks.resume(advance(tasks, jobs=jobs)[0])
     start(held_grads(one, ("slow_spatial",)))
     tasks.resume(advance(tasks, jobs=jobs)[0])
@@ -1491,17 +1598,11 @@
         late.resume(got[0])
         soon.resume(got[1])
         if step == 0:
-            whole = start(
-                reduction(
-                    [one.blocked(n) for n in ("slow_spatial", "slow_reduce", "lateral")], ways[1]
-                ),
-                (2, 2, 2, 2, 1),
-            )
-            early = start(
-                reduction([zero.blocked(n) for n in ("shortcut", "slow_expand")], ways[2]),
-                (1, 1, 2, 2, 2, 1),
-            )
+            held_one = start(held_grads(one, ("lateral",)))
+            early = start(reduction([zero.blocked(n) for n in early_names], ways[2]), PLANS[1])
         if step == 1:
+            groups = [[one.blocked(n) for n in names] for names in (early_names, late_names)]
+            whole = start(summed(groups), PLANS[0])
             start(held_grads(zero, ("slow_spatial",)))
         if step == 2:
             start(held_grads(zero, ("slow_reduce",)))
@@ -1509,37 +1610,36 @@
     got = advance(late, last, jobs=jobs)
     late.resume(got[0])
     last.resume(got[1])
-    middle = start(
-        reduction([zero.blocked(n) for n in ("slow_spatial", "slow_reduce", "lateral")], ways[0]),
-        (2, 2, 2, 1),
-    )
-    middle.resume(middle.held)
+    late_job = start(reduction([zero.blocked(n) for n in late_names], ways[0]), PLANS[2])
+    late_job.resume(late_job.held)
     for step in range(3):
         last.resume(advance(last, jobs=jobs)[0])
     rest = Job(small_reduction(jnp.concatenate([zero.fast_flat(), one.fast_flat()]))).finish()
 
     totals = {}
-    halves_one = dict(zip(("shortcut", "slow_expand"), soonest.finish()))
-    halves_one.update(zip(("slow_spatial", "slow_reduce", "lateral"), whole.finish()))
-    halves_zero = dict(zip(("shortcut", "slow_expand"), early.finish()))
-    halves_zero.update(zip(("slow_spatial", "slow_reduce", "lateral"), middle.finish()))
-    for name in ("shortcut", "slow_reduce", "slow_expand"):
-        totals[name] = place_weight(halves_zero[name], halves_one[name], which)
-    for name in ("slow_spatial", "lateral"):
-        low, high = halves_zero[name], halves_one[name]
-        to_zero, to_one = cross(low, high)
-        totals[name] = jnp.concatenate(
-            [jnp.where(lower, low, to_one), jnp.where(lower, to_zero, high)], axis=1
-        )
-    pairs, depth, double = totals["lateral"].shape
-    lateral = totals["lateral"].reshape(pairs, depth, 2, double // 2)
-    lateral = jnp.swapaxes(lateral, 1, 2).reshape(2 * pairs, depth, -1)
-    totals["lateral"] = lateral[: lateral_conv.shape[1]]
-    rows = rest.shape[0] // 2
-    flat, cursor = jnp.where(lower, rest[:rows], rest[rows:]).reshape(-1), 0
-    for name, x in zip(("fast_reduce", "fast_spatial", "fast_expand"), small):
-        totals[name] = flat[cursor : cursor + x.size]
-        cursor += x.size
+    highs = whole.finish()
+    highs, zero.fast_in_grad = lax.optimization_barrier((highs, zero.fast_in_grad))
+    low, high = early.finish(), highs[0]
+    totals["shortcut"], totals["slow_expand"] = place_weights(
+        place_early_kernel, low, high, slow_expand.shape[1] // 2, which,
+        [shortcut.shape[1:], slow_expand.shape[1:]],
+    )
+    low, high = late_job.finish(), highs[1]
+    totals["slow_spatial"], totals["slow_reduce"], totals["lateral"] = place_weights(
+        place_late_kernel, low, high, depth // 2, which,
+        [slow_spatial.shape[1:], (3 * depth, slow_reduce.shape[3]), lateral_conv.shape[1:]],
+    )
+    half = rest.shape[0] // 2
+    flat, cursor = jnp.where(lower, rest[:half], rest[half:]), 0
+    for name in ("fast_spatial", "fast_reduce", "fast_expand"):
+        size = sizes[name] if name == "fast_reduce" else sizes[name] // GROUP
+        piece = flat[cursor : cursor + size]
+        if name != "fast_reduce":
+            count = inner if name == "fast_spatial" else wide
+            piece = piece.reshape(-1, count // GROUP, GROUP, inner)
+            piece = jnp.swapaxes(piece, 1, 2)
+        totals[name] = piece
+        cursor += size
     names = (
         "fast_reduce",
         "fast_spatial",
@@ -1563,7 +1663,7 @@
     totals = [totals[name].reshape(shape) for name, shape in zip(names, shapes)]
     return (
         place_rows(zero.slow_out, one.slow_out, which, frames),
-        place_packed(zero.fast_out, one.fast_out, which, frames),
+        out_fast.finish()[0],
         place_rows(zero.slow_in_grad, one.slow_in_grad, which, frames),
         place_packed(zero.fast_in_grad, one.fast_in_grad, which, frames),
         *totals,

time: 1170 us -> 1090 us (0.932)
  Pallas kernels: 432 us -> 295 us
  waiting for transfers between devices: 171 us -> 255 us
  starting transfers between devices: 238 us -> 187 us
  other arithmetic: 103 us -> 53.2 us
  blocking collectives: 46 us -> 90.3 us
  local copies, waits for them, and re-layouts: 142 us -> 179 us
    unnamed x237 -> x445, local copies, waits for them, and re-layouts: 30.7 us -> 138 us
    pallas_call x38, Pallas kernels: 167 us -> 83.4 us  [call(): pl.pallas_call(partial(kernel, **static), grid=(1,), out_shape=[jax.Shape...]
    psum x0 -> x1, waiting for transfers between devices: none -> 62.3 us  [summed(): totals = lax.psum(tuple((core_half(arrays) for arrays in groups)), AXES)]
    all_to_all x4 -> x8, blocking collectives: 43.9 us -> 88 us  [sums_everywhere(): return lax.all_to_all(vector, AXES, 0, 0)]
    pallas_call x18, Pallas kernels: 202 us -> 166 us  [call_steps(): pl.pallas_call(partial(kernel, **static), grid=(steps,), out_shape=[jax.S...]
    ppermute x32 -> x16, starting transfers between devices: 52.3 us -> 20.1 us  [trade(): return lax.ppermute(values, ('section',) + AXES, partners)]
    pallas_call x10 -> x7, Pallas kernels: 60.2 us -> 29.5 us  [chosen(): pl.pallas_call(kernel, out_shape=jax.ShapeDtypeStruct(out, jnp.float32),...]
    ppermute x10, waiting for transfers between devices: 10.1 us -> 28.7 us  [from_next(): return lax.ppermute(edge, 'clip', [(i + 1, i) for i in range(count - 1)])]
  transfers between devices with their start and end apart: 98 -> 73, of which waited for: 31 -> 25; matrix products, arithmetic and copies ran while one was open for 17% -> 6% of each run, Pallas kernels for 32% -> 20%
where the time goes in v3:
time: 1090 us; the launch traced here: 1080 us
  Pallas kernels  295 us (27%)
  waiting for transfers between devices  255 us (23%)
  starting transfers between devices  187 us (17%)
  local copies, waits for them, and re-layouts  179 us (16%)
  blocking collectives  90.3 us (8%)
  other arithmetic  53.2 us (5%)
  between operations  17.9 us (2%)
    pallas_call x18, Pallas kernels, call_steps(): pl.pallas_call(partial(kernel, **static), grid=(steps,), out_shape=[jax.S...  166 us
    unnamed x445, local copies, waits for them, and re-layouts  138 us
    ppermute x16, waiting for transfers between devices, trade(): return lax.ppermute(values, ('section',) + AXES, partners)  90.3 us
    all_to_all x8, blocking collectives, sums_everywhere(): return lax.all_to_all(vector, AXES, 0, 0)  88 us
    pallas_call x38, Pallas kernels, call(): pl.pallas_call(partial(kernel, **static), grid=(1,), out_shape=[jax.Shape...  83.4 us
    all_to_all x12, starting transfers between devices, sums_everywhere(): return lax.all_to_all(vector, AXES, 0, 0)  73.1 us
    psum x1, waiting for transfers between devices, summed(): totals = lax.psum(tuple((core_half(arrays) for arrays in groups)), AXES)  62.3 us
    all_to_all x12, waiting for transfers between devices, sums_everywhere(): return lax.all_to_all(vector, AXES, 0, 0)  44.2 us
  transfers between devices with their start and end apart: 73, of which 25 were waited for; matrix products, arithmetic and copies ran while one was open for 6% of the time, Pallas kernels for 20%

profile of v3, /device:TPU:0, one launch (start us, length us, event | category | flops | bytes accessed | tf_op | source)
XLA Modules:
  0.0 1078.3 jit_solution(1577105189091575201)
XLA Ops:
  49.3 9.9 all_to_all.239
  62.1 9.9 all_to_all.240
  129.8 9.1 shard_map.264
  140.8 12.2 %all_to_all.241 = f32[16,1,2816]{2,1,0:T(1,128)S(1)} all-to-all(f32[16,1,2816]{2,1,0:T(1,128)S(1)} %copy.295), channel_id=1, replica_groups=mesh['section'=2,'clip'=4,'tm'=4] {'clip','tm'}, dimensions={0} | all-to-all | bytes 360448 | tf_op jit(solution)/shard_map/all_to_all | solution.py:32
  164.0 10.6 all_to_all.242
  197.4 10.5 all_to_all.243
  238.0 12.8 %all_to_all.244 = f32[16,1,2560]{2,1,0:T(1,128)S(1)} all-to-all(f32[16,1,2560]{2,1,0:T(1,128)S(1)} %copy.312), channel_id=1, replica_groups=mesh['section'=2,'clip'=4,'tm'=4] {'clip','tm'}, dimensions={0} | all-to-all | bytes 327680 | tf_op jit(solution)/shard_map/all_to_all | solution.py:32
  261.6 10.2 all_to_all.245
  301.2 11.9 %all_to_all.246 = f32[16,1,3072]{2,1,0:T(1,128)S(1)} all-to-all(f32[16,1,3072]{2,1,0:T(1,128)S(1)} %copy.327), channel_id=1, replica_groups=mesh['section'=2,'clip'=4,'tm'=4] {'clip','tm'}, dimensions={0} | all-to-all | bytes 393216 | tf_op jit(solution)/shard_map/all_to_all | solution.py:32
  333.2 11.1 %shard_map.283 = f32[5,1024,256]{2,1,0:T(8,128)S(1)} custom-call(f32[784,1024]{1,0:T(8,128)} %copy-done.33, f32[784,1024]{1,0:T(8,128)S(1)} %copy-done.3, f32[784,256]{1,0:T(8,128)S(1)} %copy-done.52), custom_call_target="tpu_custom_call" | custom-call | tf_op jit(solution)/shard_map/pallas_call | solution.py:181
  390.0 17.1 %shard_map.287 = (f32[784,1024]{1,0:T(8,128)}, f32[784,256]{1,0:T(8,128)S(1)}, f32[784,768]{1,0:T(8,128)S(1)}, f32[16,512]{1,0:T(8,128)S(1)}) custom-call(f32[784,256]{1,0:T(8,128)S(1)} %get-tuple-element.244.d_ref, f32[196,256]{1,0:T(8,128)S(1)} %collective-permute-done.14.p_ref, f32[196,256]{1,0:T(8,128)S(1)} %collective-permute-done.15.n_ref, ...), custom_call_target="tpu_custom_call" | custom-call | tf_op jit(solution)/shard_map/pallas_call | solution.py:181
  475.3 11.2 %shard_map.295 = f32[5,1024,256]{2,1,0:T(8,128)S(1)} custom-call(f32[784,1024]{1,0:T(8,128)} %copy-done.36, f32[784,1024]{1,0:T(8,128)S(1)} %copy-done.9, f32[784,256]{1,0:T(8,128)S(1)} %copy-done.45), custom_call_target="tpu_custom_call" | custom-call | tf_op jit(solution)/shard_map/pallas_call | solution.py:181
  536.7 18.7 %collective-permute-done.24 = f32[1536,256]{1,0:T(8,128)} collective-permute-done((f32[1536,256]{1,0:T(8,128)}, f32[1536,256]{1,0:T(8,128)}, u32[]{:S(2)}, u32[]{:S(2)}) %collective-permute-start.24) | collective-permute-done | bytes 1572896 | tf_op jit(solution)/shard_map/ppermute | solution.py:994
  579.7 17.4 %shard_map.300 = (f32[784,1024]{1,0:T(8,128)}, f32[784,256]{1,0:T(8,128)S(1)}, f32[784,768]{1,0:T(8,128)S(1)}, f32[16,512]{1,0:T(8,128)S(1)}) custom-call(f32[784,256]{1,0:T(8,128)S(1)} %copy-done.142, f32[196,256]{1,0:T(8,128)} %collective-permute-done.18.p_ref, f32[196,256]{1,0:T(8,128)} %collective-permute-done.19.n_ref, f32[784,1024]{1,0:T(8,128)S(1)} %copy-done.37, ...), custom_call_target="tpu_custom_call" | custom-call | tf_op jit(solution)/shard_map/pallas_call | solution.py:181
  600.1 13.1 %all-to-all-start.16 = ((f32[16,1,768]{2,1,0:T(1,128)}), f32[16,1,768]{2,1,0:T(1,128)S(1)}, u32[]{:S(2)}, u32[]{:S(2)}) async-start(f32[16,1,768]{2,1,0:T(1,128)} %copy.366), calls=%async_computation.16 | async-start | bytes 98304 | tf_op jit(solution)/shard_map/all_to_all | solution.py:32
  742.0 23.4 %all-to-all-done.18 = f32[16,1,256]{2,1,0:T(1,128)S(1)} async-done(((f32[16,1,256]{2,1,0:T(1,128)}), f32[16,1,256]{2,1,0:T(1,128)S(1)}, u32[]{:S(2)}, u32[]{:S(2)}) %all-to-all-start.18) | async-done | bytes 16416 | tf_op jit(solution)/shard_map/all_to_all | solution.py:32
  766.9 21.1 %collective-permute-done.37 = f32[216,256]{1,0:T(8,128)S(1)} collective-permute-done((f32[216,256]{1,0:T(8,128)S(1)}, f32[216,256]{1,0:T(8,128)S(1)}, u32[]{:S(2)}, u32[]{:S(2)}) %collective-permute-start.37) | collective-permute-done | bytes 221216 | tf_op jit(solution)/shard_map/ppermute | solution.py:994
  788.1 18.2 %collective-permute-done.42 = f32[216,256]{1,0:T(8,128)S(1)} collective-permute-done((f32[216,256]{1,0:T(8,128)S(1)}, f32[216,256]{1,0:T(8,128)S(1)}, u32[]{:S(2)}, u32[]{:S(2)}) %collective-permute-start.42) | collective-permute-done | bytes 221216 | tf_op jit(solution)/shard_map/ppermute | solution.py:994
  831.4 15.4 %collective-permute-done.48 = f32[768,256]{1,0:T(8,128)} collective-permute-done((f32[768,256]{1,0:T(8,128)S(1)}, f32[768,256]{1,0:T(8,128)}, u32[]{:S(2)}, u32[]{:S(2)}) %collective-permute-start.48) | collective-permute-done | bytes 786464 | tf_op jit(solution)/shard_map/ppermute | solution.py:994
  871.9 9.7 shard_map.279
  912.9 62.3 %all-reduce.4.cloned.1.call-done = (f32[3072,256]{1,0:T(8,128)}, f32[3456,256]{1,0:T(8,128)}) async-done(((f32[3072,256]{1,0:T(8,128)}, f32[3456,256]{1,0:T(8,128)}), (f32[3072,256]{1,0:T(8,128)}, f32[3456,256]{1,0:T(8,128)})) %all-reduce.4.cloned.1.call-update) | async-done | bytes 6684688 | tf_op jit(solution)/shard_map/psum | solution.py:959
  995.7 10.9 %shard_map.301 = f32[2,196,4,1024]{3,2,1,0:T(4,128)} custom-call(s32[1]{0:T(128)} %bitcast.own_ref, f32[784,1024]{1,0:T(8,128)} %get-tuple-element.276.a_ref, f32[784,1024]{1,0:T(8,128)} %collective-permute-done.20.b_ref, f32[784,1024]{1,0:T(8,128)} %collective-permute-done.21.c_ref, f32[784,1024]{1,0:T(8,128)} %get-tuple-element.247.d_ref), custom_call_target="tpu_custom_call" | custom-call | tf_op jit(solution)/shard_map/pallas_call | solution.py:742
  1022.4 11.2 %all-to-all-done.20 = f32[32,13,128]{2,1,0:T(8,128)S(1)} async-done(((f32[32,13,128]{2,1,0:T(8,128)}), f32[32,13,128]{2,1,0:T(8,128)S(1)}, u32[]{:S(2)}, u32[]{:S(2)}) %all-to-all-start.20) | async-done | bytes 213024 | tf_op jit(solution)/shard_map/all_to_all | solution.py:1003
  1037.5 10.6 all-to-all-done.21
  (798 shorter events, 692.0 us)
Async XLA Ops:
  7.2 64.9 %all-gather.7.cloned.1.call-start = ((), (), s32[]{:S(2)}) async-start(), calls=%async_computation.22 | async-start | bytes 1966080 | tf_op jit(solution)/shard_map/all_gather | solution.py:1543
  7.9 96.9 %all-gather.9.cloned.1.call-start = ((), (), s32[]{:S(2)}) async-start(), calls=%async_computation.23 | async-start | bytes 11796480 | tf_op jit(solution)/shard_map/all_gather | solution.py:1543
  8.7 119.2 %all-gather.11.cloned.1.call-start = ((), (), s32[]{:S(2)}) async-start(), calls=%async_computation.24 | async-start | bytes 15728640 | tf_op jit(solution)/shard_map/all_gather | solution.py:1543
  9.5 145.6 %all-gather.13.cloned.1.call-start = ((), (), s32[]{:S(2)}) async-start(), calls=%async_computation.25 | async-start | bytes 7077888 | tf_op jit(solution)/shard_map/all_gather | solution.py:1543
  10.0 179.0 %all-gather.15.cloned.1.call-start = ((), (), s32[]{:S(2)}) async-start(), calls=%async_computation.26 | async-start | bytes 3145728 | tf_op jit(solution)/shard_map/all_gather | solution.py:1543
  182.4 68.5 %collective-permute-start.11 = (f32[784,512]{1,0:T(8,128)S(1)}, f32[784,512]{1,0:T(8,128)}, u32[]{:S(2)}, u32[]{:S(2)}) collective-permute-start(f32[784,512]{1,0:T(8,128)S(1)} %get-tuple-element.210.x_ref.a_ref), channel_id=1, source_target_pairs={{16,0},{17,1},{18,2},{19,3},{20,4},{21,5},{22,6},{23,7},{24,8},{25... | collective-permute-start | bytes 4816904 | tf_op jit(solution)/shard_map/ppermute | solution.py:856
  183.7 67.2 %collective-permute-start.12 = (f32[784,512]{1,0:T(8,128)}, f32[784,512]{1,0:T(8,128)}, u32[]{:S(2)}, u32[]{:S(2)}) collective-permute-start(f32[784,512]{1,0:T(8,128)} %get-tuple-element.223.d_ref.x_ref), channel_id=1, source_target_pairs={{0,16},{1,17},{2,18},{3,19},{4,20},{5,21},{6,22},{7,23},{8,24},{9,... | collective-permute-start | bytes 4816904 | tf_op jit(solution)/shard_map/ppermute | solution.py:857
  558.6 68.7 %collective-permute-start.25 = (f32[768,256]{1,0:T(8,128)}, f32[768,256]{1,0:T(8,128)}, u32[]{:S(2)}, u32[]{:S(2)}) collective-permute-start(f32[768,256]{1,0:T(8,128)} %constant_dynamic-slice_fusion.12), channel_id=1, source_target_pairs={{0,8},{1,9},{2,10},{3,11},{4,12},{5,13},{6,14},{7,15},{8,0},{9,1},... | collective-permute-start | bytes 2359304 | tf_op jit(solution)/shard_map/ppermute | solution.py:994
  669.2 39.2 %collective-permute-start.23 = (f32[3456,256]{1,0:T(8,128)}, f32[3456,256]{1,0:T(8,128)}, u32[]{:S(2)}, u32[]{:S(2)}) collective-permute-start(f32[3456,256]{1,0:T(8,128)} %pad_maximum_fusion), channel_id=1, source_target_pairs={{0,16},{16,0},{1,17},{17,1},{2,18},{18,2},{3,19},{19,3},{4,20},{20... | collective-permute-start | bytes 10616840 | tf_op jit(solution)/shard_map/ppermute | solution.py:46
  685.1 290.1 %all-reduce.4.cloned.1.call-start = ((), (), s32[]{:S(2)}) async-start(), calls=%async_computation.27 | async-start | bytes 13369344 | tf_op jit(solution)/shard_map/psum | solution.py:959
  726.1 39.3 %collective-permute-start.36 = (f32[432,256]{1,0:T(8,128)}, f32[432,256]{1,0:T(8,128)}, u32[]{:S(2)}, u32[]{:S(2)}) collective-permute-start(f32[432,256]{1,0:T(8,128)} %constant_dynamic-slice_fusion.1), channel_id=1, source_target_pairs={{0,4},{1,5},{2,6},{3,7},{4,0},{5,1},{6,2},{7,3},{8,12},{9,13},{10,... | collective-permute-start | bytes 1327112 | tf_op jit(solution)/shard_map/ppermute | solution.py:994
  733.6 31.8 %all-to-all-start.18 = ((f32[16,1,256]{2,1,0:T(1,128)}), f32[16,1,256]{2,1,0:T(1,128)S(1)}, u32[]{:S(2)}, u32[]{:S(2)}) async-start(f32[16,1,256]{2,1,0:T(1,128)} %copy.375), calls=%async_computation.18 | async-start | bytes 32768 | tf_op jit(solution)/shard_map/all_to_all | solution.py:32
  740.7 116.7 %collective-permute-start.8 = (f32[784,1024]{1,0:T(8,128)}, f32[784,1024]{1,0:T(8,128)}, u32[]{:S(2)}, u32[]{:S(2)}) collective-permute-start(f32[784,1024]{1,0:T(8,128)} %copy-done.2), channel_id=1, source_target_pairs={{16,0},{17,1},{18,2},{19,3},{20,4},{21,5},{22,6},{23,7},{24,8},{25... | collective-permute-start | bytes 9633800 | tf_op jit(solution)/shard_map/ppermute | solution.py:856
  813.7 56.2 %collective-permute-start.13 = (f32[784,1024]{1,0:T(8,128)}, f32[784,1024]{1,0:T(8,128)}, u32[]{:S(2)}, u32[]{:S(2)}) collective-permute-start(f32[784,1024]{1,0:T(8,128)} %shard_map.278.d_ref), channel_id=1, source_target_pairs={{0,16},{1,17},{2,18},{3,19},{4,20},{5,21},{6,22},{7,23},{8,24},{9,... | collective-permute-start | bytes 9633800 | tf_op jit(solution)/shard_map/ppermute | solution.py:857
  849.4 125.8 %collective-permute-start.49 = (f32[1536,256]{1,0:T(8,128)}, f32[1536,256]{1,0:T(8,128)}, u32[]{:S(2)}, u32[]{:S(2)}) collective-permute-start(f32[1536,256]{1,0:T(8,128)} %pad_maximum_fusion.7), channel_id=1, source_target_pairs={{0,4},{1,5},{2,6},{3,7},{4,0},{5,1},{6,2},{7,3},{8,12},{9,13},{10,... | collective-permute-start | bytes 4718600 | tf_op jit(solution)/shard_map/ppermute | solution.py:994
  853.2 127.3 %collective-permute-start.45 = (f32[1728,256]{1,0:T(8,128)}, f32[1728,256]{1,0:T(8,128)}, u32[]{:S(2)}, u32[]{:S(2)}) collective-permute-start(f32[1728,256]{1,0:T(8,128)} %pad_maximum_fusion.6), channel_id=1, source_target_pairs={{0,1},{1,0},{2,3},{3,2},{4,5},{5,4},{6,7},{7,6},{8,9},{9,8},{10,11... | collective-permute-start | bytes 5308424 | tf_op jit(solution)/shard_map/ppermute | solution.py:994
  854.5 133.1 %collective-permute-start.21 = (f32[784,1024]{1,0:T(8,128)}, f32[784,1024]{1,0:T(8,128)}, u32[]{:S(2)}, u32[]{:S(2)}) collective-permute-start(f32[784,1024]{1,0:T(8,128)} %get-tuple-element.247.d_ref), channel_id=1, source_target_pairs={{0,16},{1,17},{2,18},{3,19},{4,20},{5,21},{6,22},{7,23},{8,24},{9,... | collective-permute-start | bytes 9633800 | tf_op jit(solution)/shard_map/ppermute | solution.py:857
  857.4 136.6 %collective-permute-start.20 = (f32[784,1024]{1,0:T(8,128)}, f32[784,1024]{1,0:T(8,128)}, u32[]{:S(2)}, u32[]{:S(2)}) collective-permute-start(f32[784,1024]{1,0:T(8,128)} %get-tuple-element.276.a_ref), channel_id=1, source_target_pairs={{16,0},{17,1},{18,2},{19,3},{20,4},{21,5},{22,6},{23,7},{24,8},{25... | collective-permute-start | bytes 9633800 | tf_op jit(solution)/shard_map/ppermute | solution.py:856
  902.4 108.2 %collective-permute-start.41 = (f32[784,512]{1,0:T(8,128)}, f32[784,512]{1,0:T(8,128)}, u32[]{:S(2)}, u32[]{:S(2)}) collective-permute-start(f32[784,512]{1,0:T(8,128)} %copy-done.73), channel_id=1, source_target_pairs={{0,16},{1,17},{2,18},{3,19},{4,20},{5,21},{6,22},{7,23},{8,24},{9,... | collective-permute-start | bytes 4816904 | tf_op jit(solution)/shard_map/ppermute | solution.py:857
  975.2 88.4 %collective-permute-start.47 = (f32[3456,256]{1,0:T(8,128)}, f32[3456,256]{1,0:T(8,128)}, u32[]{:S(2)}, u32[]{:S(2)}) collective-permute-start(f32[3456,256]{1,0:T(8,128)} %get-tuple-element.326), channel_id=1, source_target_pairs={{0,16},{1,17},{2,18},{3,19},{4,20},{5,21},{6,22},{7,23},{8,24},{9,... | collective-permute-start | bytes 10616840 | tf_op jit(solution)/shard_map/ppermute | solution.py:857
  984.4 79.2 %collective-permute-start.46 = (f32[3456,256]{1,0:T(8,128)}, f32[3456,256]{1,0:T(8,128)}, u32[]{:S(2)}, u32[]{:S(2)}) collective-permute-start(f32[3456,256]{1,0:T(8,128)} %pad_maximum_fusion.2), channel_id=1, source_target_pairs={{16,0},{17,1},{18,2},{19,3},{20,4},{21,5},{22,6},{23,7},{24,8},{25... | collective-permute-start | bytes 10616840 | tf_op jit(solution)/shard_map/ppermute | solution.py:856
  987.5 68.1 %collective-permute-start.51 = (f32[3072,256]{1,0:T(8,128)}, f32[3072,256]{1,0:T(8,128)}, u32[]{:S(2)}, u32[]{:S(2)}) collective-permute-start(f32[3072,256]{1,0:T(8,128)} %get-tuple-element.331), channel_id=1, source_target_pairs={{0,16},{1,17},{2,18},{3,19},{4,20},{5,21},{6,22},{7,23},{8,24},{9,... | collective-permute-start | bytes 9437192 | tf_op jit(solution)/shard_map/ppermute | solution.py:857
  994.0 61.7 %collective-permute-start.50 = (f32[3072,256]{1,0:T(8,128)}, f32[3072,256]{1,0:T(8,128)}, u32[]{:S(2)}, u32[]{:S(2)}) collective-permute-start(f32[3072,256]{1,0:T(8,128)} %pad_maximum_fusion.5), channel_id=1, source_target_pairs={{16,0},{17,1},{18,2},{19,3},{20,4},{21,5},{22,6},{23,7},{24,8},{25... | collective-permute-start | bytes 9437192 | tf_op jit(solution)/shard_map/ppermute | solution.py:856
  1014.2 36.3 %collective-permute-start.40 = (f32[784,512]{1,0:T(8,128)}, f32[784,512]{1,0:T(8,128)}, u32[]{:S(2)}, u32[]{:S(2)}) collective-permute-start(f32[784,512]{1,0:T(8,128)} %copy-done.106), channel_id=1, source_target_pairs={{16,0},{17,1},{18,2},{19,3},{20,4},{21,5},{22,6},{23,7},{24,8},{25... | collective-permute-start | bytes 4816904 | tf_op jit(solution)/shard_map/ppermute | solution.py:856
  (259 other events, 1951.5 us)
Sparse Core Ops, SparseCore 0:
  9.6 12.1 all-gather.6
  23.3 20.2 all-gather.8
  45.1 24.0 all-gather.10
  70.6 15.6 all-gather.12
  87.6 11.7 all-gather.14
  713.0 262.0 all-reduce.3

commit v4 on v3

--- a/solution.py
+++ b/solution.py
@@ -177,11 +177,18 @@
     return value
 
 
+def result(shape, spec):
+    pieces = [n for n in spec.block_shape if n is not None]
+    if math.prod(pieces) < math.prod(shape) and math.prod(shape) * 4 > 2**20:
+        return pltpu.HBM(shape, jnp.float32)
+    return jax.ShapeDtypeStruct(shape, jnp.float32)
+
+
 def call_steps(kernel, steps, outs, out_specs, ins, in_specs, scratch=(), **static):
     return pl.pallas_call(
         partial(kernel, **static),
         grid=(steps,),
-        out_shape=[jax.ShapeDtypeStruct(s, jnp.float32) for s in outs],
+        out_shape=[result(shape, spec) for shape, spec in zip(outs, out_specs)],
         in_specs=in_specs,
         out_specs=out_specs,
         scratch_shapes=[pltpu.VMEM(s, jnp.float32) for s in scratch],
@@ -739,9 +746,10 @@
 
 
 def chosen(kernel, own, grid, ins, in_specs, out, out_spec):
+    ins = [streamed(x, spec) for x, spec in zip(ins, in_specs)]
     return pl.pallas_call(
         kernel,
-        out_shape=jax.ShapeDtypeStruct(out, jnp.float32),
+        out_shape=result(out, out_spec),
         grid_spec=pltpu.PrefetchScalarGridSpec(
             num_scalar_prefetch=1, grid=grid, in_specs=in_specs, out_specs=out_spec
         ),
@@ -1104,7 +1112,7 @@
                 ],
             ),
             compiler_params=pltpu.CompilerParams(vmem_limit_bytes=VMEM_BYTES),
-        )(own, grid, self.mask, array_of(self.s.fast_reduce))
+        )(own, pltpu.with_memory_space_constraint(grid, pltpu.HBM), self.mask, array_of(self.s.fast_reduce))
 
     def fast_forward(self, fast_in, parts):
         s, mask, frames, rows, places = self.s, self.mask, self.frames, self.rows, self.places
@@ -1618,7 +1626,12 @@
 
     totals = {}
     highs = whole.finish()
-    highs, zero.fast_in_grad = lax.optimization_barrier((highs, zero.fast_in_grad))
+    placed = [
+        place_rows(zero.slow_out, one.slow_out, which, frames),
+        place_rows(zero.slow_in_grad, one.slow_in_grad, which, frames),
+        place_packed(zero.fast_in_grad, one.fast_in_grad, which, frames),
+    ]
+    highs, placed, rest = lax.optimization_barrier((highs, placed, rest))
     low, high = early.finish(), highs[0]
     totals["shortcut"], totals["slow_expand"] = place_weights(
         place_early_kernel, low, high, slow_expand.shape[1] // 2, which,
@@ -1662,10 +1675,10 @@
     ]
     totals = [totals[name].reshape(shape) for name, shape in zip(names, shapes)]
     return (
-        place_rows(zero.slow_out, one.slow_out, which, frames),
+        placed[0],
         out_fast.finish()[0],
-        place_rows(zero.slow_in_grad, one.slow_in_grad, which, frames),
-        place_packed(zero.fast_in_grad, one.fast_in_grad, which, frames),
+        placed[1],
+        placed[2],
         *totals,
         kept[None, 0],
         kept[None, 1],

time: 1090 us -> 1040 us (0.954)
  waiting for transfers between devices: 255 us -> 137 us
  blocking collectives: 90.3 us -> 146 us
  Pallas kernels: 295 us -> 322 us
  local copies, waits for them, and re-layouts: 179 us -> 152 us
    all_to_all x0 -> x1, blocking collectives: none -> 53.5 us  [small_reduction(): share = jnp.sum(lax.all_to_all(shares, axes, 0, 0), axis=0)]
    psum x1, waiting for transfers between devices: 62.3 us -> 15.8 us  [summed(): totals = lax.psum(tuple((core_half(arrays) for arrays in groups)), AXES)]
    unnamed x445 -> x403, local copies, waits for them, and re-layouts: 138 us -> 104 us
    all_to_all x12, waiting for transfers between devices: 44.2 us -> 17.5 us  [sums_everywhere(): return lax.all_to_all(vector, AXES, 0, 0)]
    pallas_call x25, Pallas kernels: 195 us -> 222 us  [the longest x18 178 us: call_steps(): pl.pallas_call(partial(kernel, **static), grid=(steps,), out_shape=[resul...]
    ppermute x16, waiting for transfers between devices: 90.3 us -> 66.2 us  [trade(): return lax.ppermute(values, ('section',) + AXES, partners)]
    all_to_all x1 -> x0, waiting for transfers between devices: 11.2 us -> none  [small_reduction(): share = jnp.sum(lax.all_to_all(shares, axes, 0, 0), axis=0)]
  transfers between devices with their start and end apart: 73 -> 72, of which waited for: 25 -> 23; matrix products, arithmetic and copies ran while one was open for 6% -> 8% of each run, Pallas kernels for 20% -> 23%
where the time goes in v4:
time: 1040 us; the launch traced here: 1030 us
  Pallas kernels  322 us (31%)
  starting transfers between devices  197 us (19%)
  local copies, waits for them, and re-layouts  152 us (15%)
  blocking collectives  146 us (14%)
  waiting for transfers between devices  137 us (13%)
  other arithmetic  58.4 us (6%)
  between operations  17.2 us (2%)
    pallas_call x18, Pallas kernels, call_steps(): pl.pallas_call(partial(kernel, **static), grid=(steps,), out_shape=[resul...  178 us
    unnamed x403, local copies, waits for them, and re-layouts  104 us
    all_to_all x8, blocking collectives, sums_everywhere(): return lax.all_to_all(vector, AXES, 0, 0)  90.1 us
    pallas_call x38, Pallas kernels, call(): pl.pallas_call(partial(kernel, **static), grid=(1,), out_shape=[jax.Shape...  83.6 us
    all_to_all x12, starting transfers between devices, sums_everywhere(): return lax.all_to_all(vector, AXES, 0, 0)  75.7 us
    ppermute x16, waiting for transfers between devices, trade(): return lax.ppermute(values, ('section',) + AXES, partners)  66.2 us
    all_to_all x1, blocking collectives, small_reduction(): share = jnp.sum(lax.all_to_all(shares, axes, 0, 0), axis=0)  53.5 us
    pallas_call x7, Pallas kernels, chosen(): pl.pallas_call(kernel, out_shape=result(out, out_spec), grid_spec=pltpu.P...  43.5 us
  transfers between devices with their start and end apart: 72, of which 23 were waited for; matrix products, arithmetic and copies ran while one was open for 8% of the time, Pallas kernels for 23%

profile of v4, /device:TPU:0, one launch (start us, length us, event | category | flops | bytes accessed | tf_op | source)
XLA Modules:
  0.0 1029.8 jit_solution(8785599064615034756)
XLA Ops:
  48.7 9.9 all_to_all.239
  61.5 9.9 all_to_all.240
  141.2 13.2 %all_to_all.241 = f32[16,1,2816]{2,1,0:T(1,128)S(1)} all-to-all(f32[16,1,2816]{2,1,0:T(1,128)S(1)} %copy.295), channel_id=1, replica_groups=mesh['section'=2,'clip'=4,'tm'=4] {'clip','tm'}, dimensions={0} | all-to-all | bytes 360448 | tf_op jit(solution)/shard_map/all_to_all | solution.py:32
  165.3 10.6 %all_to_all.242 = f32[16,1,768]{2,1,0:T(1,128)S(1)} all-to-all(f32[16,1,768]{2,1,0:T(1,128)S(1)} %copy.300), channel_id=1, replica_groups=mesh['section'=2,'clip'=4,'tm'=4] {'clip','tm'}, dimensions={0} | all-to-all | bytes 98304 | tf_op jit(solution)/shard_map/all_to_all | solution.py:32
  198.1 10.5 %all_to_all.243 = f32[16,1,2560]{2,1,0:T(1,128)S(1)} all-to-all(f32[16,1,2560]{2,1,0:T(1,128)S(1)} %copy.305), channel_id=1, replica_groups=mesh['section'=2,'clip'=4,'tm'=4] {'clip','tm'}, dimensions={0} | all-to-all | bytes 327680 | tf_op jit(solution)/shard_map/all_to_all | solution.py:32
  230.4 10.0 shard_map.275
  241.2 13.0 %all_to_all.244 = f32[16,1,2560]{2,1,0:T(1,128)S(1)} all-to-all(f32[16,1,2560]{2,1,0:T(1,128)S(1)} %copy.312), channel_id=1, replica_groups=mesh['section'=2,'clip'=4,'tm'=4] {'clip','tm'}, dimensions={0} | all-to-all | bytes 327680 | tf_op jit(solution)/shard_map/all_to_all | solution.py:32
  265.0 10.2 all_to_all.245
  303.9 12.8 %all_to_all.246 = f32[16,1,3072]{2,1,0:T(1,128)S(1)} all-to-all(f32[16,1,3072]{2,1,0:T(1,128)S(1)} %copy.323), channel_id=1, replica_groups=mesh['section'=2,'clip'=4,'tm'=4] {'clip','tm'}, dimensions={0} | all-to-all | bytes 393216 | tf_op jit(solution)/shard_map/all_to_all | solution.py:32
  316.8 10.0 shard_map.280
  336.1 11.9 %shard_map.281 = f32[5,1024,256]{2,1,0:T(8,128)} custom-call(f32[784,1024]{1,0:T(8,128)} %get-tuple-element.237.d_ref.k_ref, f32[784,1024]{1,0:T(8,128)S(1)} %copy-done.3, f32[784,256]{1,0:T(8,128)S(1)} %copy-done.37), custom_call_target="tpu_custom_call" | custom-call | tf_op jit(solution)/shard_map/pallas_call | solution.py:188
  391.3 17.0 %shard_map.285 = (f32[784,1024]{1,0:T(8,128)}, f32[784,256]{1,0:T(8,128)S(1)}, f32[784,768]{1,0:T(8,128)S(1)}, f32[16,512]{1,0:T(8,128)S(1)}) custom-call(f32[784,256]{1,0:T(8,128)S(1)} %get-tuple-element.249.d_ref, f32[196,256]{1,0:T(8,128)S(1)} %collective-permute-done.13.p_ref, f32[196,256]{1,0:T(8,128)S(1)} %collective-permute-done.14.n_ref, ...), custom_call_target="tpu_custom_call" | custom-call | tf_op jit(solution)/shard_map/pallas_call | solution.py:188
  444.6 10.1 shard_map.291
  473.6 12.0 %shard_map.293 = f32[5,1024,256]{2,1,0:T(8,128)} custom-call(f32[784,1024]{1,0:T(8,128)} %get-tuple-element.266.d_ref.k_ref, f32[784,1024]{1,0:T(8,128)S(1)} %copy-done.7, f32[784,256]{1,0:T(8,128)S(1)} %copy-done.30), custom_call_target="tpu_custom_call" | custom-call | tf_op jit(solution)/shard_map/pallas_call | solution.py:188
  533.2 18.7 %collective-permute-done.24 = f32[1536,256]{1,0:T(8,128)} collective-permute-done((f32[1536,256]{1,0:T(8,128)}, f32[1536,256]{1,0:T(8,128)}, u32[]{:S(2)}, u32[]{:S(2)}) %collective-permute-start.24) | collective-permute-done | bytes 1572896 | tf_op jit(solution)/shard_map/ppermute | solution.py:1002
  576.2 17.4 %shard_map.300 = (f32[784,1024]{1,0:T(8,128)}, f32[784,256]{1,0:T(8,128)S(1)}, f32[784,768]{1,0:T(8,128)S(1)}, f32[16,512]{1,0:T(8,128)S(1)}) custom-call(f32[784,256]{1,0:T(8,128)S(1)} %copy-done.122, f32[196,256]{1,0:T(8,128)} %collective-permute-done.20.p_ref, f32[196,256]{1,0:T(8,128)} %collective-permute-done.21.n_ref, f32[784,1024]{1,0:T(8,128)S(1)} %copy-done.22, ...), custom_call_target="tpu_custom_call" | custom-call | tf_op jit(solution)/shard_map/pallas_call | solution.py:188
  596.6 13.2 %all-to-all-start.16 = ((f32[16,1,768]{2,1,0:T(1,128)}), f32[16,1,768]{2,1,0:T(1,128)S(1)}, u32[]{:S(2)}, u32[]{:S(2)}) async-start(f32[16,1,768]{2,1,0:T(1,128)} %copy.366), calls=%async_computation.16 | async-start | bytes 98304 | tf_op jit(solution)/shard_map/all_to_all | solution.py:32
  745.1 14.0 %collective-permute-start.18 = (f32[784,1024]{1,0:T(8,128)}, f32[784,1024]{1,0:T(8,128)}, u32[]{:S(2)}, u32[]{:S(2)}) collective-permute-start(f32[784,1024]{1,0:T(8,128)} %shard_map.294.d_ref), channel_id=1, source_target_pairs={{0,16},{1,17},{2,18},{3,19},{4,20},{5,21},{6,22},{7,23},{8,24},{9,... | collective-permute-start | bytes 9633800 | tf_op jit(solution)/shard_map/ppermute | solution.py:865
  768.2 16.2 %collective-permute-done.37 = f32[216,256]{1,0:T(8,128)S(1)} collective-permute-done((f32[216,256]{1,0:T(8,128)S(1)}, f32[216,256]{1,0:T(8,128)S(1)}, u32[]{:S(2)}, u32[]{:S(2)}) %collective-permute-start.37) | collective-permute-done | bytes 221216 | tf_op jit(solution)/shard_map/ppermute | solution.py:1002
  796.0 10.6 %collective-permute-done.42 = f32[216,256]{1,0:T(8,128)} collective-permute-done((f32[216,256]{1,0:T(8,128)}, f32[216,256]{1,0:T(8,128)}, u32[]{:S(2)}, u32[]{:S(2)}) %collective-permute-start.42) | collective-permute-done | bytes 221216 | tf_op jit(solution)/shard_map/ppermute | solution.py:1002
  876.1 53.5 %all_to_all.247 = f32[32,13,128]{2,1,0:T(8,128)} all-to-all(f32[32,13,128]{2,1,0:T(8,128)} %reshape.366), channel_id=1, replica_groups=mesh['section'=2,'clip'=4,'tm'=4] {'section','clip','tm'}, dimensions={0} | all-to-all | bytes 425984 | tf_op jit(solution)/shard_map/all_to_all | solution.py:1011
  934.8 10.9 %shard_map.295 = f32[2,196,4,1024]{3,2,1,0:T(4,128)} custom-call(s32[1]{0:T(128)} %bitcast.own_ref, f32[784,1024]{1,0:T(8,128)} %shard_map.272.x_ref.a_ref, f32[784,1024]{1,0:T(8,128)} %collective-permute-done.17.b_ref, f32[784,1024]{1,0:T(8,128)} %collective-permute-done.18.c_ref, f32[784,1024]{1,0:T(8,128)} %shard_map.294.d_ref), custom_call_target="tpu_custom_call" | custom-call | tf_op jit(solution)/shard_map/pallas_call | solution.py:750
  945.7 10.8 %shard_map.301 = f32[2,196,4,1024]{3,2,1,0:T(4,128)} custom-call(s32[1]{0:T(128)} %bitcast.own_ref, f32[784,1024]{1,0:T(8,128)} %get-tuple-element.283.a_ref, f32[784,1024]{1,0:T(8,128)} %collective-permute-done.22.b_ref, f32[784,1024]{1,0:T(8,128)} %collective-permute-done.23.c_ref, f32[784,1024]{1,0:T(8,128)} %get-tuple-element.253.d_ref), custom_call_target="tpu_custom_call" | custom-call | tf_op jit(solution)/shard_map/pallas_call | solution.py:750
  962.4 15.8 %all-reduce.4.cloned.1.call-done = (f32[3072,256]{1,0:T(8,128)}, f32[3456,256]{1,0:T(8,128)}) async-done(((f32[3072,256]{1,0:T(8,128)}, f32[3456,256]{1,0:T(8,128)}), (f32[3072,256]{1,0:T(8,128)}, f32[3456,256]{1,0:T(8,128)})) %all-reduce.4.cloned.1.call-update) | async-done | bytes 6684688 | tf_op jit(solution)/shard_map/psum | solution.py:967
  (757 shorter events, 670.3 us)
Async XLA Ops:
  7.2 64.2 %all-gather.7.cloned.1.call-start = ((), (), s32[]{:S(2)}) async-start(), calls=%async_computation.22 | async-start | bytes 1966080 | tf_op jit(solution)/shard_map/all_gather | solution.py:1551
  7.9 96.0 %all-gather.9.cloned.1.call-start = ((), (), s32[]{:S(2)}) async-start(), calls=%async_computation.23 | async-start | bytes 11796480 | tf_op jit(solution)/shard_map/all_gather | solution.py:1551
  8.7 120.6 %all-gather.11.cloned.1.call-start = ((), (), s32[]{:S(2)}) async-start(), calls=%async_computation.24 | async-start | bytes 15728640 | tf_op jit(solution)/shard_map/all_gather | solution.py:1551
  9.5 147.0 %all-gather.13.cloned.1.call-start = ((), (), s32[]{:S(2)}) async-start(), calls=%async_computation.25 | async-start | bytes 7077888 | tf_op jit(solution)/shard_map/all_gather | solution.py:1551
  10.0 180.4 %all-gather.15.cloned.1.call-start = ((), (), s32[]{:S(2)}) async-start(), calls=%async_computation.26 | async-start | bytes 3145728 | tf_op jit(solution)/shard_map/all_gather | solution.py:1551
  183.8 70.5 %collective-permute-start.10 = (f32[784,512]{1,0:T(8,128)S(1)}, f32[784,512]{1,0:T(8,128)}, u32[]{:S(2)}, u32[]{:S(2)}) collective-permute-start(f32[784,512]{1,0:T(8,128)S(1)} %get-tuple-element.213.x_ref.a_ref), channel_id=1, source_target_pairs={{16,0},{17,1},{18,2},{19,3},{20,4},{21,5},{22,6},{23,7},{24,8},{25... | collective-permute-start | bytes 4816904 | tf_op jit(solution)/shard_map/ppermute | solution.py:864
  185.1 69.2 %collective-permute-start.11 = (f32[784,512]{1,0:T(8,128)}, f32[784,512]{1,0:T(8,128)}, u32[]{:S(2)}, u32[]{:S(2)}) collective-permute-start(f32[784,512]{1,0:T(8,128)} %get-tuple-element.226.d_ref.x_ref), channel_id=1, source_target_pairs={{0,16},{1,17},{2,18},{3,19},{4,20},{5,21},{6,22},{7,23},{8,24},{9,... | collective-permute-start | bytes 4816904 | tf_op jit(solution)/shard_map/ppermute | solution.py:865
  555.1 67.7 %collective-permute-start.25 = (f32[768,256]{1,0:T(8,128)}, f32[768,256]{1,0:T(8,128)}, u32[]{:S(2)}, u32[]{:S(2)}) collective-permute-start(f32[768,256]{1,0:T(8,128)} %constant_dynamic-slice_fusion.12), channel_id=1, source_target_pairs={{0,8},{1,9},{2,10},{3,11},{4,12},{5,13},{6,14},{7,15},{8,0},{9,1},... | collective-permute-start | bytes 2359304 | tf_op jit(solution)/shard_map/ppermute | solution.py:1002
  657.0 28.1 %collective-permute-start.12 = (f32[3072,256]{1,0:T(8,128)}, f32[3072,256]{1,0:T(8,128)}, u32[]{:S(2)}, u32[]{:S(2)}) collective-permute-start(f32[3072,256]{1,0:T(8,128)} %pad_maximum_fusion.3), channel_id=1, source_target_pairs={{0,16},{16,0},{1,17},{17,1},{2,18},{18,2},{3,19},{19,3},{4,20},{20... | collective-permute-start | bytes 9437192 | tf_op jit(solution)/shard_map/ppermute | solution.py:46
  663.7 39.8 %collective-permute-start.16 = (f32[3456,256]{1,0:T(8,128)}, f32[3456,256]{1,0:T(8,128)}, u32[]{:S(2)}, u32[]{:S(2)}) collective-permute-start(f32[3456,256]{1,0:T(8,128)} %pad_maximum_fusion), channel_id=1, source_target_pairs={{0,16},{16,0},{1,17},{17,1},{2,18},{18,2},{3,19},{19,3},{4,20},{20... | collective-permute-start | bytes 10616840 | tf_op jit(solution)/shard_map/ppermute | solution.py:46
  680.1 298.1 %all-reduce.4.cloned.1.call-start = ((), (), s32[]{:S(2)}) async-start(), calls=%async_computation.27 | async-start | bytes 13369344 | tf_op jit(solution)/shard_map/psum | solution.py:967
  720.9 41.4 %collective-permute-start.36 = (f32[432,256]{1,0:T(8,128)}, f32[432,256]{1,0:T(8,128)}, u32[]{:S(2)}, u32[]{:S(2)}) collective-permute-start(f32[432,256]{1,0:T(8,128)} %constant_dynamic-slice_fusion.1), channel_id=1, source_target_pairs={{0,4},{1,5},{2,6},{3,7},{4,0},{5,1},{6,2},{7,3},{8,12},{9,13},{10,... | collective-permute-start | bytes 1327112 | tf_op jit(solution)/shard_map/ppermute | solution.py:1002
  728.4 33.8 %all-to-all-start.18 = ((f32[16,1,256]{2,1,0:T(1,128)}), f32[16,1,256]{2,1,0:T(1,128)S(1)}, u32[]{:S(2)}, u32[]{:S(2)}) async-start(f32[16,1,256]{2,1,0:T(1,128)} %copy.375), calls=%async_computation.18 | async-start | bytes 32768 | tf_op jit(solution)/shard_map/all_to_all | solution.py:32
  735.0 31.1 %collective-permute-start.34 = (f32[384,256]{1,0:T(8,128)}, f32[384,256]{1,0:T(8,128)}, u32[]{:S(2)}, u32[]{:S(2)}) collective-permute-start(f32[384,256]{1,0:T(8,128)} %pad_maximum_fusion.11), channel_id=1, source_target_pairs={{0,1},{1,0},{2,3},{3,2},{4,5},{5,4},{6,7},{7,6},{8,9},{9,8},{10,11... | collective-permute-start | bytes 1179656 | tf_op jit(solution)/shard_map/ppermute | solution.py:1002
  736.9 124.3 %collective-permute-start.17 = (f32[784,1024]{1,0:T(8,128)}, f32[784,1024]{1,0:T(8,128)}, u32[]{:S(2)}, u32[]{:S(2)}) collective-permute-start(f32[784,1024]{1,0:T(8,128)} %shard_map.272.x_ref.a_ref), channel_id=1, source_target_pairs={{16,0},{17,1},{18,2},{19,3},{20,4},{21,5},{22,6},{23,7},{24,8},{25... | collective-permute-start | bytes 9633800 | tf_op jit(solution)/shard_map/ppermute | solution.py:864
  745.1 118.5 %collective-permute-start.18 = (f32[784,1024]{1,0:T(8,128)}, f32[784,1024]{1,0:T(8,128)}, u32[]{:S(2)}, u32[]{:S(2)}) collective-permute-start(f32[784,1024]{1,0:T(8,128)} %shard_map.294.d_ref), channel_id=1, source_target_pairs={{0,16},{1,17},{2,18},{3,19},{4,20},{5,21},{6,22},{7,23},{8,24},{9,... | collective-permute-start | bytes 9633800 | tf_op jit(solution)/shard_map/ppermute | solution.py:865
  759.1 113.1 %collective-permute-start.23 = (f32[784,1024]{1,0:T(8,128)}, f32[784,1024]{1,0:T(8,128)}, u32[]{:S(2)}, u32[]{:S(2)}) collective-permute-start(f32[784,1024]{1,0:T(8,128)} %get-tuple-element.253.d_ref), channel_id=1, source_target_pairs={{0,16},{1,17},{2,18},{3,19},{4,20},{5,21},{6,22},{7,23},{8,24},{9,... | collective-permute-start | bytes 9633800 | tf_op jit(solution)/shard_map/ppermute | solution.py:865
  826.3 28.1 %collective-permute-start.48 = (f32[768,256]{1,0:T(8,128)}, f32[768,256]{1,0:T(8,128)}, u32[]{:S(2)}, u32[]{:S(2)}) collective-permute-start(f32[768,256]{1,0:T(8,128)} %pad_maximum_fusion.9), channel_id=1, source_target_pairs={{0,8},{1,9},{2,10},{3,11},{4,12},{5,13},{6,14},{7,15},{8,0},{9,1},... | collective-permute-start | bytes 2359304 | tf_op jit(solution)/shard_map/ppermute | solution.py:1002
  831.6 114.1 %collective-permute-start.22 = (f32[784,1024]{1,0:T(8,128)}, f32[784,1024]{1,0:T(8,128)}, u32[]{:S(2)}, u32[]{:S(2)}) collective-permute-start(f32[784,1024]{1,0:T(8,128)} %get-tuple-element.283.a_ref), channel_id=1, source_target_pairs={{16,0},{17,1},{18,2},{19,3},{20,4},{21,5},{22,6},{23,7},{24,8},{25... | collective-permute-start | bytes 9633800 | tf_op jit(solution)/shard_map/ppermute | solution.py:864
  861.2 96.9 %collective-permute-start.41 = (f32[784,512]{1,0:T(8,128)S(1)}, f32[784,512]{1,0:T(8,128)}, u32[]{:S(2)}, u32[]{:S(2)}) collective-permute-start(f32[784,512]{1,0:T(8,128)S(1)} %copy-done.57), channel_id=1, source_target_pairs={{0,16},{1,17},{2,18},{3,19},{4,20},{5,21},{6,22},{7,23},{8,24},{9,... | collective-permute-start | bytes 4816904 | tf_op jit(solution)/shard_map/ppermute | solution.py:865
  863.6 94.5 %collective-permute-start.40 = (f32[784,512]{1,0:T(8,128)}, f32[784,512]{1,0:T(8,128)}, u32[]{:S(2)}, u32[]{:S(2)}) collective-permute-start(f32[784,512]{1,0:T(8,128)} %get-tuple-element.315.a_ref), channel_id=1, source_target_pairs={{16,0},{17,1},{18,2},{19,3},{20,4},{21,5},{22,6},{23,7},{24,8},{25... | collective-permute-start | bytes 4816904 | tf_op jit(solution)/shard_map/ppermute | solution.py:864
  870.7 114.0 %collective-permute-start.49 = (f32[1536,256]{1,0:T(8,128)}, f32[1536,256]{1,0:T(8,128)}, u32[]{:S(2)}, u32[]{:S(2)}) collective-permute-start(f32[1536,256]{1,0:T(8,128)} %pad_maximum_fusion.7), channel_id=1, source_target_pairs={{0,4},{1,5},{2,6},{3,7},{4,0},{5,1},{6,2},{7,3},{8,12},{9,13},{10,... | collective-permute-start | bytes 4718600 | tf_op jit(solution)/shard_map/ppermute | solution.py:1002
  872.2 114.6 %collective-permute-start.45 = (f32[1728,256]{1,0:T(8,128)}, f32[1728,256]{1,0:T(8,128)}, u32[]{:S(2)}, u32[]{:S(2)}) collective-permute-start(f32[1728,256]{1,0:T(8,128)} %pad_maximum_fusion.6), channel_id=1, source_target_pairs={{0,1},{1,0},{2,3},{3,2},{4,5},{5,4},{6,7},{7,6},{8,9},{9,8},{10,11... | collective-permute-start | bytes 5308424 | tf_op jit(solution)/shard_map/ppermute | solution.py:1002
  978.2 37.1 %collective-permute-start.47 = (f32[3456,256]{1,0:T(8,128)}, f32[3456,256]{1,0:T(8,128)}, u32[]{:S(2)}, u32[]{:S(2)}) collective-permute-start(f32[3456,256]{1,0:T(8,128)} %get-tuple-element.332), channel_id=1, source_target_pairs={{0,16},{1,17},{2,18},{3,19},{4,20},{5,21},{6,22},{7,23},{8,24},{9,... | collective-permute-start | bytes 10616840 | tf_op jit(solution)/shard_map/ppermute | solution.py:865
  (238 other events, 1950.4 us)
Sparse Core Ops, SparseCore 0:
  9.6 12.1 all-gather.6
  23.3 20.2 all-gather.8
  45.1 24.0 all-gather.10
  70.6 15.6 all-gather.12
  87.6 11.7 all-gather.14
  708.1 270.0 all-reduce.3
